TPU v7x, 256 devices: a whole 4x4x8 slice. The times are simulated.
256 devices in a mesh: pair: 32 (over z_lo, x, core), virt: 8 (over y, z_hi).
Axes of the slice: x: 4, y: 4, z: 8 (z_hi: 2, z_lo: 4; z = z_hi * 4 + z_lo), core: 2. Of those that a mesh axis runs over, the one named last changes fastest.
Arguments:
- amplitudes: bfloat16 [96, 96, 128, 128], P('pair', None, 'virt'), may hold values from -6 to 6
- integrals: bfloat16 [128, 20, 128, 128], P('virt'), may hold values from -0.125 to 0.125
- cd_tiles: int32 [128, 20], P('virt'), may hold values from 0 to 127, as said below
- tile_counts: int32 [128], P('virt'), may hold values from 10 to 20, as said below
- eps_occ: float32 [96], replicated, may hold values from -2 to -0.5
- eps_virt: float32 [128], replicated, may hold values from 0.5 to 3
Outputs:
- new_amplitudes: bfloat16 [96, 96, 128, 128], P('pair', None, 'virt')
Inputs may be any that keep to these rules, and one draw needn't show every extreme that they name: `cd_tiles`: row a holds 20 different numbers from lo(a) to lo(a) + 2 * 16 - 1, where lo(a) = min(max(a - 16, 0), 96); only its first tile_counts[a] entries are live. `tile_counts`: some entry equals 20.
All inputs are finite; a program needn't handle non-finite values.
Results may differ from a plain program's by a relative error of at most 0.001.
Values may be sent and summed in bfloat16 or wider, within the bound.
No kernel may reach another device: no remote copies, remote signals or barrier semaphores. Data moves between devices by JAX's collectives and lax.ppermute only.
A program may use at most 128 MiB of HBM per device.

v0:
```python
import jax
import jax.numpy as jnp
from jax import lax
from jax.sharding import PartitionSpec as P


def extended(cells, sides, width):
    for axis, dim in sides:
        count = lax.axis_size(axis)
        ends = count - 1
        head = lax.slice_in_dim(cells, 0, width, axis=dim)
        tail = lax.slice_in_dim(cells, cells.shape[dim] - width, cells.shape[dim], axis=dim)
        cells = jnp.concatenate(
            [
                lax.ppermute(tail, axis, [(i, (i + 1) % count) for i in range(ends)]),
                cells,
                lax.ppermute(head, axis, [((i + 1) % count, i) for i in range(ends)]),
            ],
            axis=dim,
        )
    return cells


def per_device(amplitudes, integrals, cd_tiles, tile_counts, eps_occ, eps_virt):
    own_rows = amplitudes.shape[0]
    own_tiles = amplitudes.shape[2]
    slot_count = integrals.shape[1]
    first_tile = lax.axis_index("virt") * own_tiles
    first_row = lax.axis_index("pair") * own_rows
    local_tiles = cd_tiles - first_tile + own_tiles
    slot_ids = lax.broadcasted_iota(jnp.int32, cd_tiles.shape, 1)
    kept_slots = (slot_ids < tile_counts[:, None]).astype(jnp.bfloat16)
    masked_weights = integrals * kept_slots[:, :, None, None]
    padded = extended(amplitudes, (("virt", 2),), own_tiles)
    block_width = min(4, slot_count)
    ladder = None
    for block_start in range(0, slot_count, block_width):
        block_stop = min(block_start + block_width, slot_count)
        columns = local_tiles[:, block_start:block_stop]
        picked = jnp.take(padded, columns, axis=2)
        weights = masked_weights[:, block_start:block_stop]
        term = jnp.einsum("ijasd,asdb->ijab", picked, weights, preferred_element_type=jnp.float32)
        ladder = term if ladder is None else ladder + term
    arrived_ladder = lax.all_to_all(
        lax.all_to_all(ladder, "pair", split_axis=1, concat_axis=0, tiled=True),
        "virt",
        split_axis=3,
        concat_axis=2,
        tiled=True,
    )
    partner = jnp.transpose(arrived_ladder, (1, 0, 3, 2))
    occupied_own = lax.dynamic_slice_in_dim(eps_occ, first_row, own_rows)
    virtual_own = lax.dynamic_slice_in_dim(eps_virt, first_tile, own_tiles)
    denominator = (
        occupied_own[:, None, None, None]
        + eps_occ[None, :, None, None]
        - virtual_own[None, None, :, None]
        - eps_virt[None, None, None, :]
    )
    return ((ladder + partner) / denominator).astype(jnp.bfloat16)


def solution(mesh):
    in_specs = (
        P("pair", None, "virt", None),
        P("virt", None, None, None),
        P("virt", None),
        P("virt"),
        P(),
        P(),
    )
    out_specs = P("pair", None, "virt", None)
    return jax.shard_map(
        per_device, mesh=mesh, in_specs=in_specs, out_specs=out_specs, check_vma=False
    )
```

profile of v0, /device:TPU:1, one launch (start us, length us, event | category | flops | bytes accessed | tf_op | source)
XLA Modules:
  0.0 315.9 jit_solution(15575405605856013050)
XLA Ops:
  0.0 2.6 copy.43
  2.6 10.7 %collective-permute-start = (bf16[3,96,16,128]{3,1,2,0:T(8,128)(2,1)}, bf16[3,96,16,128]{3,1,2,0:T(8,128)(2,1)}, u32[]{:S(2)}, u32[]{:S(2)}) collective-permute-start(bf16[3,96,16,128]{3,1,2,0:T(8,128)(2,1)} %copy.43), channel_id=1, source_target_pairs={{0,1},{1,2},{2,3},{3,4},{4,5},{5,6},{6,7},{8,9},{9,10},{10,11},{11... | collective-permute-start | bytes 3538952 | tf_op jit(solution)/shard_map/ppermute | solution.py:15
  17.8 10.2 %broadcast_multiply_fusion = bf16[16,20,128,128]{3,2,1,0:T(8,128)(2,1)} fusion(bf16[16,20,128,128]{3,2,1,0:T(8,128)(2,1)} %param.9, bf16[16,20]{1,0:T(8,128)(2,1)S(1)} %fusion.25), kind=kLoop, calls=%fused_computation.5 | loop fusion | flops 5242880 | bytes 20972160 | tf_op jit(solution)/shard_map/mul | solution.py:33
  27.9 16.6 %collective-permute-done = bf16[3,96,16,128]{3,1,2,0:T(8,128)(2,1)} collective-permute-done((bf16[3,96,16,128]{3,1,2,0:T(8,128)(2,1)}, bf16[3,96,16,128]{3,1,2,0:T(8,128)(2,1)}, u32[]{:S(2)}, u32[]{:S(2)}) %collective-permute-start) | collective-permute-done | bytes 1179680 | tf_op jit(solution)/shard_map/ppermute | solution.py:15
  46.3 42.8 %collective-permute-done.1 = bf16[3,96,16,128]{3,1,2,0:T(8,128)(2,1)} collective-permute-done((bf16[3,96,16,128]{3,1,2,0:T(8,128)(2,1)}, bf16[3,96,16,128]{3,1,2,0:T(8,128)(2,1)}, u32[]{:S(2)}, u32[]{:S(2)}) %collective-permute-start.1) | collective-permute-done | bytes 1179680 | tf_op jit(solution)/shard_map/ppermute | solution.py:17
  90.5 3.3 %gather_fusion.2 = bf16[64,3,96,128]{3,2,1,0:T(8,128)(2,1)} fusion(bf16[3,96,48,128]{3,1,2,0:T(8,128)(2,1)S(1)} %constant_dynamic-update-slice_fusion, s32[1024]{0:T(1024)S(1)} %get-tuple-element.18), kind=kCustom, calls=%fused_computation.2.clone | custom fusion | bytes 9437440 | tf_op jit(solution)/shard_map/jit(_take)/gather | solution.py:40
  93.7 3.3 %gather_fusion.1 = bf16[64,3,96,128]{3,2,1,0:T(8,128)(2,1)} fusion(bf16[3,96,48,128]{3,1,2,0:T(8,128)(2,1)S(1)} %constant_dynamic-update-slice_fusion, s32[1024]{0:T(1024)S(1)} %get-tuple-element.19), kind=kCustom, calls=%fused_computation.1.clone | custom fusion | bytes 9437440 | tf_op jit(solution)/shard_map/jit(_take)/gather | solution.py:40
  97.1 3.2 %gather_fusion.3 = bf16[64,3,96,128]{3,2,1,0:T(8,128)(2,1)} fusion(bf16[3,96,48,128]{3,1,2,0:T(8,128)(2,1)S(1)} %constant_dynamic-update-slice_fusion, s32[1024]{0:T(1024)S(1)} %copy-done.1), kind=kCustom, calls=%fused_computation.3.clone | custom fusion | bytes 9437440 | tf_op jit(solution)/shard_map/jit(_take)/gather | solution.py:40
  100.3 3.3 %gather_fusion = bf16[64,3,96,128]{3,2,1,0:T(8,128)(2,1)} fusion(bf16[3,96,48,128]{3,1,2,0:T(8,128)(2,1)S(1)} %constant_dynamic-update-slice_fusion, s32[1024]{0:T(1024)S(1)} %pad_clamp_fusion.4), kind=kCustom, calls=%fused_computation.clone | custom fusion | bytes 9437440 | tf_op jit(solution)/shard_map/jit(_take)/gather | solution.py:40
  103.6 3.4 %gather_fusion.4 = bf16[64,3,96,128]{3,2,1,0:T(8,128)(2,1)} fusion(bf16[3,96,48,128]{3,1,2,0:T(8,128)(2,1)S(1)} %constant_dynamic-update-slice_fusion, s32[1024]{0:T(1024)S(1)} %get-tuple-element.16), kind=kCustom, calls=%fused_computation.4.clone | custom fusion | bytes 9437440 | tf_op jit(solution)/shard_map/jit(_take)/gather | solution.py:40
  107.0 4.5 %fusion.4 = f32[16,128,3,96,1]{1,3,4,2,0:T(8,128)S(1)} fusion(bf16[16,4,3,96,128]{4,3,2,1,0:T(8,128)(2,1)} %bitcast.100, pred[16,4]{1,0:T(8,128)(4,1)S(1)} %copy-done.6, bf16[16,20,128,128]{3,2,1,0:T(8,128)(2,1)} %broadcast_multiply_fusion), kind=kOutput, calls=%fused_computation.10 | convolution fusion | flops 606339072 | bytes 9175104 | tf_op jit(solution)/shard_map/ijasd,asdb->ijab/dot_general | solution.py:42
  111.5 5.9 %fusion.6 = f32[16,128,3,96,1]{1,3,4,2,0:T(8,128)} fusion(bf16[16,4,3,96,128]{4,3,2,1,0:T(8,128)(2,1)} %bitcast.101, pred[16,4]{1,0:T(8,128)(4,1)S(1)} %copy-done.5, bf16[16,20,128,128]{3,2,1,0:T(8,128)(2,1)} %broadcast_multiply_fusion), kind=kOutput, calls=%fused_computation.12 | convolution fusion | flops 606339072 | bytes 9175104 | tf_op jit(solution)/shard_map/ijasd,asdb->ijab/dot_general | solution.py:42
  117.5 5.4 %fusion.2 = f32[16,128,3,96,1]{1,3,4,2,0:T(8,128)} fusion(bf16[16,4,3,96,128]{4,3,2,1,0:T(8,128)(2,1)} %bitcast.99, pred[16,4]{1,0:T(8,128)(4,1)S(1)} %copy-done.4, bf16[16,20,128,128]{3,2,1,0:T(8,128)(2,1)S(1)} %bitcast.92), kind=kOutput, calls=%fused_computation.8 | convolution fusion | flops 606339072 | bytes 9177088 | tf_op jit(solution)/shard_map/ijasd,asdb->ijab/dot_general | solution.py:42
  123.0 2.9 fusion.8
  125.9 4.0 %fusion.17 = f32[3,96,16,128]{3,1,0,2:T(8,128)S(1)} fusion(f32[16,128,3,96,1]{1,3,4,2,0:T(8,128)} %fusion.2, f32[16,128,3,96,1]{1,3,4,2,0:T(8,128)S(1)} %fusion.4, f32[16,128,3,96,1]{1,3,4,2,0:T(8,128)} %fusion.6, f32[16,128,3,96,1]{1,3,4,2,0:T(8,128)} %fusion.8, bf16[16,4,3,96,128]{4,3,2,1,0:T(8,128)(2,1)S(1)} %bitcast.90, ...), kind=kOutput, calls=%fused_computation.30 | convolution fusion | flops 608698368 | bytes 18614272 | tf_op jit(solution)/shard_map/ijasd,asdb->ijab/dot_general | solution.py:42
  131.3 88.3 %all_to_all.36 = f32[3,96,16,128]{3,2,0,1:T(8,128)S(1)} all-to-all(f32[3,96,16,128]{3,2,0,1:T(8,128)S(1)} %copy.51), channel_id=1, replica_groups=mesh['pair'=32,'virt'=8] {'pair'}, dimensions={1} | all-to-all | bytes 4718592 | tf_op jit(solution)/shard_map/all_to_all | solution.py:45
  219.6 1.6 copy.53
  221.2 3.4 %copy.54 = f32[96,3,16,128]{0,2,1,3:T(8,128)} copy(f32[96,3,16,128]{3,2,1,0:T(8,128)} %bitcast.95) | data formatting | bytes 4718592 | tf_op jit(solution)/shard_map/all_to_all | solution.py:45
  224.6 9.2 %all-to-all-start.1 = ((f32[96,3,16,128]{0,2,1,3:T(8,128)}), f32[96,3,16,128]{0,2,1,3:T(8,128)}, u32[]{:S(2)}, u32[]{:S(2)}) async-start(f32[96,3,16,128]{0,2,1,3:T(8,128)} %copy.54), calls=%async_computation.1 | async-start | bytes 6291456 | tf_op jit(solution)/shard_map/all_to_all | solution.py:44
  234.2 70.1 %all-to-all-done.1 = f32[96,3,16,128]{0,2,1,3:T(8,128)} async-done(((f32[96,3,16,128]{0,2,1,3:T(8,128)}), f32[96,3,16,128]{0,2,1,3:T(8,128)}, u32[]{:S(2)}, u32[]{:S(2)}) %all-to-all-start.1) | async-done | bytes 2359328 | tf_op jit(solution)/shard_map/all_to_all | solution.py:44
  304.3 4.8 %copy.56 = f32[96,3,8,16,16]{0,4,3,2,1:T(8,128)} copy(f32[96,3,8,16,16]{0,3,1,4,2:T(8,128)} %bitcast.37) | data formatting | bytes 4718592 | tf_op jit(solution)/shard_map/all_to_all | solution.py:44
  309.0 3.4 %copy.57 = f32[96,3,128,16]{2,0,1,3:T(8,128)} copy(f32[96,3,128,16]{0,3,2,1:T(8,128)} %bitcast.93) | data formatting | bytes 4718592 | tf_op jit(solution)/shard_map/all_to_all | solution.py:44
  312.4 2.1 fusion.16
  314.4 1.5 copy.58
  (56 shorter events, 9.4 us)
Async XLA Ops:
  2.6 41.9 %collective-permute-start = (bf16[3,96,16,128]{3,1,2,0:T(8,128)(2,1)}, bf16[3,96,16,128]{3,1,2,0:T(8,128)(2,1)}, u32[]{:S(2)}, u32[]{:S(2)}) collective-permute-start(bf16[3,96,16,128]{3,1,2,0:T(8,128)(2,1)} %copy.43), channel_id=1, source_target_pairs={{0,1},{1,2},{2,3},{3,4},{4,5},{5,6},{6,7},{8,9},{9,10},{10,11},{11... | collective-permute-start | bytes 3538952 | tf_op jit(solution)/shard_map/ppermute | solution.py:15
  13.2 75.8 %collective-permute-start.1 = (bf16[3,96,16,128]{3,1,2,0:T(8,128)(2,1)}, bf16[3,96,16,128]{3,1,2,0:T(8,128)(2,1)}, u32[]{:S(2)}, u32[]{:S(2)}) collective-permute-start(bf16[3,96,16,128]{3,1,2,0:T(8,128)(2,1)} %copy.43), channel_id=1, source_target_pairs={{1,0},{2,1},{3,2},{4,3},{5,4},{6,5},{7,6},{9,8},{10,9},{11,10},{12... | collective-permute-start | bytes 3538952 | tf_op jit(solution)/shard_map/ppermute | solution.py:17
  17.8 28.1 %copy-start = (bf16[3,96,16,128]{3,2,1,0:T(8,128)(2,1)S(1)}, bf16[3,96,16,128]{3,2,1,0:T(8,128)(2,1)}, u32[]{:S(2)}) copy-start(bf16[3,96,16,128]{3,2,1,0:T(8,128)(2,1)} %param.8) | copy-start | bytes 3538948
  93.7 3.3 %copy-start.1 = (s32[1024]{0:T(1024)S(1)}, s32[1024]{0:T(1024)}, u32[]{:S(2)}) copy-start(s32[1024]{0:T(1024)} %get-tuple-element.17) | copy-start | bytes 12292
  103.6 3.4 %copy-start.6 = (pred[16,4]{1,0:T(8,128)(4,1)S(1)}, pred[16,4]{1,0:T(8,128)(4,1)}, u32[]{:S(2)}) copy-start(pred[16,4]{1,0:T(8,128)(4,1)} %get-tuple-element.8) | copy-start | bytes 196
  106.9 4.6 %copy-start.5 = (pred[16,4]{1,0:T(8,128)(4,1)S(1)}, pred[16,4]{1,0:T(8,128)(4,1)}, u32[]{:S(2)}) copy-start(pred[16,4]{1,0:T(8,128)(4,1)} %get-tuple-element.9) | copy-start | bytes 196
  106.9 10.5 %slice-start.2 = ((s8[10485760]{0:T(1024)(128)(4,1)}), s8[4194304]{0:T(1024)(128)(4,1)S(1)}, s32[]{:S(2)}) async-start(s8[10485760]{0:T(1024)(128)(4,1)} %bitcast.91), calls=%async_computation.4 | async-start | bytes 8388608
  107.0 10.5 %slice-start.3 = ((s8[10485760]{0:T(1024)(128)(4,1)}), s8[4194304]{0:T(1024)(128)(4,1)S(1)}, s32[]{:S(2)}) async-start(s8[10485760]{0:T(1024)(128)(4,1)} %bitcast.91), calls=%async_computation.5 | async-start | bytes 8388608
  111.5 6.0 %slice-start.4 = ((s8[10485760]{0:T(1024)(128)(4,1)}), s8[2097152]{0:T(1024)(128)(4,1)S(1)}, s32[]{:S(2)}) async-start(s8[10485760]{0:T(1024)(128)(4,1)} %bitcast.91), calls=%async_computation.6 | async-start | bytes 4194304
  111.5 6.0 %copy-start.4 = (pred[16,4]{1,0:T(8,128)(4,1)S(1)}, pred[16,4]{1,0:T(8,128)(4,1)}, u32[]{:S(2)}) copy-start(pred[16,4]{1,0:T(8,128)(4,1)} %get-tuple-element.7) | copy-start | bytes 196
  111.5 11.4 %slice-start.5 = ((s8[4718592]{0:T(1024)(128)(4,1)}), s8[4194304]{0:T(1024)(128)(4,1)S(1)}, s32[]{:S(2)}) async-start(s8[4718592]{0:T(1024)(128)(4,1)} %bitcast.96), calls=%async_computation.7 | async-start | bytes 8388608
  117.5 5.5 %slice-start.6 = ((s8[4718592]{0:T(1024)(128)(4,1)}), s8[524288]{0:T(1024)(128)(4,1)S(1)}, s32[]{:S(2)}) async-start(s8[4718592]{0:T(1024)(128)(4,1)} %bitcast.96), calls=%async_computation.8 | async-start | bytes 1048576
  117.5 5.5 %copy-start.3 = (pred[16,4]{1,0:T(8,128)(4,1)S(1)}, pred[16,4]{1,0:T(8,128)(4,1)}, u32[]{:S(2)}) copy-start(pred[16,4]{1,0:T(8,128)(4,1)} %get-tuple-element.10) | copy-start | bytes 196
  117.5 8.4 %slice-start = ((s8[4718592]{0:T(1024)(128)(4,1)}), s8[4194304]{0:T(1024)(128)(4,1)S(1)}, s32[]{:S(2)}) async-start(s8[4718592]{0:T(1024)(128)(4,1)} %bitcast.88), calls=%async_computation.2 | async-start | bytes 8388608
  123.0 2.9 slice-start.1
  123.0 2.9 copy-start.2
  224.6 9.2 %copy-start.7 = (f32[128]{0:T(128)S(1)}, f32[128]{0:T(128)}, u32[]{:S(2)}) copy-start(f32[128]{0:T(128)} %param.13) | copy-start | bytes 1540
  224.6 9.3 %copy-start.8 = (f32[96]{0:T(128)S(1)}, f32[96]{0:T(128)}, u32[]{:S(2)}) copy-start(f32[96]{0:T(128)} %param.12) | copy-start | bytes 1156
  224.6 79.6 %all-to-all-start.1 = ((f32[96,3,16,128]{0,2,1,3:T(8,128)}), f32[96,3,16,128]{0,2,1,3:T(8,128)}, u32[]{:S(2)}, u32[]{:S(2)}) async-start(f32[96,3,16,128]{0,2,1,3:T(8,128)} %copy.54), calls=%async_computation.1 | async-start | bytes 6291456 | tf_op jit(solution)/shard_map/all_to_all | solution.py:44
where the time goes:
time: 320 us; the launch traced here: 316 us
  waiting for transfers between devices  129 us (40%)
  blocking collectives  88.3 us (28%)
  local copies, waits for them, and re-layouts  38.8 us (12%)
  matrix products  22.8 us (7%)
  starting transfers between devices  21.2 us (7%)
  other arithmetic  15.1 us (5%)
    all_to_all x1, blocking collectives, per_device(): lax.all_to_all(ladder, 'pair', split_axis=1, concat_axis=0, tiled=True)  88.3 us
    all_to_all x1, waiting for transfers between devices, per_device(): lax.all_to_all(lax.all_to_all(ladder, 'pair', split_axis=1, concat_axis=0...  70.1 us
    ppermute x1, waiting for transfers between devices, extended(): lax.ppermute(head, axis, [((i + 1) % count, i) for i in range(ends)])  42.8 us
    dot_general x5, matrix products, per_device(): jnp.einsum('ijasd,asdb->ijab', picked, weights, preferred_element_type=jn...  22.8 us
    ppermute x1, waiting for transfers between devices, extended(): lax.ppermute(tail, axis, [(i, (i + 1) % count) for i in range(ends)])  16.6 us
    gather x5, local copies, waits for them, and re-layouts, per_device(): picked = jnp.take(padded, columns, axis=2)  16.5 us
    ppermute x1, starting transfers between devices, extended(): lax.ppermute(tail, axis, [(i, (i + 1) % count) for i in range(ends)])  10.7 us
    mul x1, other arithmetic, per_device(): masked_weights = integrals * kept_slots[:, :, None, None]  10.2 us
  transfers between devices with their start and end apart: 3, of which 3 were waited for; matrix products, arithmetic and copies ran while one was open for 5% of the time, Pallas kernels for 0%

commit v1 on v0

v1 whole, which is shorter than its diff:
```python
import jax
import jax.numpy as jnp
from jax import lax
from jax.experimental import pallas as pl
from jax.experimental.pallas import tpu as pltpu
from jax.sharding import PartitionSpec as P

ROWS = 3
TILES = 16
VIRT = 8
LANES = 128
MSG = ROWS * ROWS * TILES * TILES // LANES


def exchange_groups(parts):
    parts = list(parts)
    group = lax.broadcasted_iota(jnp.int32, parts[0].shape, 1) // TILES
    for step in (1, 2, 4):
        upper = (group & step) != 0
        for p in range(8):
            if p & step:
                continue
            low, high = parts[p], parts[p + step]
            parts[p] = jnp.where(upper, pltpu.roll(high, TILES * step, 1), low)
            parts[p + step] = jnp.where(upper, high, pltpu.roll(low, LANES - TILES * step, 1))
    return parts


def ladder_kernel(index_ref, own_ref, over_ref, next_ref, weight_ref, out_ref, held, picked):
    step = pl.program_id(0)
    per_step = weight_ref.shape[0]
    slots = weight_ref.shape[1] // LANES

    @pl.when(step == 0)
    def _():
        held[0:TILES] = own_ref[...]
        held[TILES : 2 * TILES] = over_ref[...]
        held[2 * TILES : 3 * TILES] = next_ref[...]
        held[3 * TILES] = jnp.zeros_like(held[3 * TILES])

    for n in range(per_step):
        a = step * per_step + n
        for s in range(slots):
            picked[n, :, s * LANES : (s + 1) * LANES] = held[index_ref[a, s]]
        row = jnp.dot(picked[n], weight_ref[n], preferred_element_type=jnp.float32)
        out_ref[pl.ds(a, row.shape[0], stride=TILES), :] = row


def ladder_rows(index, own, over, beyond, weights):
    tiles, pairs, depth = own.shape
    k = weights.shape[1]
    per_step = 2
    whole = pl.BlockSpec((tiles, pairs, depth), lambda g, *_: (0, 0, 0))
    return pl.pallas_call(
        ladder_kernel,
        out_shape=jax.ShapeDtypeStruct((pairs * tiles, LANES), jnp.float32),
        grid_spec=pltpu.PrefetchScalarGridSpec(
            num_scalar_prefetch=1,
            grid=(tiles // per_step,),
            in_specs=[whole, whole, whole, pl.BlockSpec((per_step, k, LANES), lambda g, *_: (g, 0, 0))],
            out_specs=pl.BlockSpec((pairs * tiles, LANES), lambda g, *_: (0, 0)),
            scratch_shapes=[
                pltpu.VMEM((3 * tiles + 1, pairs, depth), jnp.bfloat16),
                pltpu.VMEM((per_step, pairs, k), jnp.bfloat16),
            ],
        ),
        compiler_params=pltpu.CompilerParams(vmem_limit_bytes=24 * 2**20),
        cost_estimate=pl.CostEstimate(
            flops=2 * pairs * k * LANES * tiles, bytes_accessed=2 * tiles * k * LANES, transcendentals=0
        ),
        name="ladder_rows",
    )(index, own, over, beyond, weights)


def pack_kernel(scale_ref, l0, l1, l2, out_ref, rest):
    ladders = (l0, l1, l2)
    scale = scale_ref[0]
    devices = out_ref.shape[0] // (VIRT * MSG)
    tile = ROWS * TILES

    @pl.loop(0, devices // 8)
    def _(octet):
        for half in range(2):
            parts = [
                l2[pl.ds(octet * 8 * tile + 2 * TILES + half * 8 + n, 8, stride=tile), :] for n in range(8)
            ]
            for v, part in enumerate(exchange_groups(parts)):
                rest[pl.ds(octet * 8 * TILES + 2 * v + half, 8, stride=TILES), :] = part

    @pl.loop(0, devices)
    def _(device):
        first = pl.multiple_of(device * tile, TILES)
        parts = [ladders[k // ROWS][pl.ds(first + (k % ROWS) * TILES, TILES), :] for k in range(8)]
        last = rest[pl.ds(pl.multiple_of(device * TILES, TILES), TILES), :]
        pieces = []
        for v, part in enumerate(exchange_groups(parts)):
            pieces += [part, last[2 * v : 2 * v + 2]]
        block = jnp.concatenate(pieces, axis=0) * scale
        out_ref[pl.ds(pl.multiple_of(device * VIRT * MSG, TILES), VIRT * MSG), :] = block.astype(out_ref.dtype)


def pack(scale, ladders):
    rows = ladders[0].shape[0] * len(ladders)
    return pl.pallas_call(
        pack_kernel,
        out_shape=jax.ShapeDtypeStruct((rows, LANES), jnp.float32),
        in_specs=[pl.BlockSpec(memory_space=pltpu.SMEM)] + [pl.BlockSpec(memory_space=pltpu.VMEM)] * 3,
        out_specs=pl.BlockSpec(memory_space=pltpu.VMEM),
        scratch_shapes=[pltpu.VMEM((rows // (ROWS * ROWS), LANES), jnp.float32)],
        compiler_params=pltpu.CompilerParams(vmem_limit_bytes=24 * 2**20),
        name="pack",
    )(scale, *ladders)


def finish_kernel(unscale_ref, occ_ref, own_occ_ref, got_ref, l0, l1, l2, va_ref, vb_ref, out_ref, rest, turned):
    ladders = (l0, l1, l2)
    unscale = unscale_ref[0]
    devices = got_ref.shape[0] // (VIRT * MSG)

    def store(i, j, partner):
        own = ladders[i][pl.ds(pl.multiple_of(j * TILES, TILES), TILES), :]
        bottom = (own_occ_ref[i] + occ_ref[j]) - va_ref[...] - vb_ref[...]
        out_ref[i, j] = ((own + partner) / bottom).astype(out_ref.dtype)

    @pl.loop(0, devices)
    def _(device):
        block = got_ref[pl.ds(pl.multiple_of(device * VIRT * MSG, TILES), VIRT * MSG), :].astype(jnp.float32)
        block = block * unscale
        cut = [block[v * MSG : (v + 1) * MSG] for v in range(VIRT)]
        main = jnp.concatenate([c[:TILES] for c in cut], axis=0).T
        rest[pl.ds(pl.multiple_of(device * TILES, TILES), TILES), :] = jnp.concatenate(
            [c[TILES:] for c in cut], axis=0
        )
        for k in range(8):
            store(k % ROWS, device * ROWS + k // ROWS, main[k * TILES : (k + 1) * TILES])

    @pl.loop(0, devices // 8)
    def _(octet):
        for half in range(2):
            parts = [rest[pl.ds(octet * 8 * TILES + 2 * v + half, 8, stride=TILES), :] for v in range(VIRT)]
            for n, part in enumerate(exchange_groups(parts)):
                turned[pl.ds(half * 8 + n, 8, stride=TILES), :] = part
        columns = turned[...].T
        parts = [columns[v * TILES : (v + 1) * TILES] for v in range(VIRT)]
        for n, part in enumerate(exchange_groups(parts)):
            store(ROWS - 1, (octet * 8 + n) * ROWS + ROWS - 1, part)


def finish(unscale, occ, own_occ, got, ladders, va, vb):
    partners = occ.shape[0]
    smem, vmem = pl.BlockSpec(memory_space=pltpu.SMEM), pl.BlockSpec(memory_space=pltpu.VMEM)
    return pl.pallas_call(
        finish_kernel,
        out_shape=jax.ShapeDtypeStruct((ROWS, partners, TILES, LANES), jnp.bfloat16),
        in_specs=[smem] * 3 + [vmem] * 6,
        out_specs=vmem,
        scratch_shapes=[
            pltpu.VMEM((got.shape[0] // (ROWS * ROWS), LANES), jnp.float32),
            pltpu.VMEM((LANES, LANES), jnp.float32),
        ],
        compiler_params=pltpu.CompilerParams(vmem_limit_bytes=24 * 2**20),
        name="finish",
    )(unscale, occ, own_occ, got, *ladders, va, vb)


def per_device(amplitudes, integrals, cd_tiles, tile_counts, eps_occ, eps_virt):
    rows, partners, tiles, depth = amplitudes.shape
    slots = integrals.shape[1]
    me = lax.axis_index("virt")
    swap = [(v, v ^ 1) for v in range(VIRT)]
    relay = [(v, v + 2) for v in range(0, VIRT - 2, 2)] + [(v, v - 2) for v in range(3, VIRT, 2)]
    own = [jnp.transpose(amplitudes[i], (1, 0, 2)) for i in range(rows)]
    over = [lax.ppermute(x, "virt", swap) for x in own]
    beyond = [lax.ppermute(x, "virt", relay) for x in over]

    live = lax.broadcasted_iota(jnp.int32, cd_tiles.shape, 1) < tile_counts[:, None]
    block = cd_tiles // tiles - me
    over_block = jnp.where(me % 2 == 0, 1, -1)
    place = jnp.where(block == 0, 0, jnp.where(block == over_block, 1, 2))
    index = jnp.where(live, place * tiles + cd_tiles % tiles, 3 * tiles).astype(jnp.int32)

    largest = jnp.stack(
        [
            jnp.max(jnp.abs(amplitudes)).astype(jnp.float32),
            jnp.max(jnp.where(live, jnp.max(jnp.abs(integrals), axis=(2, 3)), 0)).astype(jnp.float32),
        ]
    )
    largest = lax.pmax(largest, ("pair", "virt"))
    bound = jnp.maximum(largest[0] * largest[1] * (slots * depth), 1e-30)
    scale = (32768.0 / bound).reshape(1)
    unscale = (bound / 32768.0).reshape(1)

    weights = integrals.reshape(tiles, slots * depth, LANES)
    ladders = [ladder_rows(index, own[i], over[i], beyond[i], weights) for i in range(rows)]
    sent = pack(scale, ladders).astype(jnp.float16).reshape(-1, MSG // 2, 2, LANES)
    got = lax.all_to_all(sent, ("pair", "virt"), split_axis=0, concat_axis=0, tiled=True)
    own_occ = lax.dynamic_slice_in_dim(eps_occ, lax.axis_index("pair") * rows, rows)
    own_virt = lax.dynamic_slice_in_dim(eps_virt, me * tiles, tiles)
    return finish(
        unscale, eps_occ, own_occ, got.reshape(-1, LANES).astype(jnp.float32), ladders, own_virt[:, None], eps_virt[None, :]
    )


def solution(mesh):
    in_specs = (
        P("pair", None, "virt", None),
        P("virt", None, None, None),
        P("virt", None),
        P("virt"),
        P(),
        P(),
    )
    out_specs = P("pair", None, "virt", None)
    return jax.shard_map(
        per_device, mesh=mesh, in_specs=in_specs, out_specs=out_specs, check_vma=False
    )
```

time: 320 us -> 218 us (0.68); the launches traced: 316 us -> 217 us
  waiting for transfers between devices: 129 us -> 32.7 us
  Pallas kernels: 0 us -> 31.1 us
  local copies, waits for them, and re-layouts: 38.8 us -> 10.6 us
  matrix products: 22.8 us -> 0 us
  starting transfers between devices: 21.2 us -> 32.2 us
  blocking collectives: 88.3 us -> 97.5 us
    pmax x0 -> x1, blocking collectives: none -> 97.5 us  [per_device(): largest = lax.pmax(largest, ('pair', 'virt'))]
    all_to_all x1 -> x0, blocking collectives: 88.3 us -> none  [per_device(): lax.all_to_all(ladder, 'pair', split_axis=1, concat_axis=0, tiled=True)]
    ppermute x2 -> x6, waiting for transfers between devices: 59.4 us -> 0.02 us  [the longest x3 0.01 us: per_device(): over = [lax.ppermute(x, 'virt', swap) for x in own]]
    all_to_all x1, waiting for transfers between devices: 70.1 us -> 32.7 us  [per_device(): lax.all_to_all(sent, ('pair', 'virt'), split_axis=0, concat_axis=0, tiled...]
    pallas_call x0 -> x5, Pallas kernels: none -> 31.1 us  [the longest x3 15.5 us: ladder_rows(): pl.pallas_call(ladder_kernel, out_shape=jax.ShapeDtypeStruct((pairs * til...]
    dot_general x5 -> x0, matrix products: 22.8 us -> none  [per_device(): jnp.einsum('ijasd,asdb->ijab', picked, weights, preferred_element_type=jn...]
    gather x5 -> x0, local copies, waits for them, and re-layouts: 16.5 us -> none  [per_device(): picked = jnp.take(padded, columns, axis=2)]
    all_to_all x4 -> x0, local copies, waits for them, and re-layouts: 13.1 us -> none  [the longest x2 8.12 us: per_device(): lax.all_to_all(lax.all_to_all(ladder, 'pair', split_axis=1, concat_axis=0...]
  transfers between devices with their start and end apart: 3 -> 7, of which waited for: 3 -> 1; matrix products, arithmetic and copies ran while one was open for 5% -> 5% of each run, Pallas kernels for 0% -> 5%
where the time goes in v1:
time: 218 us; the launch traced here: 217 us
  blocking collectives  97.5 us (45%)
  waiting for transfers between devices  32.7 us (15%)
  starting transfers between devices  32.2 us (15%)
  Pallas kernels  31.1 us (14%)
  other arithmetic  12 us (6%)
  local copies, waits for them, and re-layouts  10.6 us (5%)
    pmax x1, blocking collectives, per_device(): largest = lax.pmax(largest, ('pair', 'virt'))  97.5 us
    all_to_all x1, waiting for transfers between devices, per_device(): lax.all_to_all(sent, ('pair', 'virt'), split_axis=0, concat_axis=0, tiled...  32.7 us
    pallas_call x3, Pallas kernels, ladder_rows(): pl.pallas_call(ladder_kernel, out_shape=jax.ShapeDtypeStruct((pairs * til...  15.5 us
    ppermute x3, starting transfers between devices, per_device(): over = [lax.ppermute(x, 'virt', swap) for x in own]  13.4 us
    all_to_all x1, starting transfers between devices, per_device(): lax.all_to_all(sent, ('pair', 'virt'), split_axis=0, concat_axis=0, tiled...  11 us
    unnamed x17, local copies, waits for them, and re-layouts  8.33 us
    pallas_call x1, Pallas kernels, pack(): pl.pallas_call(pack_kernel, out_shape=jax.ShapeDtypeStruct((rows, LANES),...  8.2 us
    ppermute x3, starting transfers between devices, per_device(): beyond = [lax.ppermute(x, 'virt', relay) for x in over]  7.86 us
  transfers between devices with their start and end apart: 7, of which 1 were waited for; matrix products, arithmetic and copies ran while one was open for 5% of the time, Pallas kernels for 5%

profile of v1, /device:TPU:1, one launch (start us, length us, event | category | flops | bytes accessed | tf_op | source)
XLA Modules:
  0.0 217.4 jit_solution(9080637126866981615)
XLA Ops:
  0.0 1.4 fusion.6
  1.5 7.8 %collective-permute-start = (bf16[16,96,128]{2,1,0:T(8,128)(2,1)S(1)}, bf16[16,96,128]{2,1,0:T(8,128)(2,1)S(1)}, u32[]{:S(2)}, u32[]{:S(2)}) collective-permute-start(bf16[16,96,128]{2,1,0:T(8,128)(2,1)S(1)} %bitcast.31), channel_id=1, source_target_pairs={{0,1},{1,0},{2,3},{3,2},{4,5},{5,4},{6,7},{7,6},{8,9},{9,8},{10,11... | collective-permute-start | bytes 1179656 | tf_op jit(solution)/shard_map/ppermute | solution.py:173
  9.5 0.1 collective-permute-start.2
  9.7 5.4 %collective-permute-start.4 = (bf16[16,96,128]{2,1,0:T(8,128)(2,1)S(1)}, bf16[16,96,128]{2,1,0:T(8,128)(2,1)S(1)}, u32[]{:S(2)}, u32[]{:S(2)}) collective-permute-start(bf16[16,96,128]{2,1,0:T(8,128)(2,1)S(1)} %bitcast.29), channel_id=1, source_target_pairs={{0,1},{1,0},{2,3},{3,2},{4,5},{5,4},{6,7},{7,6},{8,9},{9,8},{10,11... | collective-permute-start | bytes 1179656 | tf_op jit(solution)/shard_map/ppermute | solution.py:173
  15.2 6.6 %abs_reduce_fusion = bf16[16,20]{1,0:T(8,128)(2,1)S(1)} fusion(bf16[16,20,128,128]{3,2,1,0:T(8,128)(2,1)} %param.7), kind=kLoop, calls=%fused_computation | loop fusion | flops 10485440 | bytes 10486400 | tf_op jit(solution)/shard_map/reduce_max | solution.py:185
  21.8 0.7 fusion.5
  22.5 0.7 abs_reduce_fusion.1
  23.2 3.2 %collective-permute-start.1 = (bf16[16,96,128]{2,1,0:T(8,128)(2,1)S(1)}, bf16[16,96,128]{2,1,0:T(8,128)(2,1)S(1)}, u32[]{:S(2)}, u32[]{:S(2)}) collective-permute-start(bf16[16,96,128]{2,1,0:T(8,128)(2,1)S(1)} %collective-permute-done.over_ref), channel_id=1, source_target_pairs={{0,2},{2,4},{4,6},{3,1},{5,3},{7,5},{8,10},{10,12},{12,14},{11,9},... | collective-permute-start | bytes 1179656 | tf_op jit(solution)/shard_map/ppermute | solution.py:174
  26.4 1.3 maximum_convert_fusion
  27.7 97.5 %pmax.7 = f32[2]{0:T(128)S(1)} all-reduce(f32[2]{0:T(128)S(1)} %maximum_convert_fusion), channel_id=1, replica_groups=mesh['pair'=32,'virt'=8] {'pair','virt'}, use_global_device_ids=true, to_apply=%region_3.4 | all-reduce | flops 2 | bytes 16 | tf_op jit(solution)/shard_map/pmax | solution.py:188
  125.2 2.7 %collective-permute-start.3 = (bf16[16,96,128]{2,1,0:T(8,128)(2,1)S(1)}, bf16[16,96,128]{2,1,0:T(8,128)(2,1)S(1)}, u32[]{:S(2)}, u32[]{:S(2)}) collective-permute-start(bf16[16,96,128]{2,1,0:T(8,128)(2,1)S(1)} %collective-permute-done.2.over_ref), channel_id=1, source_target_pairs={{0,2},{2,4},{4,6},{3,1},{5,3},{7,5},{8,10},{10,12},{12,14},{11,9},... | collective-permute-start | bytes 1179656 | tf_op jit(solution)/shard_map/ppermute | solution.py:174
  127.9 0.6 fusion.7
  129.8 1.9 collective-permute-start.5
  131.8 4.0 %copy-done = bf16[16,20,128,128]{3,2,1,0:T(8,128)(2,1)S(1)} copy-done((bf16[16,20,128,128]{3,2,1,0:T(8,128)(2,1)S(1)}, bf16[16,20,128,128]{3,2,1,0:T(8,128)(2,1)}, u32[]{:S(2)}) %copy-start) | copy-done | bytes 10485784
  135.8 5.2 %ladder_rows.3.l0 = f32[1536,128]{1,0:T(8,128)S(1)} custom-call(s32[16,20]{1,0:T(8,128)S(1)} %fusion.2.index_ref, bf16[16,96,128]{2,1,0:T(8,128)(2,1)S(1)} %bitcast.32, bf16[16,96,128]{2,1,0:T(8,128)(2,1)S(1)} %collective-permute-done.over_ref, bf16[16,96,128]{2,1,0:T(8,128)(2,1)S(1)} %collective-permute-done.1.next_ref, bf16[16,2560,128]{2,1,0:T(8,128)(2,1)S(1)} %bitcast.24), custom_call_target="tpu_custom_call" | custom-call | flops 1006632960 | bytes 10485760 | tf_op jit(solution)/shard_map/ladder_rows/pallas_call | solution.py:54
  141.0 4.0 %copy-done.1 = bf16[16,20,128,128]{3,2,1,0:T(8,128)(2,1)S(1)} copy-done((bf16[16,20,128,128]{3,2,1,0:T(8,128)(2,1)S(1)}, bf16[16,20,128,128]{3,2,1,0:T(8,128)(2,1)}, u32[]{:S(2)}) %copy-start.1) | copy-done | bytes 10485784
  145.0 5.2 %ladder_rows.4.l1 = f32[1536,128]{1,0:T(8,128)S(1)} custom-call(s32[16,20]{1,0:T(8,128)S(1)} %fusion.2.index_ref, bf16[16,96,128]{2,1,0:T(8,128)(2,1)S(1)} %bitcast.28, bf16[16,96,128]{2,1,0:T(8,128)(2,1)S(1)} %collective-permute-done.2.over_ref, bf16[16,96,128]{2,1,0:T(8,128)(2,1)S(1)} %collective-permute-done.3.next_ref, bf16[16,2560,128]{2,1,0:T(8,128)(2,1)S(1)} %bitcast.25), custom_call_target="tpu_custom_call" | custom-call | flops 1006632960 | bytes 10485760 | tf_op jit(solution)/shard_map/ladder_rows/pallas_call | solution.py:54
  150.1 5.2 %ladder_rows.5.l2 = f32[1536,128]{1,0:T(8,128)S(1)} custom-call(s32[16,20]{1,0:T(8,128)S(1)} %fusion.2.index_ref, bf16[16,96,128]{2,1,0:T(8,128)(2,1)S(1)} %bitcast.30, bf16[16,96,128]{2,1,0:T(8,128)(2,1)S(1)} %collective-permute-done.4.over_ref, bf16[16,96,128]{2,1,0:T(8,128)(2,1)S(1)} %collective-permute-done.5.next_ref, bf16[16,2560,128]{2,1,0:T(8,128)(2,1)S(1)} %bitcast.26), custom_call_target="tpu_custom_call" | custom-call | flops 1006632960 | bytes 10485760 | tf_op jit(solution)/shard_map/ladder_rows/pallas_call | solution.py:54
  155.3 8.2 %pack.1 = f32[4608,128]{1,0:T(8,128)S(1)} custom-call(f32[1]{0:T(128)S(6)} %div.20.scale_ref, f32[1536,128]{1,0:T(8,128)S(1)} %ladder_rows.3.l0, f32[1536,128]{1,0:T(8,128)S(1)} %ladder_rows.4.l1, f32[1536,128]{1,0:T(8,128)S(1)} %ladder_rows.5.l2), custom_call_target="tpu_custom_call" | custom-call | tf_op jit(solution)/shard_map/pack/pallas_call | solution.py:104
  163.5 1.2 convert_element_type.12
  164.7 11.0 %all-to-all-start = ((f16[256,9,2,128]{3,2,1,0:T(2,128)(2,1)}), f16[256,9,2,128]{3,2,1,0:T(2,128)(2,1)}, u32[]{:S(2)}, u32[]{:S(2)}) async-start(f16[256,9,2,128]{3,2,1,0:T(2,128)(2,1)} %bitcast.12), calls=%async_computation | async-start | bytes 2359296 | tf_op jit(solution)/shard_map/all_to_all | solution.py:196
  175.9 32.7 %all-to-all-done = f16[256,9,2,128]{3,2,1,0:T(2,128)(2,1)} async-done(((f16[256,9,2,128]{3,2,1,0:T(2,128)(2,1)}), f16[256,9,2,128]{3,2,1,0:T(2,128)(2,1)}, u32[]{:S(2)}, u32[]{:S(2)}) %all-to-all-start) | async-done | bytes 1179680 | tf_op jit(solution)/shard_map/all_to_all | solution.py:196
  208.6 1.4 convert.4.got_ref
  210.0 7.4 %finish.1 = bf16[3,96,16,128]{3,2,1,0:T(8,128)(2,1)} custom-call(f32[1]{0:T(128)S(6)} %div.19.unscale_ref, f32[96]{0:T(128)S(1)} %copy-done.2, f32[3]{0:T(128)S(1)} %dynamic_slice.6.own_occ_ref, f32[4608,128]{1,0:T(8,128)S(1)} %convert.4.got_ref, f32[1536,128]{1,0:T(8,128)S(1)} %ladder_rows.3.l0, f32[1536,128]{1,0:T(8,128)S(1)} %ladder_rows.4.l1, ...), custom_call_target="tpu_custom_call" | custom-call | tf_op jit(solution)/shard_map/finish/pallas_call | solution.py:152
  (25 shorter events, 0.7 us)
Async XLA Ops:
  1.5 21.7 %collective-permute-start = (bf16[16,96,128]{2,1,0:T(8,128)(2,1)S(1)}, bf16[16,96,128]{2,1,0:T(8,128)(2,1)S(1)}, u32[]{:S(2)}, u32[]{:S(2)}) collective-permute-start(bf16[16,96,128]{2,1,0:T(8,128)(2,1)S(1)} %bitcast.31), channel_id=1, source_target_pairs={{0,1},{1,0},{2,3},{3,2},{4,5},{5,4},{6,7},{7,6},{8,9},{9,8},{10,11... | collective-permute-start | bytes 1179656 | tf_op jit(solution)/shard_map/ppermute | solution.py:173
  9.5 115.7 %collective-permute-start.2 = (bf16[16,96,128]{2,1,0:T(8,128)(2,1)S(1)}, bf16[16,96,128]{2,1,0:T(8,128)(2,1)S(1)}, u32[]{:S(2)}, u32[]{:S(2)}) collective-permute-start(bf16[16,96,128]{2,1,0:T(8,128)(2,1)S(1)} %bitcast.27), channel_id=1, source_target_pairs={{0,1},{1,0},{2,3},{3,2},{4,5},{5,4},{6,7},{7,6},{8,9},{9,8},{10,11... | collective-permute-start | bytes 1179656 | tf_op jit(solution)/shard_map/ppermute | solution.py:173
  9.7 12.1 %copy-start.6 = (s32[16]{0:T(128)S(1)}, s32[16]{0:T(128)}, u32[]{:S(2)}) copy-start(s32[16]{0:T(128)} %param.9) | copy-start | bytes 196
  9.7 12.8 %copy-start.4 = (bf16[3,96,16,128]{3,2,1,0:T(8,128)(2,1)S(1)}, bf16[3,96,16,128]{3,2,1,0:T(8,128)(2,1)}, u32[]{:S(2)}) copy-start(bf16[3,96,16,128]{3,2,1,0:T(8,128)(2,1)} %param.6) | copy-start | bytes 3538948
  9.7 120.0 %collective-permute-start.4 = (bf16[16,96,128]{2,1,0:T(8,128)(2,1)S(1)}, bf16[16,96,128]{2,1,0:T(8,128)(2,1)S(1)}, u32[]{:S(2)}, u32[]{:S(2)}) collective-permute-start(bf16[16,96,128]{2,1,0:T(8,128)(2,1)S(1)} %bitcast.29), channel_id=1, source_target_pairs={{0,1},{1,0},{2,3},{3,2},{4,5},{5,4},{6,7},{7,6},{8,9},{9,8},{10,11... | collective-permute-start | bytes 1179656 | tf_op jit(solution)/shard_map/ppermute | solution.py:173
  21.8 109.9 %copy-start.5 = (s32[16,20]{1,0:T(8,128)S(1)}, s32[16,20]{1,0:T(8,128)}, u32[]{:S(2)}) copy-start(s32[16,20]{1,0:T(8,128)} %param.8) | copy-start | bytes 3844
  23.2 108.6 %collective-permute-start.1 = (bf16[16,96,128]{2,1,0:T(8,128)(2,1)S(1)}, bf16[16,96,128]{2,1,0:T(8,128)(2,1)S(1)}, u32[]{:S(2)}, u32[]{:S(2)}) collective-permute-start(bf16[16,96,128]{2,1,0:T(8,128)(2,1)S(1)} %collective-permute-done.over_ref), channel_id=1, source_target_pairs={{0,2},{2,4},{4,6},{3,1},{5,3},{7,5},{8,10},{10,12},{12,14},{11,9},... | collective-permute-start | bytes 1179656 | tf_op jit(solution)/shard_map/ppermute | solution.py:174
  125.2 15.8 %collective-permute-start.3 = (bf16[16,96,128]{2,1,0:T(8,128)(2,1)S(1)}, bf16[16,96,128]{2,1,0:T(8,128)(2,1)S(1)}, u32[]{:S(2)}, u32[]{:S(2)}) collective-permute-start(bf16[16,96,128]{2,1,0:T(8,128)(2,1)S(1)} %collective-permute-done.2.over_ref), channel_id=1, source_target_pairs={{0,2},{2,4},{4,6},{3,1},{5,3},{7,5},{8,10},{10,12},{12,14},{11,9},... | collective-permute-start | bytes 1179656 | tf_op jit(solution)/shard_map/ppermute | solution.py:174
  129.8 20.4 %collective-permute-start.5 = (bf16[16,96,128]{2,1,0:T(8,128)(2,1)S(1)}, bf16[16,96,128]{2,1,0:T(8,128)(2,1)S(1)}, u32[]{:S(2)}, u32[]{:S(2)}) collective-permute-start(bf16[16,96,128]{2,1,0:T(8,128)(2,1)S(1)} %collective-permute-done.4.over_ref), channel_id=1, source_target_pairs={{0,2},{2,4},{4,6},{3,1},{5,3},{7,5},{8,10},{10,12},{12,14},{11,9},... | collective-permute-start | bytes 1179656 | tf_op jit(solution)/shard_map/ppermute | solution.py:174
  131.8 4.0 %copy-start = (bf16[16,20,128,128]{3,2,1,0:T(8,128)(2,1)S(1)}, bf16[16,20,128,128]{3,2,1,0:T(8,128)(2,1)}, u32[]{:S(2)}) copy-start(bf16[16,20,128,128]{3,2,1,0:T(8,128)(2,1)} %param.7) | copy-start | bytes 31457284
  141.0 4.0 %copy-start.1 = (bf16[16,20,128,128]{3,2,1,0:T(8,128)(2,1)S(1)}, bf16[16,20,128,128]{3,2,1,0:T(8,128)(2,1)}, u32[]{:S(2)}) copy-start(bf16[16,20,128,128]{3,2,1,0:T(8,128)(2,1)} %param.7) | copy-start | bytes 31457284
  164.7 11.0 %copy-start.3 = (f32[128]{0:T(128)S(1)}, f32[128]{0:T(128)}, u32[]{:S(2)}) copy-start(f32[128]{0:T(128)} %param.11) | copy-start | bytes 1540
  164.7 11.2 %copy-start.2 = (f32[96]{0:T(128)S(1)}, f32[96]{0:T(128)}, u32[]{:S(2)}) copy-start(f32[96]{0:T(128)} %occ_ref.1) | copy-start | bytes 1156
  164.7 43.9 %all-to-all-start = ((f16[256,9,2,128]{3,2,1,0:T(2,128)(2,1)}), f16[256,9,2,128]{3,2,1,0:T(2,128)(2,1)}, u32[]{:S(2)}, u32[]{:S(2)}) async-start(f16[256,9,2,128]{3,2,1,0:T(2,128)(2,1)} %bitcast.12), calls=%async_computation | async-start | bytes 2359296 | tf_op jit(solution)/shard_map/all_to_all | solution.py:196

commit v2 on v1

v2 whole, which is shorter than its diff:
```python
import jax
import jax.numpy as jnp
from jax import lax
from jax.experimental import pallas as pl
from jax.experimental.pallas import tpu as pltpu
from jax.sharding import PartitionSpec as P

ROWS = 3
TILES = 16
VIRT = 8
LANES = 128
VALUES = ROWS * ROWS * TILES * TILES // LANES
MSG = VALUES + 2


def exchange_groups(parts):
    parts = list(parts)
    group = lax.broadcasted_iota(jnp.int32, parts[0].shape, 1) // TILES
    for step in (1, 2, 4):
        upper = (group & step) != 0
        for p in range(8):
            if p & step:
                continue
            low, high = parts[p], parts[p + step]
            parts[p] = jnp.where(upper, pltpu.roll(high, TILES * step, 1), low)
            parts[p + step] = jnp.where(upper, high, pltpu.roll(low, LANES - TILES * step, 1))
    return parts


def ladder_kernel(index_ref, own_ref, over_ref, next_ref, weight_ref, out_ref, held, picked, weights, arrived):
    group = weights.shape[1]
    slots = weight_ref.shape[1] // LANES

    def fetch(step):
        return pltpu.make_async_copy(
            weight_ref.at[pl.ds(step * group, group)], weights.at[step % 2], arrived.at[step % 2]
        )

    fetch(0).start()
    held[0:TILES] = own_ref[...]
    held[TILES : 2 * TILES] = over_ref[...]
    held[2 * TILES : 3 * TILES] = next_ref[...]
    held[3 * TILES] = jnp.zeros_like(held[3 * TILES])
    for step in range(TILES // group):
        if step + 1 < TILES // group:
            fetch(step + 1).start()
        fetch(step).wait()
        for n in range(group):
            a = step * group + n
            for s in range(slots):
                picked[n, :, s * LANES : (s + 1) * LANES] = held[index_ref[a, s]]
            row = jnp.dot(picked[n], weights[step % 2, n], preferred_element_type=jnp.float32)
            out_ref[pl.ds(a, row.shape[0], stride=TILES), :] = row


def ladder_rows(index, own, over, beyond, weights):
    tiles, pairs, depth = own.shape
    k = weights.shape[1]
    group = 4
    smem, vmem = pl.BlockSpec(memory_space=pltpu.SMEM), pl.BlockSpec(memory_space=pltpu.VMEM)
    return pl.pallas_call(
        ladder_kernel,
        out_shape=jax.ShapeDtypeStruct((pairs * tiles, LANES), jnp.float32),
        in_specs=[smem] + [vmem] * 3 + [pl.BlockSpec(memory_space=pltpu.HBM)],
        out_specs=vmem,
        scratch_shapes=[
            pltpu.VMEM((3 * tiles + 1, pairs, depth), jnp.bfloat16),
            pltpu.VMEM((group, pairs, k), jnp.bfloat16),
            pltpu.VMEM((2, group, k, LANES), jnp.bfloat16),
            pltpu.SemaphoreType.DMA((2,)),
        ],
        compiler_params=pltpu.CompilerParams(vmem_limit_bytes=20 * 2**20),
        cost_estimate=pl.CostEstimate(
            flops=2 * pairs * k * LANES * tiles, bytes_accessed=2 * tiles * k * LANES, transcendentals=0
        ),
        name="ladder_rows",
    )(index, own, over, beyond, weights)


def pack_kernel(ladder_ref, out_ref, rest):
    devices = out_ref.shape[0] // (VIRT * MSG)
    tile = ROWS * TILES
    row = devices * tile

    def widest(step, so_far):
        return jnp.maximum(so_far, jnp.abs(ladder_ref[pl.ds(pl.multiple_of(step * tile, TILES), tile), :]))

    largest = lax.fori_loop(0, ROWS * devices, widest, jnp.zeros((tile, LANES), jnp.float32), unroll=4)
    largest = jnp.maximum(jnp.max(jnp.max(largest, axis=0, keepdims=True), axis=1, keepdims=True), 1e-30)
    power = 14.0 - jnp.ceil(jnp.log2(jnp.broadcast_to(largest, (2, LANES))))
    scale = jnp.exp2(power)[:1]

    @pl.loop(0, devices // 8)
    def _(octet):
        for half in range(2):
            first = (ROWS - 1) * (row + TILES) + half * 8
            parts = [ladder_ref[pl.ds(octet * 8 * tile + first + n, 8, stride=tile), :] for n in range(8)]
            for v, part in enumerate(exchange_groups(parts)):
                rest[pl.ds(octet * 8 * TILES + 2 * v + half, 8, stride=TILES), :] = part

    @pl.loop(0, devices, unroll=2)
    def _(device):
        first = pl.multiple_of(device * tile, TILES)
        parts = [
            ladder_ref[pl.ds(first + (k // ROWS) * row + (k % ROWS) * TILES, TILES), :] * scale for k in range(8)
        ]
        last = rest[pl.ds(pl.multiple_of(device * TILES, TILES), TILES), :] * scale
        pieces = []
        for v, part in enumerate(exchange_groups(parts)):
            pieces += [part, last[2 * v : 2 * v + 2], power]
        out_ref[pl.ds(pl.multiple_of(device * VIRT * MSG, TILES), VIRT * MSG), :] = jnp.concatenate(pieces, axis=0)


def pack(ladder):
    rows = ladder.shape[0]
    vmem = pl.BlockSpec(memory_space=pltpu.VMEM)
    return pl.pallas_call(
        pack_kernel,
        out_shape=jax.ShapeDtypeStruct((rows // VALUES * MSG, LANES), jnp.float32),
        in_specs=[vmem],
        out_specs=vmem,
        scratch_shapes=[pltpu.VMEM((rows // (ROWS * ROWS), LANES), jnp.float32)],
        compiler_params=pltpu.CompilerParams(vmem_limit_bytes=12 * 2**20),
        cost_estimate=pl.CostEstimate(flops=rows * LANES * 32, bytes_accessed=rows * LANES * 8, transcendentals=0),
        name="pack",
    )(ladder)


def finish_kernel(got_ref, *refs):
    count = (len(refs) - 3) // 2
    own_refs, factor_refs = refs[:count], refs[count : 2 * count]
    out_ref, rest, turned = refs[2 * count :]
    begin = 0
    for own_ref, factor_ref in zip(own_refs, factor_refs):
        devices = own_ref.shape[1] // ROWS

        def store(i, j, partner, begin=begin, own_ref=own_ref, factor_ref=factor_ref):
            out_ref[i, begin * ROWS + j] = (own_ref[i, j] + partner * factor_ref[i, j]).astype(out_ref.dtype)

        @pl.loop(0, devices, unroll=2)
        def _(device, begin=begin, store=store):
            first = pl.multiple_of((begin + device) * VIRT * MSG, TILES)
            block = got_ref[pl.ds(first, VIRT * MSG), :].astype(jnp.float32)
            cut = [block[v * MSG : (v + 1) * MSG] for v in range(VIRT)]
            cut = [c[:VALUES] * jnp.exp2(-c[VALUES : VALUES + 1]) for c in cut]
            main = jnp.concatenate([c[:TILES] for c in cut], axis=0).T
            rest[pl.ds(pl.multiple_of(device * TILES, TILES), TILES), :] = jnp.concatenate(
                [c[TILES:] for c in cut], axis=0
            )
            for k in range(8):
                store(k % ROWS, device * ROWS + k // ROWS, main[k * TILES : (k + 1) * TILES])

        @pl.loop(0, devices // 8)
        def _(octet, store=store):
            for half in range(2):
                parts = [rest[pl.ds(octet * 8 * TILES + 2 * v + half, 8, stride=TILES), :] for v in range(VIRT)]
                for n, part in enumerate(exchange_groups(parts)):
                    turned[pl.ds(half * 8 + n, 8, stride=TILES), :] = part
            columns = turned[...].T
            parts = [columns[v * TILES : (v + 1) * TILES] for v in range(VIRT)]
            for n, part in enumerate(exchange_groups(parts)):
                store(ROWS - 1, (octet * 8 + n) * ROWS + ROWS - 1, part)

        begin += devices


def finish(got, owns, factors):
    partners = sum(own.shape[1] for own in owns)
    vmem = pl.BlockSpec(memory_space=pltpu.VMEM)
    return pl.pallas_call(
        finish_kernel,
        out_shape=jax.ShapeDtypeStruct((ROWS, partners, TILES, LANES), jnp.bfloat16),
        in_specs=[vmem] * (1 + 2 * len(owns)),
        out_specs=vmem,
        scratch_shapes=[
            pltpu.VMEM((got.shape[0] // MSG * 2, LANES), jnp.float32),
            pltpu.VMEM((LANES, LANES), jnp.float32),
        ],
        compiler_params=pltpu.CompilerParams(vmem_limit_bytes=12 * 2**20),
        cost_estimate=pl.CostEstimate(flops=2**25, bytes_accessed=2**23, transcendentals=0),
        name="finish",
    )(got, *owns, *factors)


def after_kernel(x_ref, first_ref, out_ref):
    out_ref[...] = x_ref[...]


def after(x, first):
    vmem = pl.BlockSpec(memory_space=pltpu.VMEM)
    return pl.pallas_call(
        after_kernel,
        out_shape=jax.ShapeDtypeStruct(x.shape, x.dtype),
        in_specs=[vmem, vmem],
        out_specs=vmem,
        compiler_params=pltpu.CompilerParams(vmem_limit_bytes=4 * 2**20),
        name="after",
    )(x, first)


CHUNKS = (8, 8, 8, 8)


def per_device(amplitudes, integrals, cd_tiles, tile_counts, eps_occ, eps_virt):
    rows, partners, tiles, depth = amplitudes.shape
    slots = integrals.shape[1]
    me = lax.axis_index("virt")
    swap = [(v, v ^ 1) for v in range(VIRT)]
    relay = [(v, v + 2) for v in range(0, VIRT - 2, 2)] + [(v, v - 2) for v in range(3, VIRT, 2)]
    own, begin = [], 0
    for devices in CHUNKS:
        part = amplitudes[:, begin * rows : (begin + devices) * rows]
        own.append(jnp.transpose(part, (2, 0, 1, 3)).reshape(tiles, rows * rows * devices, depth))
        begin += devices
    over, beyond = [], []
    for n in range(len(own)):
        if n >= 2:
            own[n] = after(own[n], over[n - 2])
        over.append(lax.ppermute(own[n], "virt", swap))
    for x in over:
        beyond.append(lax.ppermute(x, "virt", relay))

    live = lax.broadcasted_iota(jnp.int32, cd_tiles.shape, 1) < tile_counts[:, None]
    block = cd_tiles // tiles - me
    over_block = jnp.where(me % 2 == 0, 1, -1)
    place = jnp.where(block == 0, 0, jnp.where(block == over_block, 1, 2))
    index = jnp.where(live, place * tiles + cd_tiles % tiles, 3 * tiles).astype(jnp.int32)

    weights = integrals.reshape(tiles, slots * depth, LANES)
    ladders = [ladder_rows(index, *parts, weights) for parts in zip(own, over, beyond)]
    sent = jnp.zeros((partners // rows * VIRT * MSG, LANES), jnp.float16)
    begin = 0
    for devices, ladder in zip(CHUNKS, ladders):
        sent = lax.dynamic_update_slice(sent, pack(ladder).astype(jnp.float16), (begin * VIRT * MSG, 0))
        begin += devices
    sent = sent.reshape(-1, MSG // 2, 2, LANES)
    got = lax.all_to_all(sent, ("pair", "virt"), split_axis=0, concat_axis=0, tiled=True)
    own_occ = lax.dynamic_slice_in_dim(eps_occ, lax.axis_index("pair") * rows, rows)
    own_virt = lax.dynamic_slice_in_dim(eps_virt, me * tiles, tiles)
    owns, factors, begin = [], [], 0
    for devices, ladder in zip(CHUNKS, ladders):
        denominator = (
            own_occ[:, None, None, None]
            + eps_occ[None, begin * rows : (begin + devices) * rows, None, None]
            - own_virt[None, None, :, None]
            - eps_virt[None, None, None, :]
        )
        owns.append(ladder.reshape(rows, rows * devices, tiles, LANES) / denominator)
        factors.append(1.0 / denominator)
        begin += devices
    return finish(got.reshape(-1, LANES).astype(jnp.float32), owns, factors)


def solution(mesh):
    in_specs = (
        P("pair", None, "virt", None),
        P("virt", None, None, None),
        P("virt", None),
        P("virt"),
        P(),
        P(),
    )
    out_specs = P("pair", None, "virt", None)
    return jax.shard_map(
        per_device, mesh=mesh, in_specs=in_specs, out_specs=out_specs, check_vma=False
    )
```

time: 218 us -> 145 us (0.67)
  blocking collectives: 97.5 us -> 0 us
  starting transfers between devices: 32.2 us -> 53.5 us
  other arithmetic: 12 us -> 4.61 us
  waiting for transfers between devices: 32.7 us -> 39.4 us
  local copies, waits for them, and re-layouts: 10.6 us -> 16.2 us
    pmax x1 -> x0, blocking collectives: 97.5 us -> none  [per_device(): largest = lax.pmax(largest, ('pair', 'virt'))]
    all_to_all x1, starting transfers between devices: 11 us -> 26 us  [per_device(): lax.all_to_all(sent, ('pair', 'virt'), split_axis=0, concat_axis=0, tiled...]
    reduce_max x3 -> x0, other arithmetic: 8.04 us -> none  [the longest x1 6.62 us: per_device(): jnp.max(jnp.abs(integrals), axis=(2, 3))]
    ppermute x6 -> x8, waiting for transfers between devices: 0.02 us -> 7 us  [the longest x4 6.99 us: per_device(): over.append(lax.ppermute(own[n], 'virt', swap))]
    ppermute x6 -> x8, starting transfers between devices: 21.2 us -> 27.5 us  [the longest x4 14 us: per_device(): beyond.append(lax.ppermute(x, 'virt', relay))]
    transpose x0 -> x5, local copies, waits for them, and re-layouts: none -> 5.95 us  [per_device(): jnp.transpose(part, (2, 0, 1, 3))]
    pallas_call x3 -> x4, Pallas kernels: 15.5 us -> 20.2 us  [ladder_rows(): pl.pallas_call(ladder_kernel, out_shape=jax.ShapeDtypeStruct((pairs * til...]
    pallas_call x1 -> x6, Pallas kernels: 8.2 us -> 5.19 us  [the longest x4 5.15 us: pack(): pl.pallas_call(pack_kernel, out_shape=jax.ShapeDtypeStruct((rows // VALUE...]
  transfers between devices with their start and end apart: 7 -> 9, of which waited for: 1 -> 2; matrix products, arithmetic and copies ran while one was open for 5% -> 5% of each run, Pallas kernels for 5% -> 13%
where the time goes in v2:
time: 145 us
  starting transfers between devices  53.5 us (37%)
  waiting for transfers between devices  39.4 us (27%)
  Pallas kernels  30.5 us (21%)
  local copies, waits for them, and re-layouts  16.2 us (11%)
  other arithmetic  4.61 us (3%)
    all_to_all x1, waiting for transfers between devices, per_device(): lax.all_to_all(sent, ('pair', 'virt'), split_axis=0, concat_axis=0, tiled...  32.4 us
    all_to_all x1, starting transfers between devices, per_device(): lax.all_to_all(sent, ('pair', 'virt'), split_axis=0, concat_axis=0, tiled...  26 us
    pallas_call x4, Pallas kernels, ladder_rows(): pl.pallas_call(ladder_kernel, out_shape=jax.ShapeDtypeStruct((pairs * til...  20.2 us
    ppermute x4, starting transfers between devices, per_device(): beyond.append(lax.ppermute(x, 'virt', relay))  14 us
    ppermute x4, starting transfers between devices, per_device(): over.append(lax.ppermute(own[n], 'virt', swap))  13.5 us
    unnamed x56, local copies, waits for them, and re-layouts  9.85 us
    ppermute x4, waiting for transfers between devices, per_device(): over.append(lax.ppermute(own[n], 'virt', swap))  6.99 us
    transpose x5, local copies, waits for them, and re-layouts, per_device(): jnp.transpose(part, (2, 0, 1, 3))  5.95 us
  transfers between devices with their start and end apart: 9, of which 2 were waited for; matrix products, arithmetic and copies ran while one was open for 5% of the time, Pallas kernels for 13%

profile of v2, /device:TPU:1, one launch (start us, length us, event | category | flops | bytes accessed | tf_op | source)
XLA Modules:
  0.0 144.6 jit_solution(5845896948872104781)
XLA Ops:
  0.0 2.3 %slice_bitcast_fusion = (bf16[16,3,24,128]{3,0,2,1:T(8,128)(2,1)}, bf16[16,3,24,128]{3,0,2,1:T(8,128)(2,1)S(1)}, bf16[16,3,24,128]{3,0,2,1:T(8,128)(2,1)S(1)}, bf16[16,3,24,128]{3,0,2,1:T(8,128)(2,1)}) fusion(bf16[3,96,16,128]{3,2,1,0:T(8,128)(2,1)} %param.6), kind=kLoop, calls=%fused_computation.11 | loop fusion | bytes 2359296 | tf_op jit(solution)/shard_map/transpose | solution.py:213
  2.4 7.8 %collective-permute-start = (bf16[16,72,128]{2,1,0:T(8,128)(2,1)S(1)}, bf16[16,72,128]{2,1,0:T(8,128)(2,1)S(1)}, u32[]{:S(2)}, u32[]{:S(2)}) collective-permute-start(bf16[16,72,128]{2,1,0:T(8,128)(2,1)S(1)} %bitcast.32), channel_id=1, source_target_pairs={{0,1},{1,0},{2,3},{3,2},{4,5},{5,4},{6,7},{7,6},{8,9},{9,8},{10,11... | collective-permute-start | bytes 884744 | tf_op jit(solution)/shard_map/ppermute | solution.py:219
  10.4 7.0 %collective-permute-done.over_ref.first_ref = bf16[16,72,128]{2,1,0:T(8,128)(2,1)S(1)} collective-permute-done((bf16[16,72,128]{2,1,0:T(8,128)(2,1)S(1)}, bf16[16,72,128]{2,1,0:T(8,128)(2,1)S(1)}, u32[]{:S(2)}, u32[]{:S(2)}) %collective-permute-start) | collective-permute-done | bytes 294944 | tf_op jit(solution)/shard_map/ppermute | solution.py:219
  17.4 4.5 %collective-permute-start.1 = (bf16[16,72,128]{2,1,0:T(8,128)(2,1)S(1)}, bf16[16,72,128]{2,1,0:T(8,128)(2,1)}, u32[]{:S(2)}, u32[]{:S(2)}) collective-permute-start(bf16[16,72,128]{2,1,0:T(8,128)(2,1)S(1)} %collective-permute-done.over_ref.first_ref), channel_id=1, source_target_pairs={{0,2},{2,4},{4,6},{3,1},{5,3},{7,5},{8,10},{10,12},{12,14},{11,9},... | collective-permute-start | bytes 884744 | tf_op jit(solution)/shard_map/ppermute | solution.py:221
  21.8 1.7 %copy.10 = bf16[16,3,24,128]{3,2,1,0:T(8,128)(2,1)} copy(bf16[16,3,24,128]{3,0,2,1:T(8,128)(2,1)} %get-tuple-element.5) | data formatting | bytes 589824 | tf_op jit(solution)/shard_map/transpose | solution.py:213
  23.6 1.8 %copy.9 = bf16[16,3,24,128]{3,2,1,0:T(8,128)(2,1)} copy(bf16[16,3,24,128]{3,0,2,1:T(8,128)(2,1)} %get-tuple-element.8) | data formatting | bytes 589824 | tf_op jit(solution)/shard_map/transpose | solution.py:213
  26.5 5.2 %collective-permute-start.6 = (bf16[16,72,128]{2,1,0:T(8,128)(2,1)S(1)}, bf16[16,72,128]{2,1,0:T(8,128)(2,1)S(1)}, u32[]{:S(2)}, u32[]{:S(2)}) collective-permute-start(bf16[16,72,128]{2,1,0:T(8,128)(2,1)S(1)} %after.3.own_ref), channel_id=1, source_target_pairs={{0,1},{1,0},{2,3},{3,2},{4,5},{5,4},{6,7},{7,6},{8,9},{9,8},{10,11... | collective-permute-start | bytes 884744 | tf_op jit(solution)/shard_map/ppermute | solution.py:219
  33.0 3.2 %collective-permute-start.3 = (bf16[16,72,128]{2,1,0:T(8,128)(2,1)S(1)}, bf16[16,72,128]{2,1,0:T(8,128)(2,1)S(1)}, u32[]{:S(2)}, u32[]{:S(2)}) collective-permute-start(bf16[16,72,128]{2,1,0:T(8,128)(2,1)S(1)} %collective-permute-done.2.over_ref.first_ref), channel_id=1, source_target_pairs={{0,2},{2,4},{4,6},{3,1},{5,3},{7,5},{8,10},{10,12},{12,14},{11,9},... | collective-permute-start | bytes 884744 | tf_op jit(solution)/shard_map/ppermute | solution.py:221
  36.4 4.0 %copy-done = bf16[16,20,128,128]{3,2,1,0:T(8,128)(2,1)S(1)} copy-done((bf16[16,20,128,128]{3,2,1,0:T(8,128)(2,1)S(1)}, bf16[16,20,128,128]{3,2,1,0:T(8,128)(2,1)}, u32[]{:S(2)}) %copy-start) | copy-done | bytes 10485784
  41.3 5.4 %ladder_rows.4.ladder_ref = f32[1152,128]{1,0:T(8,128)S(1)} custom-call(s32[16,20]{1,0:T(8,128)S(1)} %fusion.2.index_ref, bf16[16,72,128]{2,1,0:T(8,128)(2,1)S(1)} %bitcast.33, bf16[16,72,128]{2,1,0:T(8,128)(2,1)S(1)} %collective-permute-done.over_ref.first_ref, bf16[16,72,128]{2,1,0:T(8,128)(2,1)} %collective-permute-done.1.next_ref, ...), custom_call_target="tpu_custom_call" | custom-call | flops 754974720 | bytes 10485760 | tf_op jit(solution)/shard_map/ladder_rows/pallas_call | solution.py:61
  46.7 1.3 pack.4
  48.3 3.2 %collective-permute-start.7 = (bf16[16,72,128]{2,1,0:T(8,128)(2,1)S(1)}, bf16[16,72,128]{2,1,0:T(8,128)(2,1)S(1)}, u32[]{:S(2)}, u32[]{:S(2)}) collective-permute-start(bf16[16,72,128]{2,1,0:T(8,128)(2,1)S(1)} %collective-permute-done.6.over_ref), channel_id=1, source_target_pairs={{0,2},{2,4},{4,6},{3,1},{5,3},{7,5},{8,10},{10,12},{12,14},{11,9},... | collective-permute-start | bytes 884744 | tf_op jit(solution)/shard_map/ppermute | solution.py:221
  51.6 5.0 %ladder_rows.5.ladder_ref = f32[1152,128]{1,0:T(8,128)S(1)} custom-call(s32[16,20]{1,0:T(8,128)S(1)} %fusion.2.index_ref, bf16[16,72,128]{2,1,0:T(8,128)(2,1)S(1)} %bitcast.31, bf16[16,72,128]{2,1,0:T(8,128)(2,1)S(1)} %copy-done.13, bf16[16,72,128]{2,1,0:T(8,128)(2,1)S(1)} %collective-permute-done.3.next_ref, bf16[16,2560,128]{2,1,0:T(8,128)(2,1)S(1)} %bitcast.23), custom_call_target="tpu_custom_call" | custom-call | flops 754974720 | bytes 10485760 | tf_op jit(solution)/shard_map/ladder_rows/pallas_call | solution.py:61
  56.6 1.3 pack.5
  57.9 3.1 %collective-permute-start.5 = (bf16[16,72,128]{2,1,0:T(8,128)(2,1)S(1)}, bf16[16,72,128]{2,1,0:T(8,128)(2,1)S(1)}, u32[]{:S(2)}, u32[]{:S(2)}) collective-permute-start(bf16[16,72,128]{2,1,0:T(8,128)(2,1)S(1)} %collective-permute-done.4.over_ref), channel_id=1, source_target_pairs={{0,2},{2,4},{4,6},{3,1},{5,3},{7,5},{8,10},{10,12},{12,14},{11,9},... | collective-permute-start | bytes 884744 | tf_op jit(solution)/shard_map/ppermute | solution.py:221
  61.1 4.9 %ladder_rows.7.ladder_ref = f32[1152,128]{1,0:T(8,128)S(1)} custom-call(s32[16,20]{1,0:T(8,128)S(1)} %fusion.2.index_ref, bf16[16,72,128]{2,1,0:T(8,128)(2,1)S(1)} %after.3.own_ref, bf16[16,72,128]{2,1,0:T(8,128)(2,1)S(1)} %collective-permute-done.6.over_ref, bf16[16,72,128]{2,1,0:T(8,128)(2,1)S(1)} %collective-permute-done.7.next_ref, ...), custom_call_target="tpu_custom_call" | custom-call | flops 754974720 | bytes 10485760 | tf_op jit(solution)/shard_map/ladder_rows/pallas_call | solution.py:61
  66.0 1.3 pack.7
  67.3 4.9 %ladder_rows.6.ladder_ref = f32[1152,128]{1,0:T(8,128)S(1)} custom-call(s32[16,20]{1,0:T(8,128)S(1)} %fusion.2.index_ref, bf16[16,72,128]{2,1,0:T(8,128)(2,1)S(1)} %after.2.own_ref, bf16[16,72,128]{2,1,0:T(8,128)(2,1)S(1)} %collective-permute-done.4.over_ref, bf16[16,72,128]{2,1,0:T(8,128)(2,1)S(1)} %collective-permute-done.5.next_ref, ...), custom_call_target="tpu_custom_call" | custom-call | flops 754974720 | bytes 10485760 | tf_op jit(solution)/shard_map/ladder_rows/pallas_call | solution.py:61
  72.3 1.3 pack.6
  74.9 26.0 %all-to-all-start = ((f16[256,10,2,128]{3,2,1,0:T(2,128)(2,1)}), f16[256,10,2,128]{3,2,1,0:T(2,128)(2,1)}, u32[]{:S(2)}, u32[]{:S(2)}) async-start(f16[256,10,2,128]{3,2,1,0:T(2,128)(2,1)} %bitcast.36), calls=%async_computation | async-start | bytes 2621440 | tf_op jit(solution)/shard_map/all_to_all | solution.py:237
  101.3 2.4 %subtract_divide_fusion = (f32[3,24,16,128]{3,2,1,0:T(8,128)S(1)}, f32[3,24,16,128]{3,2,1,0:T(8,128)}, f32[3,24,16,128]{3,2,1,0:T(8,128)}, f32[3,24,16,128]{3,2,...) fusion(f32[3,24,16]{2,1,0:T(8,128)S(1)} %get-tuple-element.23, ...), kind=kLoop, calls=%fused_computation | loop fusion | flops 1769472 | bytes 7096832 | tf_op jit(solution)/shard_map/div | solution.py:249
  103.7 32.4 %all-to-all-done = f16[256,10,2,128]{3,2,1,0:T(2,128)(2,1)} async-done(((f16[256,10,2,128]{3,2,1,0:T(2,128)(2,1)}), f16[256,10,2,128]{3,2,1,0:T(2,128)(2,1)}, u32[]{:S(2)}, u32[]{:S(2)}) %all-to-all-start) | async-done | bytes 1310752 | tf_op jit(solution)/shard_map/all_to_all | solution.py:237
  136.2 1.6 %convert.1.got_ref = f32[5120,128]{1,0:T(8,128)S(1)} convert(f16[5120,128]{1,0:T(8,128)(2,1)} %bitcast.15) | non-fusion elementwise | flops 655360 | bytes 3932160 | tf_op jit(solution)/shard_map/convert_element_type | solution.py:251
  139.5 5.0 %finish.1 = bf16[3,96,16,128]{3,2,1,0:T(8,128)(2,1)} custom-call(f32[5120,128]{1,0:T(8,128)S(1)} %convert.1.got_ref, f32[3,24,16,128]{3,2,1,0:T(8,128)S(1)} %copy-done.10, f32[3,24,16,128]{3,2,1,0:T(8,128)S(1)} %copy-done.8, f32[3,24,16,128]{3,2,1,0:T(8,128)S(1)} %copy-done.6, f32[3,24,16,128]{3,2,1,0:T(8,128)S(1)} %copy-done.5, ...), custom_call_target="tpu_custom_call" | custom-call | flops 33554432 | bytes 8388608 | tf_op jit(solution)/shard_map/finish/pallas_call | solution.py:170
  (80 shorter events, 7.4 us)
Async XLA Ops:
  2.3 49.3 %slice-start = ((s8[10485760]{0:T(1024)(128)(4,1)}), s8[2097152]{0:T(1024)(128)(4,1)S(1)}, s32[]{:S(2)}) async-start(s8[10485760]{0:T(1024)(128)(4,1)} %bitcast.21), calls=%async_computation.1 | async-start | bytes 4194304
  2.4 24.1 %copy-start.16 = (bf16[16,3,24,128]{3,2,1,0:T(8,128)(2,1)}, bf16[16,3,24,128]{3,2,1,0:T(8,128)(2,1)S(1)}, u32[]{:S(2)}) copy-start(bf16[16,3,24,128]{3,2,1,0:T(8,128)(2,1)S(1)} %copy.7) | copy-start | bytes 884740
  2.4 15.0 %collective-permute-start = (bf16[16,72,128]{2,1,0:T(8,128)(2,1)S(1)}, bf16[16,72,128]{2,1,0:T(8,128)(2,1)S(1)}, u32[]{:S(2)}, u32[]{:S(2)}) collective-permute-start(bf16[16,72,128]{2,1,0:T(8,128)(2,1)S(1)} %bitcast.32), channel_id=1, source_target_pairs={{0,1},{1,0},{2,3},{3,2},{4,5},{5,4},{6,7},{7,6},{8,9},{9,8},{10,11... | collective-permute-start | bytes 884744 | tf_op jit(solution)/shard_map/ppermute | solution.py:219
  10.3 22.4 %copy-start.14 = (bf16[16,3,24,128]{3,2,1,0:T(8,128)(2,1)}, bf16[16,3,24,128]{3,2,1,0:T(8,128)(2,1)S(1)}, u32[]{:S(2)}) copy-start(bf16[16,3,24,128]{3,2,1,0:T(8,128)(2,1)S(1)} %copy.8) | copy-start | bytes 884740
  10.3 15.1 %collective-permute-start.2 = (bf16[16,72,128]{2,1,0:T(8,128)(2,1)S(1)}, bf16[16,72,128]{2,1,0:T(8,128)(2,1)S(1)}, u32[]{:S(2)}, u32[]{:S(2)}) collective-permute-start(bf16[16,72,128]{2,1,0:T(8,128)(2,1)S(1)} %bitcast.30), channel_id=1, source_target_pairs={{0,1},{1,0},{2,3},{3,2},{4,5},{5,4},{6,7},{7,6},{8,9},{9,8},{10,11... | collective-permute-start | bytes 884744 | tf_op jit(solution)/shard_map/ppermute | solution.py:219
  17.4 19.0 %collective-permute-start.1 = (bf16[16,72,128]{2,1,0:T(8,128)(2,1)S(1)}, bf16[16,72,128]{2,1,0:T(8,128)(2,1)}, u32[]{:S(2)}, u32[]{:S(2)}) collective-permute-start(bf16[16,72,128]{2,1,0:T(8,128)(2,1)S(1)} %collective-permute-done.over_ref.first_ref), channel_id=1, source_target_pairs={{0,2},{2,4},{4,6},{3,1},{5,3},{7,5},{8,10},{10,12},{12,14},{11,9},... | collective-permute-start | bytes 884744 | tf_op jit(solution)/shard_map/ppermute | solution.py:221
  23.6 12.7 %copy-start.21 = (s32[16,20]{1,0:T(8,128)S(1)}, s32[16,20]{1,0:T(8,128)}, u32[]{:S(2)}) copy-start(s32[16,20]{1,0:T(8,128)} %param.8) | copy-start | bytes 3844
  23.6 12.7 %copy-start.24 = (s32[16]{0:T(128)S(1)}, s32[16]{0:T(128)}, u32[]{:S(2)}) copy-start(s32[16]{0:T(128)} %param.9) | copy-start | bytes 196
  25.4 21.4 %copy-start.12 = (bf16[16,72,128]{2,1,0:T(8,128)(2,1)}, bf16[16,72,128]{2,1,0:T(8,128)(2,1)S(1)}, u32[]{:S(2)}) copy-start(bf16[16,72,128]{2,1,0:T(8,128)(2,1)S(1)} %collective-permute-done.2.over_ref.first_ref) | copy-start | bytes 884740
  26.5 21.8 %collective-permute-start.6 = (bf16[16,72,128]{2,1,0:T(8,128)(2,1)S(1)}, bf16[16,72,128]{2,1,0:T(8,128)(2,1)S(1)}, u32[]{:S(2)}, u32[]{:S(2)}) collective-permute-start(bf16[16,72,128]{2,1,0:T(8,128)(2,1)S(1)} %after.3.own_ref), channel_id=1, source_target_pairs={{0,1},{1,0},{2,3},{3,2},{4,5},{5,4},{6,7},{7,6},{8,9},{9,8},{10,11... | collective-permute-start | bytes 884744 | tf_op jit(solution)/shard_map/ppermute | solution.py:219
  32.7 25.2 %collective-permute-start.4 = (bf16[16,72,128]{2,1,0:T(8,128)(2,1)S(1)}, bf16[16,72,128]{2,1,0:T(8,128)(2,1)S(1)}, u32[]{:S(2)}, u32[]{:S(2)}) collective-permute-start(bf16[16,72,128]{2,1,0:T(8,128)(2,1)S(1)} %after.2.own_ref), channel_id=1, source_target_pairs={{0,1},{1,0},{2,3},{3,2},{4,5},{5,4},{6,7},{7,6},{8,9},{9,8},{10,11... | collective-permute-start | bytes 884744 | tf_op jit(solution)/shard_map/ppermute | solution.py:219
  33.0 18.5 %collective-permute-start.3 = (bf16[16,72,128]{2,1,0:T(8,128)(2,1)S(1)}, bf16[16,72,128]{2,1,0:T(8,128)(2,1)S(1)}, u32[]{:S(2)}, u32[]{:S(2)}) collective-permute-start(bf16[16,72,128]{2,1,0:T(8,128)(2,1)S(1)} %collective-permute-done.2.over_ref.first_ref), channel_id=1, source_target_pairs={{0,2},{2,4},{4,6},{3,1},{5,3},{7,5},{8,10},{10,12},{12,14},{11,9},... | collective-permute-start | bytes 884744 | tf_op jit(solution)/shard_map/ppermute | solution.py:221
  36.4 4.0 %copy-start = (bf16[16,20,128,128]{3,2,1,0:T(8,128)(2,1)S(1)}, bf16[16,20,128,128]{3,2,1,0:T(8,128)(2,1)}, u32[]{:S(2)}) copy-start(bf16[16,20,128,128]{3,2,1,0:T(8,128)(2,1)} %param.7) | copy-start | bytes 31457284
  41.3 10.2 %slice-start.1 = ((s8[10485760]{0:T(1024)(128)(4,1)}), s8[4194304]{0:T(1024)(128)(4,1)S(1)}, s32[]{:S(2)}) async-start(s8[10485760]{0:T(1024)(128)(4,1)} %bitcast.21), calls=%async_computation.2 | async-start | bytes 8388608
  41.3 10.2 %slice-start.2 = ((s8[10485760]{0:T(1024)(128)(4,1)}), s8[4194304]{0:T(1024)(128)(4,1)S(1)}, s32[]{:S(2)}) async-start(s8[10485760]{0:T(1024)(128)(4,1)} %bitcast.21), calls=%async_computation.3 | async-start | bytes 8388608
  48.0 3.5 %copy-start.13 = (bf16[16,72,128]{2,1,0:T(8,128)(2,1)S(1)}, bf16[16,72,128]{2,1,0:T(8,128)(2,1)}, u32[]{:S(2)}) copy-start(bf16[16,72,128]{2,1,0:T(8,128)(2,1)} %copy-done.12) | copy-start | bytes 884740
  48.3 12.7 %collective-permute-start.7 = (bf16[16,72,128]{2,1,0:T(8,128)(2,1)S(1)}, bf16[16,72,128]{2,1,0:T(8,128)(2,1)S(1)}, u32[]{:S(2)}, u32[]{:S(2)}) collective-permute-start(bf16[16,72,128]{2,1,0:T(8,128)(2,1)S(1)} %collective-permute-done.6.over_ref), channel_id=1, source_target_pairs={{0,2},{2,4},{4,6},{3,1},{5,3},{7,5},{8,10},{10,12},{12,14},{11,9},... | collective-permute-start | bytes 884744 | tf_op jit(solution)/shard_map/ppermute | solution.py:221
  57.9 9.5 %collective-permute-start.5 = (bf16[16,72,128]{2,1,0:T(8,128)(2,1)S(1)}, bf16[16,72,128]{2,1,0:T(8,128)(2,1)S(1)}, u32[]{:S(2)}, u32[]{:S(2)}) collective-permute-start(bf16[16,72,128]{2,1,0:T(8,128)(2,1)S(1)} %collective-permute-done.4.over_ref), channel_id=1, source_target_pairs={{0,2},{2,4},{4,6},{3,1},{5,3},{7,5},{8,10},{10,12},{12,14},{11,9},... | collective-permute-start | bytes 884744 | tf_op jit(solution)/shard_map/ppermute | solution.py:221
  66.0 6.3 %copy-start.1 = (f32[1152,128]{1,0:T(8,128)}, f32[1152,128]{1,0:T(8,128)S(1)}, u32[]{:S(2)}) copy-start(f32[1152,128]{1,0:T(8,128)S(1)} %ladder_rows.7.ladder_ref) | copy-start | bytes 1769476
  74.8 26.0 %copy-start.22 = (f32[96]{0:T(128)S(1)}, f32[96]{0:T(128)}, u32[]{:S(2)}) copy-start(f32[96]{0:T(128)} %param.10) | copy-start | bytes 1156
  74.8 26.1 %copy-start.23 = (f32[128]{0:T(128)S(1)}, f32[128]{0:T(128)}, u32[]{:S(2)}) copy-start(f32[128]{0:T(128)} %param.11) | copy-start | bytes 1540
  74.9 26.4 %copy-start.2 = (f32[1152,128]{1,0:T(8,128)S(1)}, f32[1152,128]{1,0:T(8,128)}, u32[]{:S(2)}) copy-start(f32[1152,128]{1,0:T(8,128)} %copy-done.1) | copy-start | bytes 1769476
  74.9 26.4 %copy-start.4 = (f32[1152,128]{1,0:T(8,128)S(1)}, f32[1152,128]{1,0:T(8,128)}, u32[]{:S(2)}) copy-start(f32[1152,128]{1,0:T(8,128)} %copy-done.3) | copy-start | bytes 1769476
  74.9 61.3 %all-to-all-start = ((f16[256,10,2,128]{3,2,1,0:T(2,128)(2,1)}), f16[256,10,2,128]{3,2,1,0:T(2,128)(2,1)}, u32[]{:S(2)}, u32[]{:S(2)}) async-start(f16[256,10,2,128]{3,2,1,0:T(2,128)(2,1)} %bitcast.36), calls=%async_computation | async-start | bytes 2621440 | tf_op jit(solution)/shard_map/all_to_all | solution.py:237
  (13 other events, 21.8 us)

commit v3 on v2

--- a/solution.py
+++ b/solution.py
@@ -1,3 +1,5 @@
+import functools
+
 import jax
 import jax.numpy as jnp
 from jax import lax
@@ -27,7 +29,12 @@
     return parts
 
 
-def ladder_kernel(index_ref, own_ref, over_ref, next_ref, weight_ref, out_ref, held, picked, weights, arrived):
+def ladder_kernel(pieces, index_ref, *refs):
+    own_ref, over_refs, next_refs = refs[0], refs[1 : 1 + pieces], refs[1 + pieces : 1 + 2 * pieces]
+    ladder_body(index_ref, own_ref, over_refs, next_refs, *refs[1 + 2 * pieces :])
+
+
+def ladder_body(index_ref, own_ref, over_refs, next_refs, weight_ref, out_ref, held, weights, arrived):
     group = weights.shape[1]
     slots = weight_ref.shape[1] // LANES
 
@@ -38,8 +45,10 @@
 
     fetch(0).start()
     held[0:TILES] = own_ref[...]
-    held[TILES : 2 * TILES] = over_ref[...]
-    held[2 * TILES : 3 * TILES] = next_ref[...]
+    for n, (over_ref, next_ref) in enumerate(zip(over_refs, next_refs)):
+        count = over_ref.shape[0]
+        held[TILES + n * count : TILES + (n + 1) * count] = over_ref[...]
+        held[2 * TILES + n * count : 2 * TILES + (n + 1) * count] = next_ref[...]
     held[3 * TILES] = jnp.zeros_like(held[3 * TILES])
     for step in range(TILES // group):
         if step + 1 < TILES // group:
@@ -47,9 +56,12 @@
         fetch(step).wait()
         for n in range(group):
             a = step * group + n
-            for s in range(slots):
-                picked[n, :, s * LANES : (s + 1) * LANES] = held[index_ref[a, s]]
-            row = jnp.dot(picked[n], weights[step % 2, n], preferred_element_type=jnp.float32)
+            row = None
+            for s in range(0, slots, 4):
+                four = jnp.concatenate([held[index_ref[a, s + t]] for t in range(4)], axis=1)
+                part = weights[step % 2, n, s * LANES : (s + 4) * LANES]
+                term = jnp.dot(four, part, preferred_element_type=jnp.float32)
+                row = term if row is None else row + term
             out_ref[pl.ds(a, row.shape[0], stride=TILES), :] = row
 
 
@@ -59,22 +71,21 @@
     group = 4
     smem, vmem = pl.BlockSpec(memory_space=pltpu.SMEM), pl.BlockSpec(memory_space=pltpu.VMEM)
     return pl.pallas_call(
-        ladder_kernel,
+        functools.partial(ladder_kernel, len(over)),
         out_shape=jax.ShapeDtypeStruct((pairs * tiles, LANES), jnp.float32),
-        in_specs=[smem] + [vmem] * 3 + [pl.BlockSpec(memory_space=pltpu.HBM)],
+        in_specs=[smem] + [vmem] * (1 + 2 * len(over)) + [pl.BlockSpec(memory_space=pl.ANY)],
         out_specs=vmem,
         scratch_shapes=[
             pltpu.VMEM((3 * tiles + 1, pairs, depth), jnp.bfloat16),
-            pltpu.VMEM((group, pairs, k), jnp.bfloat16),
             pltpu.VMEM((2, group, k, LANES), jnp.bfloat16),
             pltpu.SemaphoreType.DMA((2,)),
         ],
-        compiler_params=pltpu.CompilerParams(vmem_limit_bytes=20 * 2**20),
+        compiler_params=pltpu.CompilerParams(vmem_limit_bytes=48 * 2**20),
         cost_estimate=pl.CostEstimate(
             flops=2 * pairs * k * LANES * tiles, bytes_accessed=2 * tiles * k * LANES, transcendentals=0
         ),
         name="ladder_rows",
-    )(index, own, over, beyond, weights)
+    )(index, own, *over, *beyond, weights)
 
 
 def pack_kernel(ladder_ref, out_ref, rest):
@@ -126,60 +137,42 @@
     )(ladder)
 
 
-def finish_kernel(got_ref, *refs):
-    count = (len(refs) - 3) // 2
-    own_refs, factor_refs = refs[:count], refs[count : 2 * count]
-    out_ref, rest, turned = refs[2 * count :]
-    begin = 0
-    for own_ref, factor_ref in zip(own_refs, factor_refs):
-        devices = own_ref.shape[1] // ROWS
-
-        def store(i, j, partner, begin=begin, own_ref=own_ref, factor_ref=factor_ref):
-            out_ref[i, begin * ROWS + j] = (own_ref[i, j] + partner * factor_ref[i, j]).astype(out_ref.dtype)
-
-        @pl.loop(0, devices, unroll=2)
-        def _(device, begin=begin, store=store):
-            first = pl.multiple_of((begin + device) * VIRT * MSG, TILES)
-            block = got_ref[pl.ds(first, VIRT * MSG), :].astype(jnp.float32)
-            cut = [block[v * MSG : (v + 1) * MSG] for v in range(VIRT)]
-            cut = [c[:VALUES] * jnp.exp2(-c[VALUES : VALUES + 1]) for c in cut]
-            main = jnp.concatenate([c[:TILES] for c in cut], axis=0).T
-            rest[pl.ds(pl.multiple_of(device * TILES, TILES), TILES), :] = jnp.concatenate(
-                [c[TILES:] for c in cut], axis=0
-            )
-            for k in range(8):
-                store(k % ROWS, device * ROWS + k // ROWS, main[k * TILES : (k + 1) * TILES])
-
-        @pl.loop(0, devices // 8)
-        def _(octet, store=store):
-            for half in range(2):
-                parts = [rest[pl.ds(octet * 8 * TILES + 2 * v + half, 8, stride=TILES), :] for v in range(VIRT)]
-                for n, part in enumerate(exchange_groups(parts)):
-                    turned[pl.ds(half * 8 + n, 8, stride=TILES), :] = part
-            columns = turned[...].T
-            parts = [columns[v * TILES : (v + 1) * TILES] for v in range(VIRT)]
-            for n, part in enumerate(exchange_groups(parts)):
-                store(ROWS - 1, (octet * 8 + n) * ROWS + ROWS - 1, part)
-
-        begin += devices
-
-
-def finish(got, owns, factors):
-    partners = sum(own.shape[1] for own in owns)
-    vmem = pl.BlockSpec(memory_space=pltpu.VMEM)
+def finish_kernel(got_ref, own_ref, factor_ref, out_ref, rest, turned):
+    def store(i, j, partner):
+        out_ref[i, j] = (own_ref[i, j] + partner * factor_ref[i, j]).astype(out_ref.dtype)
+
+    for device in range(8):
+        block = got_ref[device * VIRT * MSG : (device + 1) * VIRT * MSG, :]
+        cut = [block[v * MSG : (v + 1) * MSG] for v in range(VIRT)]
+        cut = [c[:VALUES] * jnp.exp2(-c[VALUES : VALUES + 1]) for c in cut]
+        main = jnp.concatenate([c[:TILES] for c in cut], axis=0).T
+        rest[device * TILES : (device + 1) * TILES, :] = jnp.concatenate([c[TILES:] for c in cut], axis=0)
+        for k in range(8):
+            store(k % ROWS, device * ROWS + k // ROWS, main[k * TILES : (k + 1) * TILES])
+    for half in range(2):
+        parts = [rest[pl.ds(2 * v + half, 8, stride=TILES), :] for v in range(VIRT)]
+        for n, part in enumerate(exchange_groups(parts)):
+            turned[pl.ds(half * 8 + n, 8, stride=TILES), :] = part
+    columns = turned[...].T
+    parts = [columns[v * TILES : (v + 1) * TILES] for v in range(VIRT)]
+    for n, part in enumerate(exchange_groups(parts)):
+        store(ROWS - 1, n * ROWS + ROWS - 1, part)
+
+
+def finish(got, own, factor):
+    rows, partners = own.shape[:2]
+    tile = pl.BlockSpec((rows, 8 * rows, TILES, LANES), lambda g: (0, g, 0, 0))
     return pl.pallas_call(
         finish_kernel,
-        out_shape=jax.ShapeDtypeStruct((ROWS, partners, TILES, LANES), jnp.bfloat16),
-        in_specs=[vmem] * (1 + 2 * len(owns)),
-        out_specs=vmem,
-        scratch_shapes=[
-            pltpu.VMEM((got.shape[0] // MSG * 2, LANES), jnp.float32),
-            pltpu.VMEM((LANES, LANES), jnp.float32),
-        ],
+        out_shape=jax.ShapeDtypeStruct(own.shape, jnp.bfloat16),
+        grid=(partners // (8 * rows),),
+        in_specs=[pl.BlockSpec((8 * VIRT * MSG, LANES), lambda g: (g, 0)), tile, tile],
+        out_specs=tile,
+        scratch_shapes=[pltpu.VMEM((8 * TILES, LANES), jnp.float32), pltpu.VMEM((LANES, LANES), jnp.float32)],
         compiler_params=pltpu.CompilerParams(vmem_limit_bytes=12 * 2**20),
         cost_estimate=pl.CostEstimate(flops=2**25, bytes_accessed=2**23, transcendentals=0),
         name="finish",
-    )(got, *owns, *factors)
+    )(got, own, factor)
 
 
 def after_kernel(x_ref, first_ref, out_ref):
@@ -198,7 +191,8 @@
     )(x, first)
 
 
-CHUNKS = (8, 8, 8, 8)
+CHUNKS = (16, 8, 8)
+PIECES = (2, 1, 1)
 
 
 def per_device(amplitudes, integrals, cd_tiles, tile_counts, eps_occ, eps_virt):
@@ -212,13 +206,17 @@
         part = amplitudes[:, begin * rows : (begin + devices) * rows]
         own.append(jnp.transpose(part, (2, 0, 1, 3)).reshape(tiles, rows * rows * devices, depth))
         begin += devices
-    over, beyond = [], []
-    for n in range(len(own)):
-        if n >= 2:
-            own[n] = after(own[n], over[n - 2])
-        over.append(lax.ppermute(own[n], "virt", swap))
-    for x in over:
-        beyond.append(lax.ppermute(x, "virt", relay))
+    over, beyond, order = [], [], []
+    for part, pieces in zip(own, PIECES):
+        count = tiles // pieces
+        over.append([])
+        for n in range(pieces):
+            piece = part[n * count : (n + 1) * count]
+            if len(order) >= 2:
+                piece = after(piece, order[-2])
+            order.append(lax.ppermute(piece, "virt", swap))
+            over[-1].append(order[-1])
+    beyond = [[lax.ppermute(x, "virt", relay) for x in group] for group in over]
 
     live = lax.broadcasted_iota(jnp.int32, cd_tiles.shape, 1) < tile_counts[:, None]
     block = cd_tiles // tiles - me
@@ -237,18 +235,14 @@
     got = lax.all_to_all(sent, ("pair", "virt"), split_axis=0, concat_axis=0, tiled=True)
     own_occ = lax.dynamic_slice_in_dim(eps_occ, lax.axis_index("pair") * rows, rows)
     own_virt = lax.dynamic_slice_in_dim(eps_virt, me * tiles, tiles)
-    owns, factors, begin = [], [], 0
-    for devices, ladder in zip(CHUNKS, ladders):
-        denominator = (
-            own_occ[:, None, None, None]
-            + eps_occ[None, begin * rows : (begin + devices) * rows, None, None]
-            - own_virt[None, None, :, None]
-            - eps_virt[None, None, None, :]
-        )
-        owns.append(ladder.reshape(rows, rows * devices, tiles, LANES) / denominator)
-        factors.append(1.0 / denominator)
-        begin += devices
-    return finish(got.reshape(-1, LANES).astype(jnp.float32), owns, factors)
+    denominator = (
+        own_occ[:, None, None, None]
+        + eps_occ[None, :, None, None]
+        - own_virt[None, None, :, None]
+        - eps_virt[None, None, None, :]
+    )
+    ladder = jnp.concatenate([x.reshape(rows, -1, tiles, LANES) for x in ladders], axis=1)
+    return finish(got.reshape(-1, LANES).astype(jnp.float32), ladder / denominator, 1.0 / denominator)
 
 
 def solution(mesh):

time: 145 us -> 153 us (1.055)
  starting transfers between devices: 53.5 us -> 71 us
  local copies, waits for them, and re-layouts: 16.2 us -> 3.75 us
  waiting for transfers between devices: 39.4 us -> 41.9 us
  other arithmetic: 4.61 us -> 6.29 us
    all_to_all x1, starting transfers between devices: 26 us -> 38.4 us  [per_device(): lax.all_to_all(sent, ('pair', 'virt'), split_axis=0, concat_axis=0, tiled...]
    unnamed x56 -> x16, local copies, waits for them, and re-layouts: 9.85 us -> 0.45 us
    ppermute x8, starting transfers between devices: 27.5 us -> 32.5 us  [the longest x4 19.4 us: per_device(): order.append(lax.ppermute(piece, 'virt', swap))]
    transpose x5, local copies, waits for them, and re-layouts: 5.95 us -> 1.67 us  [per_device(): jnp.transpose(part, (2, 0, 1, 3))]
    ppermute x8, waiting for transfers between devices: 7 us -> 9.69 us  [the longest x4 9.68 us: per_device(): order.append(lax.ppermute(piece, 'virt', swap))]
    pallas_call x5 -> x4, Pallas kernels: 25.3 us -> 23.9 us  [the longest x3 20 us: ladder_rows(): pl.pallas_call(functools.partial(ladder_kernel, len(over)), out_shape=jax...]
    pallas_call x4 -> x3, Pallas kernels: 5.15 us -> 5.22 us  [pack(): pl.pallas_call(pack_kernel, out_shape=jax.ShapeDtypeStruct((rows // VALUE...]
  transfers between devices with their start and end apart: 9 -> 9, of which waited for: 2 -> 4; matrix products, arithmetic and copies ran while one was open for 5% -> 3% of each run, Pallas kernels for 13% -> 12%
where the time goes in v3:
time: 153 us; the launch traced here: 152 us
  starting transfers between devices  71 us (46%)
  waiting for transfers between devices  41.9 us (27%)
  Pallas kernels  29.2 us (19%)
  other arithmetic  6.29 us (4%)
  local copies, waits for them, and re-layouts  3.75 us (2%)
    all_to_all x1, starting transfers between devices, per_device(): lax.all_to_all(sent, ('pair', 'virt'), split_axis=0, concat_axis=0, tiled...  38.4 us
    all_to_all x1, waiting for transfers between devices, per_device(): lax.all_to_all(sent, ('pair', 'virt'), split_axis=0, concat_axis=0, tiled...  32.2 us
    pallas_call x3, Pallas kernels, ladder_rows(): pl.pallas_call(functools.partial(ladder_kernel, len(over)), out_shape=jax...  20 us
    ppermute x4, starting transfers between devices, per_device(): order.append(lax.ppermute(piece, 'virt', swap))  19.4 us
    ppermute x4, starting transfers between devices, per_device(): beyond = [[lax.ppermute(x, 'virt', relay) for x in group] for group in over]  13.1 us
    ppermute x4, waiting for transfers between devices, per_device(): order.append(lax.ppermute(piece, 'virt', swap))  9.68 us
    pallas_call x3, Pallas kernels, pack(): pl.pallas_call(pack_kernel, out_shape=jax.ShapeDtypeStruct((rows // VALUE...  5.22 us
    pallas_call x1, Pallas kernels, finish(): pl.pallas_call(finish_kernel, out_shape=jax.ShapeDtypeStruct(own.shape, j...  3.94 us
  transfers between devices with their start and end apart: 9, of which 4 were waited for; matrix products, arithmetic and copies ran while one was open for 3% of the time, Pallas kernels for 12%

profile of v3, /device:TPU:1, one launch (start us, length us, event | category | flops | bytes accessed | tf_op | source)
XLA Modules:
  0.0 152.4 jit_solution(2865514432747316530)
XLA Ops:
  0.0 1.3 slice_bitcast_fusion
  1.4 7.8 %collective-permute-start = (bf16[8,144,128]{2,1,0:T(8,128)(2,1)S(1)}, bf16[8,144,128]{2,1,0:T(8,128)(2,1)S(1)}, u32[]{:S(2)}, u32[]{:S(2)}) collective-permute-start(bf16[8,144,128]{2,1,0:T(8,128)(2,1)S(1)} %bitcast.30), channel_id=1, source_target_pairs={{0,1},{1,0},{2,3},{3,2},{4,5},{5,4},{6,7},{7,6},{8,9},{9,8},{10,11... | collective-permute-start | bytes 884744 | tf_op jit(solution)/shard_map/ppermute | solution.py:217
  9.7 6.7 %collective-permute-done.refs_1_.first_ref = bf16[8,144,128]{2,1,0:T(8,128)(2,1)S(1)} collective-permute-done((bf16[8,144,128]{2,1,0:T(8,128)(2,1)S(1)}, bf16[8,144,128]{2,1,0:T(8,128)(2,1)S(1)}, u32[]{:S(2)}, u32[]{:S(2)}) %collective-permute-start) | collective-permute-done | bytes 294944 | tf_op jit(solution)/shard_map/ppermute | solution.py:217
  16.5 5.7 %collective-permute-start.4 = (bf16[16,72,128]{2,1,0:T(8,128)(2,1)S(1)}, bf16[16,72,128]{2,1,0:T(8,128)(2,1)S(1)}, u32[]{:S(2)}, u32[]{:S(2)}) collective-permute-start(bf16[16,72,128]{2,1,0:T(8,128)(2,1)S(1)} %after.2), channel_id=1, source_target_pairs={{0,1},{1,0},{2,3},{3,2},{4,5},{5,4},{6,7},{7,6},{8,9},{9,8},{10,11... | collective-permute-start | bytes 884744 | tf_op jit(solution)/shard_map/ppermute | solution.py:217
  22.2 1.7 %collective-permute-done.1.refs_2_.first_ref = bf16[8,144,128]{2,1,0:T(8,128)(2,1)S(1)} collective-permute-done((bf16[8,144,128]{2,1,0:T(8,128)(2,1)S(1)}, bf16[8,144,128]{2,1,0:T(8,128)(2,1)S(1)}, u32[]{:S(2)}, u32[]{:S(2)}) %collective-permute-start.1) | collective-permute-done | bytes 294944 | tf_op jit(solution)/shard_map/ppermute | solution.py:217
  23.9 5.8 %collective-permute-start.6 = (bf16[16,72,128]{2,1,0:T(8,128)(2,1)S(1)}, bf16[16,72,128]{2,1,0:T(8,128)(2,1)S(1)}, u32[]{:S(2)}, u32[]{:S(2)}) collective-permute-start(bf16[16,72,128]{2,1,0:T(8,128)(2,1)S(1)} %after.3), channel_id=1, source_target_pairs={{0,1},{1,0},{2,3},{3,2},{4,5},{5,4},{6,7},{7,6},{8,9},{9,8},{10,11... | collective-permute-start | bytes 884744 | tf_op jit(solution)/shard_map/ppermute | solution.py:217
  29.7 3.2 %collective-permute-start.2 = (bf16[8,144,128]{2,1,0:T(8,128)(2,1)S(1)}, bf16[8,144,128]{2,1,0:T(8,128)(2,1)S(1)}, u32[]{:S(2)}, u32[]{:S(2)}) collective-permute-start(bf16[8,144,128]{2,1,0:T(8,128)(2,1)S(1)} %collective-permute-done.refs_1_.first_ref), channel_id=1, source_target_pairs={{0,2},{2,4},{4,6},{3,1},{5,3},{7,5},{8,10},{10,12},{12,14},{11,9},... | collective-permute-start | bytes 884744 | tf_op jit(solution)/shard_map/ppermute | solution.py:219
  32.9 3.2 %collective-permute-start.3 = (bf16[8,144,128]{2,1,0:T(8,128)(2,1)S(1)}, bf16[8,144,128]{2,1,0:T(8,128)(2,1)S(1)}, u32[]{:S(2)}, u32[]{:S(2)}) collective-permute-start(bf16[8,144,128]{2,1,0:T(8,128)(2,1)S(1)} %collective-permute-done.1.refs_2_.first_ref), channel_id=1, source_target_pairs={{0,2},{2,4},{4,6},{3,1},{5,3},{7,5},{8,10},{10,12},{12,14},{11,9},... | collective-permute-start | bytes 884744 | tf_op jit(solution)/shard_map/ppermute | solution.py:219
  36.1 2.9 %collective-permute-start.5 = (bf16[16,72,128]{2,1,0:T(8,128)(2,1)S(1)}, bf16[16,72,128]{2,1,0:T(8,128)(2,1)S(1)}, u32[]{:S(2)}, u32[]{:S(2)}) collective-permute-start(bf16[16,72,128]{2,1,0:T(8,128)(2,1)S(1)} %collective-permute-done.4.refs_1_), channel_id=1, source_target_pairs={{0,2},{2,4},{4,6},{3,1},{5,3},{7,5},{8,10},{10,12},{12,14},{11,9},... | collective-permute-start | bytes 884744 | tf_op jit(solution)/shard_map/ppermute | solution.py:219
  39.1 1.2 collective-permute-done.6.refs_1_
  40.3 3.8 %collective-permute-start.7 = (bf16[16,72,128]{2,1,0:T(8,128)(2,1)S(1)}, bf16[16,72,128]{2,1,0:T(8,128)(2,1)S(1)}, u32[]{:S(2)}, u32[]{:S(2)}) collective-permute-start(bf16[16,72,128]{2,1,0:T(8,128)(2,1)S(1)} %collective-permute-done.6.refs_1_), channel_id=1, source_target_pairs={{0,2},{2,4},{4,6},{3,1},{5,3},{7,5},{8,10},{10,12},{12,14},{11,9},... | collective-permute-start | bytes 884744 | tf_op jit(solution)/shard_map/ppermute | solution.py:219
  44.3 7.1 %ladder_rows.3.ladder_ref = f32[2304,128]{1,0:T(8,128)S(1)} custom-call(s32[16,20]{1,0:T(8,128)S(1)} %fusion.2.index_ref, bf16[16,144,128]{2,1,0:T(8,128)(2,1)S(1)} %bitcast.25, bf16[8,144,128]{2,1,0:T(8,128)(2,1)S(1)} %collective-permute-done.refs_1_.first_ref, bf16[8,144,128]{2,1,0:T(8,128)(2,1)S(1)} %collective-permute-done.1.refs_2_.first_ref, ...), custom_call_target="tpu_custom_call" | custom-call | flops 1509949440 | bytes 10485760 | tf_op jit(solution)/shard_map/ladder_rows/pallas_call | solution.py:73
  51.5 2.6 %pack.3 = f32[2560,128]{1,0:T(8,128)S(1)} custom-call(f32[2304,128]{1,0:T(8,128)S(1)} %ladder_rows.3.ladder_ref), custom_call_target="tpu_custom_call" | custom-call | flops 9437184 | bytes 2359296 | tf_op jit(solution)/shard_map/pack/pallas_call | solution.py:128
  54.2 1.3 dynamic_update_slice.9
  55.5 6.4 %ladder_rows.4.ladder_ref = f32[1152,128]{1,0:T(8,128)S(1)} custom-call(s32[16,20]{1,0:T(8,128)S(1)} %fusion.2.index_ref, bf16[16,72,128]{2,1,0:T(8,128)(2,1)S(1)} %bitcast.24, bf16[16,72,128]{2,1,0:T(8,128)(2,1)S(1)} %collective-permute-done.4.refs_1_, bf16[16,72,128]{2,1,0:T(8,128)(2,1)S(1)} %collective-permute-done.5.refs_2_, bf16[16,2560,128]{2,1,0:T(8,128)(2,1)} %bitcast.27), custom_call_target="tpu_custom_call" | custom-call | flops 754974720 | bytes 10485760 | tf_op jit(solution)/shard_map/ladder_rows/pallas_call | solution.py:73
  62.0 1.3 pack.4
  63.3 6.4 %ladder_rows.5.ladder_ref = f32[1152,128]{1,0:T(8,128)S(1)} custom-call(s32[16,20]{1,0:T(8,128)S(1)} %fusion.2.index_ref, bf16[16,72,128]{2,1,0:T(8,128)(2,1)S(1)} %bitcast.22, bf16[16,72,128]{2,1,0:T(8,128)(2,1)S(1)} %collective-permute-done.6.refs_1_, bf16[16,72,128]{2,1,0:T(8,128)(2,1)S(1)} %collective-permute-done.7.refs_2_, bf16[16,2560,128]{2,1,0:T(8,128)(2,1)} %bitcast.28), custom_call_target="tpu_custom_call" | custom-call | flops 754974720 | bytes 10485760 | tf_op jit(solution)/shard_map/ladder_rows/pallas_call | solution.py:73
  69.8 1.3 pack.5
  71.8 0.8 convert_dynamic-update-slice_fusion
  72.6 38.4 %all-to-all-start = ((f16[256,10,2,128]{3,2,1,0:T(2,128)(2,1)}), f16[256,10,2,128]{3,2,1,0:T(2,128)(2,1)}, u32[]{:S(2)}, u32[]{:S(2)}) async-start(f16[256,10,2,128]{3,2,1,0:T(2,128)(2,1)} %bitcast.9), calls=%async_computation | async-start | bytes 2621440 | tf_op jit(solution)/shard_map/all_to_all | solution.py:235
  111.4 2.8 %subtract_divide_fusion = (f32[3,96,16,128]{3,2,1,0:T(8,128)S(1)}, f32[3,96,16,128]{3,2,1,0:T(8,128)}) fusion(f32[128]{0:T(128)S(1)} %copy-done.5, f32[3,96,16]{2,1,0:T(8,128)S(1)} %broadcast_subtract_fusion, f32[3,24,16,128]{3,2,1,0:T(8,128)} %bitcast.20, f32[3,24,16,128]{3,2,1,0:T(8,128)} %bitcast.19, f32[3,48,16,128]{3,2,1,0:T(8,128)S(1)} %bitcast.18), kind=kLoop, calls=%fused_computation | loop fusion | flops 2949120 | bytes 7096832 | tf_op jit(solution)/shard_map/div | solution.py:245
  114.2 32.2 %all-to-all-done = f16[256,10,2,128]{3,2,1,0:T(2,128)(2,1)} async-done(((f16[256,10,2,128]{3,2,1,0:T(2,128)(2,1)}), f16[256,10,2,128]{3,2,1,0:T(2,128)(2,1)}, u32[]{:S(2)}, u32[]{:S(2)}) %all-to-all-start) | async-done | bytes 1310752 | tf_op jit(solution)/shard_map/all_to_all | solution.py:235
  146.4 1.6 %convert.1.got_ref = f32[5120,128]{1,0:T(8,128)S(1)} convert(f16[5120,128]{1,0:T(8,128)(2,1)} %bitcast.14) | non-fusion elementwise | flops 655360 | bytes 3932160 | tf_op jit(solution)/shard_map/convert_element_type | solution.py:245
  148.4 3.9 %finish.1 = bf16[3,96,16,128]{3,2,1,0:T(8,128)(2,1)} custom-call(f32[5120,128]{1,0:T(8,128)S(1)} %convert.1.got_ref, f32[3,96,16,128]{3,2,1,0:T(8,128)S(1)} %copy-done, f32[3,96,16,128]{3,2,1,0:T(8,128)S(1)} %get-tuple-element.9.factor_ref), custom_call_target="tpu_custom_call" | custom-call | flops 33554432 | bytes 8388608 | tf_op jit(solution)/shard_map/finish/pallas_call | solution.py:165
  (38 shorter events, 2.5 us)
Async XLA Ops:
  0.0 9.4 %copy-start.3 = (bf16[3,96,16,128]{3,2,1,0:T(8,128)(2,1)S(1)}, bf16[3,96,16,128]{3,2,1,0:T(8,128)(2,1)}, u32[]{:S(2)}) copy-start(bf16[3,96,16,128]{3,2,1,0:T(8,128)(2,1)} %param.6) | copy-start | bytes 3538948
  1.4 15.0 %collective-permute-start = (bf16[8,144,128]{2,1,0:T(8,128)(2,1)S(1)}, bf16[8,144,128]{2,1,0:T(8,128)(2,1)S(1)}, u32[]{:S(2)}, u32[]{:S(2)}) collective-permute-start(bf16[8,144,128]{2,1,0:T(8,128)(2,1)S(1)} %bitcast.30), channel_id=1, source_target_pairs={{0,1},{1,0},{2,3},{3,2},{4,5},{5,4},{6,7},{7,6},{8,9},{9,8},{10,11... | collective-permute-start | bytes 884744 | tf_op jit(solution)/shard_map/ppermute | solution.py:217
  9.3 34.8 %copy-start.4 = (s32[16,20]{1,0:T(8,128)S(1)}, s32[16,20]{1,0:T(8,128)}, u32[]{:S(2)}) copy-start(s32[16,20]{1,0:T(8,128)} %param.8) | copy-start | bytes 3844
  9.3 34.8 %copy-start.6 = (s32[16]{0:T(128)S(1)}, s32[16]{0:T(128)}, u32[]{:S(2)}) copy-start(s32[16]{0:T(128)} %param.9) | copy-start | bytes 196
  9.3 14.6 %collective-permute-start.1 = (bf16[8,144,128]{2,1,0:T(8,128)(2,1)S(1)}, bf16[8,144,128]{2,1,0:T(8,128)(2,1)S(1)}, u32[]{:S(2)}, u32[]{:S(2)}) collective-permute-start(bf16[8,144,128]{2,1,0:T(8,128)(2,1)S(1)} %bitcast.29), channel_id=1, source_target_pairs={{0,1},{1,0},{2,3},{3,2},{4,5},{5,4},{6,7},{7,6},{8,9},{9,8},{10,11... | collective-permute-start | bytes 884744 | tf_op jit(solution)/shard_map/ppermute | solution.py:217
  16.5 19.7 %collective-permute-start.4 = (bf16[16,72,128]{2,1,0:T(8,128)(2,1)S(1)}, bf16[16,72,128]{2,1,0:T(8,128)(2,1)S(1)}, u32[]{:S(2)}, u32[]{:S(2)}) collective-permute-start(bf16[16,72,128]{2,1,0:T(8,128)(2,1)S(1)} %after.2), channel_id=1, source_target_pairs={{0,1},{1,0},{2,3},{3,2},{4,5},{5,4},{6,7},{7,6},{8,9},{9,8},{10,11... | collective-permute-start | bytes 884744 | tf_op jit(solution)/shard_map/ppermute | solution.py:217
  23.9 16.4 %collective-permute-start.6 = (bf16[16,72,128]{2,1,0:T(8,128)(2,1)S(1)}, bf16[16,72,128]{2,1,0:T(8,128)(2,1)S(1)}, u32[]{:S(2)}, u32[]{:S(2)}) collective-permute-start(bf16[16,72,128]{2,1,0:T(8,128)(2,1)S(1)} %after.3), channel_id=1, source_target_pairs={{0,1},{1,0},{2,3},{3,2},{4,5},{5,4},{6,7},{7,6},{8,9},{9,8},{10,11... | collective-permute-start | bytes 884744 | tf_op jit(solution)/shard_map/ppermute | solution.py:217
  29.7 14.6 %collective-permute-start.2 = (bf16[8,144,128]{2,1,0:T(8,128)(2,1)S(1)}, bf16[8,144,128]{2,1,0:T(8,128)(2,1)S(1)}, u32[]{:S(2)}, u32[]{:S(2)}) collective-permute-start(bf16[8,144,128]{2,1,0:T(8,128)(2,1)S(1)} %collective-permute-done.refs_1_.first_ref), channel_id=1, source_target_pairs={{0,2},{2,4},{4,6},{3,1},{5,3},{7,5},{8,10},{10,12},{12,14},{11,9},... | collective-permute-start | bytes 884744 | tf_op jit(solution)/shard_map/ppermute | solution.py:219
  32.9 11.4 %collective-permute-start.3 = (bf16[8,144,128]{2,1,0:T(8,128)(2,1)S(1)}, bf16[8,144,128]{2,1,0:T(8,128)(2,1)S(1)}, u32[]{:S(2)}, u32[]{:S(2)}) collective-permute-start(bf16[8,144,128]{2,1,0:T(8,128)(2,1)S(1)} %collective-permute-done.1.refs_2_.first_ref), channel_id=1, source_target_pairs={{0,2},{2,4},{4,6},{3,1},{5,3},{7,5},{8,10},{10,12},{12,14},{11,9},... | collective-permute-start | bytes 884744 | tf_op jit(solution)/shard_map/ppermute | solution.py:219
  36.1 19.4 %collective-permute-start.5 = (bf16[16,72,128]{2,1,0:T(8,128)(2,1)S(1)}, bf16[16,72,128]{2,1,0:T(8,128)(2,1)S(1)}, u32[]{:S(2)}, u32[]{:S(2)}) collective-permute-start(bf16[16,72,128]{2,1,0:T(8,128)(2,1)S(1)} %collective-permute-done.4.refs_1_), channel_id=1, source_target_pairs={{0,2},{2,4},{4,6},{3,1},{5,3},{7,5},{8,10},{10,12},{12,14},{11,9},... | collective-permute-start | bytes 884744 | tf_op jit(solution)/shard_map/ppermute | solution.py:219
  40.3 23.0 %collective-permute-start.7 = (bf16[16,72,128]{2,1,0:T(8,128)(2,1)S(1)}, bf16[16,72,128]{2,1,0:T(8,128)(2,1)S(1)}, u32[]{:S(2)}, u32[]{:S(2)}) collective-permute-start(bf16[16,72,128]{2,1,0:T(8,128)(2,1)S(1)} %collective-permute-done.6.refs_1_), channel_id=1, source_target_pairs={{0,2},{2,4},{4,6},{3,1},{5,3},{7,5},{8,10},{10,12},{12,14},{11,9},... | collective-permute-start | bytes 884744 | tf_op jit(solution)/shard_map/ppermute | solution.py:219
  62.0 7.8 %copy-start.1 = (f32[1152,128]{1,0:T(8,128)}, f32[1152,128]{1,0:T(8,128)S(1)}, u32[]{:S(2)}) copy-start(f32[1152,128]{1,0:T(8,128)S(1)} %ladder_rows.4.ladder_ref) | copy-start | bytes 1769476
  69.7 2.9 %copy-start.2 = (f32[1152,128]{1,0:T(8,128)}, f32[1152,128]{1,0:T(8,128)S(1)}, u32[]{:S(2)}) copy-start(f32[1152,128]{1,0:T(8,128)S(1)} %ladder_rows.5.ladder_ref) | copy-start | bytes 1769476
  71.0 40.1 %copy-start.5 = (f32[128]{0:T(128)S(1)}, f32[128]{0:T(128)}, u32[]{:S(2)}) copy-start(f32[128]{0:T(128)} %param.11) | copy-start | bytes 1540
  71.1 40.1 %copy-start.7 = (f32[96]{0:T(128)S(1)}, f32[96]{0:T(128)}, u32[]{:S(2)}) copy-start(f32[96]{0:T(128)} %param.10) | copy-start | bytes 1156
  72.6 73.7 %all-to-all-start = ((f16[256,10,2,128]{3,2,1,0:T(2,128)(2,1)}), f16[256,10,2,128]{3,2,1,0:T(2,128)(2,1)}, u32[]{:S(2)}, u32[]{:S(2)}) async-start(f16[256,10,2,128]{3,2,1,0:T(2,128)(2,1)} %bitcast.9), calls=%async_computation | async-start | bytes 2621440 | tf_op jit(solution)/shard_map/all_to_all | solution.py:235
  146.4 2.1 %copy-start = (f32[3,96,16,128]{3,2,1,0:T(8,128)S(1)}, f32[3,96,16,128]{3,2,1,0:T(8,128)}, u32[]{:S(2)}) copy-start(f32[3,96,16,128]{3,2,1,0:T(8,128)} %get-tuple-element.10.own_ref) | copy-start | bytes 7077892

commit v4 on v3

--- a/solution.py
+++ b/solution.py
@@ -29,37 +29,32 @@
     return parts
 
 
-def ladder_kernel(pieces, index_ref, *refs):
-    own_ref, over_refs, next_refs = refs[0], refs[1 : 1 + pieces], refs[1 + pieces : 1 + 2 * pieces]
-    ladder_body(index_ref, own_ref, over_refs, next_refs, *refs[1 + 2 * pieces :])
-
-
-def ladder_body(index_ref, own_ref, over_refs, next_refs, weight_ref, out_ref, held, weights, arrived):
-    group = weights.shape[1]
+def ladder_kernel(pieces, index_ref, own_ref, *refs):
+    over_refs, next_refs = refs[:pieces], refs[pieces : 2 * pieces]
+    weight_ref, out_ref, held, weights, arrived = refs[2 * pieces :]
     slots = weight_ref.shape[1] // LANES
 
-    def fetch(step):
-        return pltpu.make_async_copy(
-            weight_ref.at[pl.ds(step * group, group)], weights.at[step % 2], arrived.at[step % 2]
-        )
-
-    fetch(0).start()
+    def fetch(a):
+        return pltpu.make_async_copy(weight_ref.at[a], weights.at[a], arrived.at[a])
+
+    for a in range(TILES):
+        fetch(a).start()
     held[0:TILES] = own_ref[...]
     for n, (over_ref, next_ref) in enumerate(zip(over_refs, next_refs)):
         count = over_ref.shape[0]
         held[TILES + n * count : TILES + (n + 1) * count] = over_ref[...]
         held[2 * TILES + n * count : 2 * TILES + (n + 1) * count] = next_ref[...]
     held[3 * TILES] = jnp.zeros_like(held[3 * TILES])
-    for step in range(TILES // group):
-        if step + 1 < TILES // group:
-            fetch(step + 1).start()
-        fetch(step).wait()
-        for n in range(group):
-            a = step * group + n
+
+    @pl.loop(0, TILES // 4)
+    def _(step):
+        for n in range(4):
+            a = step * 4 + n
+            fetch(a).wait()
             row = None
             for s in range(0, slots, 4):
                 four = jnp.concatenate([held[index_ref[a, s + t]] for t in range(4)], axis=1)
-                part = weights[step % 2, n, s * LANES : (s + 4) * LANES]
+                part = weights[a, s * LANES : (s + 4) * LANES]
                 term = jnp.dot(four, part, preferred_element_type=jnp.float32)
                 row = term if row is None else row + term
             out_ref[pl.ds(a, row.shape[0], stride=TILES), :] = row
@@ -68,7 +63,6 @@
 def ladder_rows(index, own, over, beyond, weights):
     tiles, pairs, depth = own.shape
     k = weights.shape[1]
-    group = 4
     smem, vmem = pl.BlockSpec(memory_space=pltpu.SMEM), pl.BlockSpec(memory_space=pltpu.VMEM)
     return pl.pallas_call(
         functools.partial(ladder_kernel, len(over)),
@@ -77,8 +71,8 @@
         out_specs=vmem,
         scratch_shapes=[
             pltpu.VMEM((3 * tiles + 1, pairs, depth), jnp.bfloat16),
-            pltpu.VMEM((2, group, k, LANES), jnp.bfloat16),
-            pltpu.SemaphoreType.DMA((2,)),
+            pltpu.VMEM(weights.shape, jnp.bfloat16),
+            pltpu.SemaphoreType.DMA((tiles,)),
         ],
         compiler_params=pltpu.CompilerParams(vmem_limit_bytes=48 * 2**20),
         cost_estimate=pl.CostEstimate(
@@ -175,24 +169,23 @@
     )(got, own, factor)
 
 
-def after_kernel(x_ref, first_ref, out_ref):
-    out_ref[...] = x_ref[...]
-
-
-def after(x, first):
+def after_kernel(x_ref, *refs):
+    refs[-1][...] = x_ref[...]
+
+
+def after(x, *first):
     vmem = pl.BlockSpec(memory_space=pltpu.VMEM)
     return pl.pallas_call(
         after_kernel,
         out_shape=jax.ShapeDtypeStruct(x.shape, x.dtype),
-        in_specs=[vmem, vmem],
+        in_specs=[vmem] * (1 + len(first)),
         out_specs=vmem,
-        compiler_params=pltpu.CompilerParams(vmem_limit_bytes=4 * 2**20),
+        compiler_params=pltpu.CompilerParams(vmem_limit_bytes=12 * 2**20),
         name="after",
-    )(x, first)
+    )(x, *first)
 
 
 CHUNKS = (16, 8, 8)
-PIECES = (2, 1, 1)
 
 
 def per_device(amplitudes, integrals, cd_tiles, tile_counts, eps_occ, eps_virt):
@@ -206,18 +199,6 @@
         part = amplitudes[:, begin * rows : (begin + devices) * rows]
         own.append(jnp.transpose(part, (2, 0, 1, 3)).reshape(tiles, rows * rows * devices, depth))
         begin += devices
-    over, beyond, order = [], [], []
-    for part, pieces in zip(own, PIECES):
-        count = tiles // pieces
-        over.append([])
-        for n in range(pieces):
-            piece = part[n * count : (n + 1) * count]
-            if len(order) >= 2:
-                piece = after(piece, order[-2])
-            order.append(lax.ppermute(piece, "virt", swap))
-            over[-1].append(order[-1])
-    beyond = [[lax.ppermute(x, "virt", relay) for x in group] for group in over]
-
     live = lax.broadcasted_iota(jnp.int32, cd_tiles.shape, 1) < tile_counts[:, None]
     block = cd_tiles // tiles - me
     over_block = jnp.where(me % 2 == 0, 1, -1)
@@ -225,7 +206,26 @@
     index = jnp.where(live, place * tiles + cd_tiles % tiles, 3 * tiles).astype(jnp.int32)
 
     weights = integrals.reshape(tiles, slots * depth, LANES)
-    ladders = [ladder_rows(index, *parts, weights) for parts in zip(own, over, beyond)]
+
+    def swapped(x):
+        return lax.ppermute(x, "virt", swap)
+
+    def passed_on(x):
+        return lax.ppermute(x, "virt", relay)
+
+    half = tiles // 2
+    over_a = [swapped(own[0][:half]), swapped(own[0][half:])]
+    own[1] = after(own[1], over_a[0])
+    over_b = swapped(own[1])
+    beyond_a = [passed_on(x) for x in over_a]
+    own[2] = after(own[2], over_a[1], beyond_a[0])
+    over_c = swapped(own[2])
+    beyond_b = passed_on(over_b)
+    ladder_a = ladder_rows(index, own[0], over_a, beyond_a, weights)
+    beyond_c = passed_on(after(over_c, ladder_a))
+    ladder_b = ladder_rows(index, own[1], [over_b], [beyond_b], weights)
+    ladder_c = ladder_rows(index, own[2], [over_c], [beyond_c], weights)
+    ladders = [ladder_a, ladder_b, ladder_c]
     sent = jnp.zeros((partners // rows * VIRT * MSG, LANES), jnp.float16)
     begin = 0
     for devices, ladder in zip(CHUNKS, ladders):

time: 153 us -> 145 us (0.948)
  starting transfers between devices: 71 us -> 63 us
    ppermute x8, starting transfers between devices: 32.5 us -> 27.2 us  [the longest x4 14.5 us: swapped(): return lax.ppermute(x, 'virt', swap)]
    all_to_all x1, starting transfers between devices: 38.4 us -> 35.8 us  [per_device(): lax.all_to_all(sent, ('pair', 'virt'), split_axis=0, concat_axis=0, tiled...]
  transfers between devices with their start and end apart: 9 -> 9, of which waited for: 4 -> 4; matrix products, arithmetic and copies ran while one was open for 3% -> 4% of each run, Pallas kernels for 12% -> 12%
where the time goes in v4:
time: 145 us; the launch traced here: 144 us
  starting transfers between devices  63 us (43%)
  waiting for transfers between devices  40.6 us (28%)
  Pallas kernels  29.6 us (20%)
  other arithmetic  6.28 us (4%)
  local copies, waits for them, and re-layouts  4.46 us (3%)
    all_to_all x1, starting transfers between devices, per_device(): lax.all_to_all(sent, ('pair', 'virt'), split_axis=0, concat_axis=0, tiled...  35.8 us
    all_to_all x1, waiting for transfers between devices, per_device(): lax.all_to_all(sent, ('pair', 'virt'), split_axis=0, concat_axis=0, tiled...  32.2 us
    pallas_call x3, Pallas kernels, ladder_rows(): pl.pallas_call(functools.partial(ladder_kernel, len(over)), out_shape=jax...  20.4 us
    ppermute x4, starting transfers between devices, swapped(): return lax.ppermute(x, 'virt', swap)  14.5 us
    ppermute x4, starting transfers between devices, passed_on(): return lax.ppermute(x, 'virt', relay)  12.8 us
    ppermute x4, waiting for transfers between devices, swapped(): return lax.ppermute(x, 'virt', swap)  8.45 us
    pallas_call x3, Pallas kernels, pack(): pl.pallas_call(pack_kernel, out_shape=jax.ShapeDtypeStruct((rows // VALUE...  5.22 us
    pallas_call x1, Pallas kernels, finish(): pl.pallas_call(finish_kernel, out_shape=jax.ShapeDtypeStruct(own.shape, j...  3.94 us
  transfers between devices with their start and end apart: 9, of which 4 were waited for; matrix products, arithmetic and copies ran while one was open for 4% of the time, Pallas kernels for 12%

profile of v4, /device:TPU:1, one launch (start us, length us, event | category | flops | bytes accessed | tf_op | source)
XLA Modules:
  0.0 144.3 jit_solution(16082599991010745740)
XLA Ops:
  0.0 1.3 slice_bitcast_fusion
  1.4 7.8 %collective-permute-start = (bf16[8,144,128]{2,1,0:T(8,128)(2,1)S(1)}, bf16[8,144,128]{2,1,0:T(8,128)(2,1)S(1)}, u32[]{:S(2)}, u32[]{:S(2)}) collective-permute-start(bf16[8,144,128]{2,1,0:T(8,128)(2,1)S(1)} %bitcast.28), channel_id=1, source_target_pairs={{0,1},{1,0},{2,3},{3,2},{4,5},{5,4},{6,7},{7,6},{8,9},{9,8},{10,11... | collective-permute-start | bytes 884744 | tf_op jit(solution)/shard_map/ppermute | solution.py:211
  9.4 0.8 slice_bitcast_fusion.1
  10.2 6.2 %collective-permute-done.refs_0_ = bf16[8,144,128]{2,1,0:T(8,128)(2,1)S(1)} collective-permute-done((bf16[8,144,128]{2,1,0:T(8,128)(2,1)S(1)}, bf16[8,144,128]{2,1,0:T(8,128)(2,1)S(1)}, u32[]{:S(2)}, u32[]{:S(2)}) %collective-permute-start) | collective-permute-done | bytes 294944 | tf_op jit(solution)/shard_map/ppermute | solution.py:211
  16.4 3.8 %collective-permute-start.2 = (bf16[8,144,128]{2,1,0:T(8,128)(2,1)S(1)}, bf16[8,144,128]{2,1,0:T(8,128)(2,1)S(1)}, u32[]{:S(2)}, u32[]{:S(2)}) collective-permute-start(bf16[8,144,128]{2,1,0:T(8,128)(2,1)S(1)} %collective-permute-done.refs_0_), channel_id=1, source_target_pairs={{0,2},{2,4},{4,6},{3,1},{5,3},{7,5},{8,10},{10,12},{12,14},{11,9},... | collective-permute-start | bytes 884744 | tf_op jit(solution)/shard_map/ppermute | solution.py:214
  20.3 3.3 %collective-permute-start.4 = (bf16[16,72,128]{2,1,0:T(8,128)(2,1)S(1)}, bf16[16,72,128]{2,1,0:T(8,128)(2,1)S(1)}, u32[]{:S(2)}, u32[]{:S(2)}) collective-permute-start(bf16[16,72,128]{2,1,0:T(8,128)(2,1)S(1)} %after.3.own_ref), channel_id=1, source_target_pairs={{0,1},{1,0},{2,3},{3,2},{4,5},{5,4},{6,7},{7,6},{8,9},{9,8},{10,11... | collective-permute-start | bytes 884744 | tf_op jit(solution)/shard_map/ppermute | solution.py:211
  23.9 3.8 %collective-permute-start.3 = (bf16[8,144,128]{2,1,0:T(8,128)(2,1)S(1)}, bf16[8,144,128]{2,1,0:T(8,128)(2,1)S(1)}, u32[]{:S(2)}, u32[]{:S(2)}) collective-permute-start(bf16[8,144,128]{2,1,0:T(8,128)(2,1)S(1)} %collective-permute-done.1.refs_1_.refs_0_), channel_id=1, source_target_pairs={{0,2},{2,4},{4,6},{3,1},{5,3},{7,5},{8,10},{10,12},{12,14},{11,9},... | collective-permute-start | bytes 884744 | tf_op jit(solution)/shard_map/ppermute | solution.py:214
  28.0 3.3 %collective-permute-start.6 = (bf16[16,72,128]{2,1,0:T(8,128)(2,1)S(1)}, bf16[16,72,128]{2,1,0:T(8,128)(2,1)S(1)}, u32[]{:S(2)}, u32[]{:S(2)}) collective-permute-start(bf16[16,72,128]{2,1,0:T(8,128)(2,1)S(1)} %after.4.own_ref), channel_id=1, source_target_pairs={{0,1},{1,0},{2,3},{3,2},{4,5},{5,4},{6,7},{7,6},{8,9},{9,8},{10,11... | collective-permute-start | bytes 884744 | tf_op jit(solution)/shard_map/ppermute | solution.py:211
  31.3 1.9 %collective-permute-done.4.refs_0_ = bf16[16,72,128]{2,1,0:T(8,128)(2,1)S(1)} collective-permute-done((bf16[16,72,128]{2,1,0:T(8,128)(2,1)S(1)}, bf16[16,72,128]{2,1,0:T(8,128)(2,1)S(1)}, u32[]{:S(2)}, u32[]{:S(2)}) %collective-permute-start.4) | collective-permute-done | bytes 294944 | tf_op jit(solution)/shard_map/ppermute | solution.py:211
  33.2 2.1 %collective-permute-start.5 = (bf16[16,72,128]{2,1,0:T(8,128)(2,1)S(1)}, bf16[16,72,128]{2,1,0:T(8,128)(2,1)S(1)}, u32[]{:S(2)}, u32[]{:S(2)}) collective-permute-start(bf16[16,72,128]{2,1,0:T(8,128)(2,1)S(1)} %collective-permute-done.4.refs_0_), channel_id=1, source_target_pairs={{0,2},{2,4},{4,6},{3,1},{5,3},{7,5},{8,10},{10,12},{12,14},{11,9},... | collective-permute-start | bytes 884744 | tf_op jit(solution)/shard_map/ppermute | solution.py:214
  35.4 7.7 %ladder_rows.3.ladder_ref.refs_0_ = f32[2304,128]{1,0:T(8,128)S(1)} custom-call(s32[16,20]{1,0:T(8,128)S(1)} %fusion.2.index_ref, bf16[16,144,128]{2,1,0:T(8,128)(2,1)S(1)} %bitcast.21, bf16[8,144,128]{2,1,0:T(8,128)(2,1)S(1)} %collective-permute-done.refs_0_, bf16[8,144,128]{2,1,0:T(8,128)(2,1)S(1)} %collective-permute-done.1.refs_1_.refs_0_, ...), custom_call_target="tpu_custom_call" | custom-call | flops 1509949440 | bytes 10485760 | tf_op jit(solution)/shard_map/ladder_rows/pallas_call | solution.py:67
  43.1 2.6 %pack.3 = f32[2560,128]{1,0:T(8,128)S(1)} custom-call(f32[2304,128]{1,0:T(8,128)S(1)} %ladder_rows.3.ladder_ref.refs_0_), custom_call_target="tpu_custom_call" | custom-call | flops 9437184 | bytes 2359296 | tf_op jit(solution)/shard_map/pack/pallas_call | solution.py:122
  45.9 1.3 dynamic_update_slice.9
  47.2 3.1 %collective-permute-start.7 = (bf16[16,72,128]{2,1,0:T(8,128)(2,1)S(1)}, bf16[16,72,128]{2,1,0:T(8,128)(2,1)S(1)}, u32[]{:S(2)}, u32[]{:S(2)}) collective-permute-start(bf16[16,72,128]{2,1,0:T(8,128)(2,1)S(1)} %after.5), channel_id=1, source_target_pairs={{0,2},{2,4},{4,6},{3,1},{5,3},{7,5},{8,10},{10,12},{12,14},{11,9},... | collective-permute-start | bytes 884744 | tf_op jit(solution)/shard_map/ppermute | solution.py:214
  50.3 6.4 %ladder_rows.4.ladder_ref = f32[1152,128]{1,0:T(8,128)S(1)} custom-call(s32[16,20]{1,0:T(8,128)S(1)} %fusion.2.index_ref, bf16[16,72,128]{2,1,0:T(8,128)(2,1)S(1)} %after.3.own_ref, bf16[16,72,128]{2,1,0:T(8,128)(2,1)S(1)} %collective-permute-done.4.refs_0_, bf16[16,72,128]{2,1,0:T(8,128)(2,1)S(1)} %collective-permute-done.5.refs_1_, ...), custom_call_target="tpu_custom_call" | custom-call | flops 754974720 | bytes 10485760 | tf_op jit(solution)/shard_map/ladder_rows/pallas_call | solution.py:67
  56.7 1.3 pack.4
  58.8 6.3 %ladder_rows.5.ladder_ref = f32[1152,128]{1,0:T(8,128)S(1)} custom-call(s32[16,20]{1,0:T(8,128)S(1)} %fusion.2.index_ref, bf16[16,72,128]{2,1,0:T(8,128)(2,1)S(1)} %after.4.own_ref, bf16[16,72,128]{2,1,0:T(8,128)(2,1)S(1)} %collective-permute-done.6.x_ref.refs_0_, bf16[16,72,128]{2,1,0:T(8,128)(2,1)S(1)} %collective-permute-done.7.refs_1_, ...), custom_call_target="tpu_custom_call" | custom-call | flops 754974720 | bytes 10485760 | tf_op jit(solution)/shard_map/ladder_rows/pallas_call | solution.py:67
  65.2 1.3 pack.5
  66.5 0.8 convert_dynamic-update-slice_fusion
  67.2 35.8 %all-to-all-start = ((f16[256,10,2,128]{3,2,1,0:T(2,128)(2,1)}), f16[256,10,2,128]{3,2,1,0:T(2,128)(2,1)}, u32[]{:S(2)}, u32[]{:S(2)}) async-start(f16[256,10,2,128]{3,2,1,0:T(2,128)(2,1)} %bitcast.9), calls=%async_computation | async-start | bytes 2621440 | tf_op jit(solution)/shard_map/all_to_all | solution.py:235
  103.4 2.7 %subtract_divide_fusion = (f32[3,96,16,128]{3,2,1,0:T(8,128)S(1)}, f32[3,96,16,128]{3,2,1,0:T(8,128)}) fusion(f32[128]{0:T(128)S(1)} %copy-done.6, f32[3,96,16]{2,1,0:T(8,128)S(1)} %broadcast_subtract_fusion, f32[3,24,16,128]{3,2,1,0:T(8,128)} %bitcast.20, f32[3,24,16,128]{3,2,1,0:T(8,128)} %bitcast.19, f32[3,48,16,128]{3,2,1,0:T(8,128)S(1)} %bitcast.18), kind=kLoop, calls=%fused_computation | loop fusion | flops 2949120 | bytes 7096832 | tf_op jit(solution)/shard_map/div | solution.py:245
  106.1 32.2 %all-to-all-done = f16[256,10,2,128]{3,2,1,0:T(2,128)(2,1)} async-done(((f16[256,10,2,128]{3,2,1,0:T(2,128)(2,1)}), f16[256,10,2,128]{3,2,1,0:T(2,128)(2,1)}, u32[]{:S(2)}, u32[]{:S(2)}) %all-to-all-start) | async-done | bytes 1310752 | tf_op jit(solution)/shard_map/all_to_all | solution.py:235
  138.3 1.6 %convert.1.got_ref = f32[5120,128]{1,0:T(8,128)S(1)} convert(f16[5120,128]{1,0:T(8,128)(2,1)} %bitcast.14) | non-fusion elementwise | flops 655360 | bytes 3932160 | tf_op jit(solution)/shard_map/convert_element_type | solution.py:245
  140.3 3.9 %finish.1 = bf16[3,96,16,128]{3,2,1,0:T(8,128)(2,1)} custom-call(f32[5120,128]{1,0:T(8,128)S(1)} %convert.1.got_ref, f32[3,96,16,128]{3,2,1,0:T(8,128)S(1)} %copy-done, f32[3,96,16,128]{3,2,1,0:T(8,128)S(1)} %get-tuple-element.9.factor_ref), custom_call_target="tpu_custom_call" | custom-call | flops 33554432 | bytes 8388608 | tf_op jit(solution)/shard_map/finish/pallas_call | solution.py:159
  (41 shorter events, 2.7 us)
Async XLA Ops:
  0.0 9.4 %copy-start.3 = (bf16[3,96,16,128]{3,2,1,0:T(8,128)(2,1)S(1)}, bf16[3,96,16,128]{3,2,1,0:T(8,128)(2,1)}, u32[]{:S(2)}) copy-start(bf16[3,96,16,128]{3,2,1,0:T(8,128)(2,1)} %param.6) | copy-start | bytes 3538948
  1.4 15.0 %collective-permute-start = (bf16[8,144,128]{2,1,0:T(8,128)(2,1)S(1)}, bf16[8,144,128]{2,1,0:T(8,128)(2,1)S(1)}, u32[]{:S(2)}, u32[]{:S(2)}) collective-permute-start(bf16[8,144,128]{2,1,0:T(8,128)(2,1)S(1)} %bitcast.28), channel_id=1, source_target_pairs={{0,1},{1,0},{2,3},{3,2},{4,5},{5,4},{6,7},{7,6},{8,9},{9,8},{10,11... | collective-permute-start | bytes 884744 | tf_op jit(solution)/shard_map/ppermute | solution.py:211
  9.3 14.6 %collective-permute-start.1 = (bf16[8,144,128]{2,1,0:T(8,128)(2,1)S(1)}, bf16[8,144,128]{2,1,0:T(8,128)(2,1)S(1)}, u32[]{:S(2)}, u32[]{:S(2)}) collective-permute-start(bf16[8,144,128]{2,1,0:T(8,128)(2,1)S(1)} %bitcast.27), channel_id=1, source_target_pairs={{0,1},{1,0},{2,3},{3,2},{4,5},{5,4},{6,7},{7,6},{8,9},{9,8},{10,11... | collective-permute-start | bytes 884744 | tf_op jit(solution)/shard_map/ppermute | solution.py:211
  10.2 17.6 %copy-start.4 = (bf16[16,3,24,128]{3,0,2,1:T(8,128)(2,1)S(1)}, bf16[16,3,24,128]{3,0,2,1:T(8,128)(2,1)}, u32[]{:S(2)}) copy-start(bf16[16,3,24,128]{3,0,2,1:T(8,128)(2,1)} %get-tuple-element.5) | copy-start | bytes 884740
  10.2 25.1 %copy-start.5 = (s32[16,20]{1,0:T(8,128)S(1)}, s32[16,20]{1,0:T(8,128)}, u32[]{:S(2)}) copy-start(s32[16,20]{1,0:T(8,128)} %param.8) | copy-start | bytes 3844
  10.2 25.1 %copy-start.7 = (s32[16]{0:T(128)S(1)}, s32[16]{0:T(128)}, u32[]{:S(2)}) copy-start(s32[16]{0:T(128)} %param.9) | copy-start | bytes 196
  16.4 11.5 %collective-permute-start.2 = (bf16[8,144,128]{2,1,0:T(8,128)(2,1)S(1)}, bf16[8,144,128]{2,1,0:T(8,128)(2,1)S(1)}, u32[]{:S(2)}, u32[]{:S(2)}) collective-permute-start(bf16[8,144,128]{2,1,0:T(8,128)(2,1)S(1)} %collective-permute-done.refs_0_), channel_id=1, source_target_pairs={{0,2},{2,4},{4,6},{3,1},{5,3},{7,5},{8,10},{10,12},{12,14},{11,9},... | collective-permute-start | bytes 884744 | tf_op jit(solution)/shard_map/ppermute | solution.py:214
  20.3 12.9 %collective-permute-start.4 = (bf16[16,72,128]{2,1,0:T(8,128)(2,1)S(1)}, bf16[16,72,128]{2,1,0:T(8,128)(2,1)S(1)}, u32[]{:S(2)}, u32[]{:S(2)}) collective-permute-start(bf16[16,72,128]{2,1,0:T(8,128)(2,1)S(1)} %after.3.own_ref), channel_id=1, source_target_pairs={{0,1},{1,0},{2,3},{3,2},{4,5},{5,4},{6,7},{7,6},{8,9},{9,8},{10,11... | collective-permute-start | bytes 884744 | tf_op jit(solution)/shard_map/ppermute | solution.py:211
  23.9 11.5 %collective-permute-start.3 = (bf16[8,144,128]{2,1,0:T(8,128)(2,1)S(1)}, bf16[8,144,128]{2,1,0:T(8,128)(2,1)S(1)}, u32[]{:S(2)}, u32[]{:S(2)}) collective-permute-start(bf16[8,144,128]{2,1,0:T(8,128)(2,1)S(1)} %collective-permute-done.1.refs_1_.refs_0_), channel_id=1, source_target_pairs={{0,2},{2,4},{4,6},{3,1},{5,3},{7,5},{8,10},{10,12},{12,14},{11,9},... | collective-permute-start | bytes 884744 | tf_op jit(solution)/shard_map/ppermute | solution.py:214
  28.0 19.1 %collective-permute-start.6 = (bf16[16,72,128]{2,1,0:T(8,128)(2,1)S(1)}, bf16[16,72,128]{2,1,0:T(8,128)(2,1)S(1)}, u32[]{:S(2)}, u32[]{:S(2)}) collective-permute-start(bf16[16,72,128]{2,1,0:T(8,128)(2,1)S(1)} %after.4.own_ref), channel_id=1, source_target_pairs={{0,1},{1,0},{2,3},{3,2},{4,5},{5,4},{6,7},{7,6},{8,9},{9,8},{10,11... | collective-permute-start | bytes 884744 | tf_op jit(solution)/shard_map/ppermute | solution.py:211
  33.2 17.1 %collective-permute-start.5 = (bf16[16,72,128]{2,1,0:T(8,128)(2,1)S(1)}, bf16[16,72,128]{2,1,0:T(8,128)(2,1)S(1)}, u32[]{:S(2)}, u32[]{:S(2)}) collective-permute-start(bf16[16,72,128]{2,1,0:T(8,128)(2,1)S(1)} %collective-permute-done.4.refs_0_), channel_id=1, source_target_pairs={{0,2},{2,4},{4,6},{3,1},{5,3},{7,5},{8,10},{10,12},{12,14},{11,9},... | collective-permute-start | bytes 884744 | tf_op jit(solution)/shard_map/ppermute | solution.py:214
  47.2 11.6 %collective-permute-start.7 = (bf16[16,72,128]{2,1,0:T(8,128)(2,1)S(1)}, bf16[16,72,128]{2,1,0:T(8,128)(2,1)S(1)}, u32[]{:S(2)}, u32[]{:S(2)}) collective-permute-start(bf16[16,72,128]{2,1,0:T(8,128)(2,1)S(1)} %after.5), channel_id=1, source_target_pairs={{0,2},{2,4},{4,6},{3,1},{5,3},{7,5},{8,10},{10,12},{12,14},{11,9},... | collective-permute-start | bytes 884744 | tf_op jit(solution)/shard_map/ppermute | solution.py:214
  56.7 8.4 %copy-start.1 = (f32[1152,128]{1,0:T(8,128)}, f32[1152,128]{1,0:T(8,128)S(1)}, u32[]{:S(2)}) copy-start(f32[1152,128]{1,0:T(8,128)S(1)} %ladder_rows.4.ladder_ref) | copy-start | bytes 1769476
  65.1 2.1 %copy-start.2 = (f32[1152,128]{1,0:T(8,128)}, f32[1152,128]{1,0:T(8,128)S(1)}, u32[]{:S(2)}) copy-start(f32[1152,128]{1,0:T(8,128)S(1)} %ladder_rows.5.ladder_ref) | copy-start | bytes 1769476
  65.1 37.9 %copy-start.6 = (f32[128]{0:T(128)S(1)}, f32[128]{0:T(128)}, u32[]{:S(2)}) copy-start(f32[128]{0:T(128)} %param.11) | copy-start | bytes 1540
  65.1 38.0 %copy-start.8 = (f32[96]{0:T(128)S(1)}, f32[96]{0:T(128)}, u32[]{:S(2)}) copy-start(f32[96]{0:T(128)} %param.10) | copy-start | bytes 1156
  67.2 71.0 %all-to-all-start = ((f16[256,10,2,128]{3,2,1,0:T(2,128)(2,1)}), f16[256,10,2,128]{3,2,1,0:T(2,128)(2,1)}, u32[]{:S(2)}, u32[]{:S(2)}) async-start(f16[256,10,2,128]{3,2,1,0:T(2,128)(2,1)} %bitcast.9), calls=%async_computation | async-start | bytes 2621440 | tf_op jit(solution)/shard_map/all_to_all | solution.py:235
  138.3 2.1 %copy-start = (f32[3,96,16,128]{3,2,1,0:T(8,128)S(1)}, f32[3,96,16,128]{3,2,1,0:T(8,128)}, u32[]{:S(2)}) copy-start(f32[3,96,16,128]{3,2,1,0:T(8,128)} %get-tuple-element.10.own_ref) | copy-start | bytes 7077892

commit v5 on v4

--- a/solution.py
+++ b/solution.py
@@ -37,7 +37,7 @@
     def fetch(a):
         return pltpu.make_async_copy(weight_ref.at[a], weights.at[a], arrived.at[a])
 
-    for a in range(TILES):
+    for a in range(4):
         fetch(a).start()
     held[0:TILES] = own_ref[...]
     for n, (over_ref, next_ref) in enumerate(zip(over_refs, next_refs)):
@@ -51,6 +51,11 @@
         for n in range(4):
             a = step * 4 + n
             fetch(a).wait()
+
+            @pl.when(a + 4 < TILES)
+            def _(a=a):
+                fetch(a + 4).start()
+
             row = None
             for s in range(0, slots, 4):
                 four = jnp.concatenate([held[index_ref[a, s + t]] for t in range(4)], axis=1)
@@ -82,8 +87,13 @@
     )(index, own, *over, *beyond, weights)
 
 
-def pack_kernel(ladder_ref, out_ref, rest):
-    devices = out_ref.shape[0] // (VIRT * MSG)
+def pack_kernel(ladder_ref, *refs):
+    out_ref, rest = refs[-2:]
+    devices = ladder_ref.shape[0] // (VIRT * VALUES)
+    begin = 0
+    for earlier in refs[:-2]:
+        out_ref[begin : begin + earlier.shape[0], :] = earlier[...]
+        begin += earlier.shape[0]
     tile = ROWS * TILES
     row = devices * tile
 
@@ -113,22 +123,24 @@
         pieces = []
         for v, part in enumerate(exchange_groups(parts)):
             pieces += [part, last[2 * v : 2 * v + 2], power]
-        out_ref[pl.ds(pl.multiple_of(device * VIRT * MSG, TILES), VIRT * MSG), :] = jnp.concatenate(pieces, axis=0)
-
-
-def pack(ladder):
+        place = pl.multiple_of(begin + device * VIRT * MSG, TILES)
+        out_ref[pl.ds(place, VIRT * MSG), :] = jnp.concatenate(pieces, axis=0)
+
+
+def pack(ladder, *earlier):
     rows = ladder.shape[0]
+    before = sum(x.shape[0] for x in earlier)
     vmem = pl.BlockSpec(memory_space=pltpu.VMEM)
     return pl.pallas_call(
         pack_kernel,
-        out_shape=jax.ShapeDtypeStruct((rows // VALUES * MSG, LANES), jnp.float32),
-        in_specs=[vmem],
+        out_shape=jax.ShapeDtypeStruct((before + rows // VALUES * MSG, LANES), jnp.float32),
+        in_specs=[vmem] * (1 + len(earlier)),
         out_specs=vmem,
         scratch_shapes=[pltpu.VMEM((rows // (ROWS * ROWS), LANES), jnp.float32)],
         compiler_params=pltpu.CompilerParams(vmem_limit_bytes=12 * 2**20),
         cost_estimate=pl.CostEstimate(flops=rows * LANES * 32, bytes_accessed=rows * LANES * 8, transcendentals=0),
         name="pack",
-    )(ladder)
+    )(ladder, *earlier)
 
 
 def finish_kernel(got_ref, own_ref, factor_ref, out_ref, rest, turned):
@@ -185,7 +197,7 @@
     )(x, *first)
 
 
-CHUNKS = (16, 8, 8)
+CHUNKS = (16, 16)
 
 
 def per_device(amplitudes, integrals, cd_tiles, tile_counts, eps_occ, eps_virt):
@@ -215,23 +227,14 @@
 
     half = tiles // 2
     over_a = [swapped(own[0][:half]), swapped(own[0][half:])]
-    own[1] = after(own[1], over_a[0])
-    over_b = swapped(own[1])
+    over_b = [swapped(after(own[1][:half], over_a[0])), swapped(after(own[1][half:], over_a[0]))]
     beyond_a = [passed_on(x) for x in over_a]
-    own[2] = after(own[2], over_a[1], beyond_a[0])
-    over_c = swapped(own[2])
-    beyond_b = passed_on(over_b)
-    ladder_a = ladder_rows(index, own[0], over_a, beyond_a, weights)
-    beyond_c = passed_on(after(over_c, ladder_a))
-    ladder_b = ladder_rows(index, own[1], [over_b], [beyond_b], weights)
-    ladder_c = ladder_rows(index, own[2], [over_c], [beyond_c], weights)
-    ladders = [ladder_a, ladder_b, ladder_c]
-    sent = jnp.zeros((partners // rows * VIRT * MSG, LANES), jnp.float16)
-    begin = 0
-    for devices, ladder in zip(CHUNKS, ladders):
-        sent = lax.dynamic_update_slice(sent, pack(ladder).astype(jnp.float16), (begin * VIRT * MSG, 0))
-        begin += devices
-    sent = sent.reshape(-1, MSG // 2, 2, LANES)
+    beyond_b = [passed_on(x) for x in over_b]
+    ladders = [
+        ladder_rows(index, own[0], over_a, beyond_a, weights),
+        ladder_rows(index, own[1], over_b, beyond_b, weights),
+    ]
+    sent = pack(ladders[1], pack(ladders[0])).astype(jnp.float16).reshape(-1, MSG // 2, 2, LANES)
     got = lax.all_to_all(sent, ("pair", "virt"), split_axis=0, concat_axis=0, tiled=True)
     own_occ = lax.dynamic_slice_in_dim(eps_occ, lax.axis_index("pair") * rows, rows)
     own_virt = lax.dynamic_slice_in_dim(eps_virt, me * tiles, tiles)

time: 145 us -> 146 us (level)
  Pallas kernels: 29.6 us -> 24.7 us
  waiting for transfers between devices: 40.6 us -> 45.5 us
  local copies, waits for them, and re-layouts: 4.46 us -> 8.45 us
  starting transfers between devices: 63 us -> 60.8 us
    pallas_call x3 -> x2, Pallas kernels: 20.4 us -> 15.3 us  [ladder_rows(): pl.pallas_call(functools.partial(ladder_kernel, len(over)), out_shape=jax...]
    ppermute x4, waiting for transfers between devices: 8.45 us -> 13.2 us  [swapped(): return lax.ppermute(x, 'virt', swap)]
    unnamed x18 -> x22, local copies, waits for them, and re-layouts: 0.46 us -> 5.05 us
    all_to_all x1, starting transfers between devices: 35.8 us -> 31.5 us  [per_device(): lax.all_to_all(sent, ('pair', 'virt'), split_axis=0, concat_axis=0, tiled...]
    ppermute x4, starting transfers between devices: 12.8 us -> 15.6 us  [passed_on(): return lax.ppermute(x, 'virt', relay)]
    dynamic_update_slice x2 -> x0, other arithmetic: 1.55 us -> none  [per_device(): lax.dynamic_update_slice(sent, pack(ladder).astype(jnp.float16), (begin *...]
    pallas_call x3 -> x2, Pallas kernels: 5.22 us -> 5.38 us  [pack(): pl.pallas_call(pack_kernel, out_shape=jax.ShapeDtypeStruct((before + rows...]
  transfers between devices with their start and end apart: 9 -> 9, of which waited for: 4 -> 4; matrix products, arithmetic and copies ran while one was open for 4% -> 3% of each run, Pallas kernels for 12% -> 7%
where the time goes in v5:
time: 146 us; the launch traced here: 145 us
  starting transfers between devices  60.8 us (42%)
  waiting for transfers between devices  45.5 us (31%)
  Pallas kernels  24.7 us (17%)
  local copies, waits for them, and re-layouts  8.45 us (6%)
  other arithmetic  5.55 us (4%)
    all_to_all x1, waiting for transfers between devices, per_device(): lax.all_to_all(sent, ('pair', 'virt'), split_axis=0, concat_axis=0, tiled...  32.3 us
    all_to_all x1, starting transfers between devices, per_device(): lax.all_to_all(sent, ('pair', 'virt'), split_axis=0, concat_axis=0, tiled...  31.5 us
    ppermute x4, starting transfers between devices, passed_on(): return lax.ppermute(x, 'virt', relay)  15.6 us
    pallas_call x2, Pallas kernels, ladder_rows(): pl.pallas_call(functools.partial(ladder_kernel, len(over)), out_shape=jax...  15.3 us
    ppermute x4, starting transfers between devices, swapped(): return lax.ppermute(x, 'virt', swap)  13.8 us
    ppermute x4, waiting for transfers between devices, swapped(): return lax.ppermute(x, 'virt', swap)  13.2 us
    pallas_call x2, Pallas kernels, pack(): pl.pallas_call(pack_kernel, out_shape=jax.ShapeDtypeStruct((before + rows...  5.38 us
    unnamed x22, local copies, waits for them, and re-layouts  5.05 us
  transfers between devices with their start and end apart: 9, of which 4 were waited for; matrix products, arithmetic and copies ran while one was open for 3% of the time, Pallas kernels for 7%

profile of v5, /device:TPU:1, one launch (start us, length us, event | category | flops | bytes accessed | tf_op | source)
XLA Modules:
  0.0 145.3 jit_solution(5363908089239591317)
XLA Ops:
  0.0 1.4 slice_bitcast_fusion
  1.8 7.8 %collective-permute-start = (bf16[8,144,128]{2,1,0:T(8,128)(2,1)S(1)}, bf16[8,144,128]{2,1,0:T(8,128)(2,1)S(1)}, u32[]{:S(2)}, u32[]{:S(2)}) collective-permute-start(bf16[8,144,128]{2,1,0:T(8,128)(2,1)S(1)} %bitcast.26), channel_id=1, source_target_pairs={{0,1},{1,0},{2,3},{3,2},{4,5},{5,4},{6,7},{7,6},{8,9},{9,8},{10,11... | collective-permute-start | bytes 884744 | tf_op jit(solution)/shard_map/ppermute | solution.py:223
  9.9 6.9 %collective-permute-done.refs_0_ = bf16[8,144,128]{2,1,0:T(8,128)(2,1)S(1)} collective-permute-done((bf16[8,144,128]{2,1,0:T(8,128)(2,1)S(1)}, bf16[8,144,128]{2,1,0:T(8,128)(2,1)S(1)}, u32[]{:S(2)}, u32[]{:S(2)}) %collective-permute-start) | collective-permute-done | bytes 294944 | tf_op jit(solution)/shard_map/ppermute | solution.py:223
  16.8 5.7 %collective-permute-start.2 = (bf16[8,144,128]{2,1,0:T(8,128)(2,1)S(1)}, bf16[8,144,128]{2,1,0:T(8,128)(2,1)S(1)}, u32[]{:S(2)}, u32[]{:S(2)}) collective-permute-start(bf16[8,144,128]{2,1,0:T(8,128)(2,1)S(1)} %after.3), channel_id=1, source_target_pairs={{0,1},{1,0},{2,3},{3,2},{4,5},{5,4},{6,7},{7,6},{8,9},{9,8},{10,11... | collective-permute-start | bytes 884744 | tf_op jit(solution)/shard_map/ppermute | solution.py:223
  22.7 3.5 %collective-permute-start.6 = (bf16[8,144,128]{2,1,0:T(8,128)(2,1)S(1)}, bf16[8,144,128]{2,1,0:T(8,128)(2,1)S(1)}, u32[]{:S(2)}, u32[]{:S(2)}) collective-permute-start(bf16[8,144,128]{2,1,0:T(8,128)(2,1)S(1)} %collective-permute-done.refs_0_), channel_id=1, source_target_pairs={{0,2},{2,4},{4,6},{3,1},{5,3},{7,5},{8,10},{10,12},{12,14},{11,9},... | collective-permute-start | bytes 884744 | tf_op jit(solution)/shard_map/ppermute | solution.py:226
  26.2 3.2 %collective-permute-start.7 = (bf16[8,144,128]{2,1,0:T(8,128)(2,1)S(1)}, bf16[8,144,128]{2,1,0:T(8,128)(2,1)S(1)}, u32[]{:S(2)}, u32[]{:S(2)}) collective-permute-start(bf16[8,144,128]{2,1,0:T(8,128)(2,1)S(1)} %collective-permute-done.5.refs_1_), channel_id=1, source_target_pairs={{0,2},{2,4},{4,6},{3,1},{5,3},{7,5},{8,10},{10,12},{12,14},{11,9},... | collective-permute-start | bytes 884744 | tf_op jit(solution)/shard_map/ppermute | solution.py:226
  29.6 1.2 copy.7
  30.8 2.3 %collective-permute-done.2.refs_1_ = bf16[8,144,128]{2,1,0:T(8,128)(2,1)S(1)} collective-permute-done((bf16[8,144,128]{2,1,0:T(8,128)(2,1)S(1)}, bf16[8,144,128]{2,1,0:T(8,128)(2,1)S(1)}, u32[]{:S(2)}, u32[]{:S(2)}) %collective-permute-start.2) | collective-permute-done | bytes 294944 | tf_op jit(solution)/shard_map/ppermute | solution.py:223
  33.0 3.8 %collective-permute-start.4 = (bf16[8,144,128]{2,1,0:T(8,128)(2,1)S(1)}, bf16[8,144,128]{2,1,0:T(8,128)(2,1)S(1)}, u32[]{:S(2)}, u32[]{:S(2)}) collective-permute-start(bf16[8,144,128]{2,1,0:T(8,128)(2,1)S(1)} %collective-permute-done.2.refs_1_), channel_id=1, source_target_pairs={{0,2},{2,4},{4,6},{3,1},{5,3},{7,5},{8,10},{10,12},{12,14},{11,9},... | collective-permute-start | bytes 884744 | tf_op jit(solution)/shard_map/ppermute | solution.py:226
  36.8 4.0 %collective-permute-done.1.refs_0_ = bf16[8,144,128]{2,1,0:T(8,128)(2,1)S(1)} collective-permute-done((bf16[8,144,128]{2,1,0:T(8,128)(2,1)S(1)}, bf16[8,144,128]{2,1,0:T(8,128)(2,1)S(1)}, u32[]{:S(2)}, u32[]{:S(2)}) %collective-permute-start.1) | collective-permute-done | bytes 294944 | tf_op jit(solution)/shard_map/ppermute | solution.py:223
  40.8 5.2 %collective-permute-start.3 = (bf16[8,144,128]{2,1,0:T(8,128)(2,1)S(1)}, bf16[8,144,128]{2,1,0:T(8,128)(2,1)S(1)}, u32[]{:S(2)}, u32[]{:S(2)}) collective-permute-start(bf16[8,144,128]{2,1,0:T(8,128)(2,1)S(1)} %collective-permute-done.1.refs_0_), channel_id=1, source_target_pairs={{0,2},{2,4},{4,6},{3,1},{5,3},{7,5},{8,10},{10,12},{12,14},{11,9},... | collective-permute-start | bytes 884744 | tf_op jit(solution)/shard_map/ppermute | solution.py:226
  47.5 1.0 copy-done.3
  48.5 1.0 copy-done.5
  49.4 7.7 %ladder_rows.3.ladder_ref = f32[2304,128]{1,0:T(8,128)S(1)} custom-call(s32[16,20]{1,0:T(8,128)S(1)} %fusion.2.index_ref, bf16[16,144,128]{2,1,0:T(8,128)(2,1)S(1)} %bitcast.19, bf16[8,144,128]{2,1,0:T(8,128)(2,1)S(1)} %collective-permute-done.refs_0_, bf16[8,144,128]{2,1,0:T(8,128)(2,1)S(1)} %collective-permute-done.5.refs_1_, ...), custom_call_target="tpu_custom_call" | custom-call | flops 1509949440 | bytes 10485760 | tf_op jit(solution)/shard_map/ladder_rows/pallas_call | solution.py:72
  57.1 2.6 %pack.2.refs_0_ = f32[2560,128]{1,0:T(8,128)S(1)} custom-call(f32[2304,128]{1,0:T(8,128)S(1)} %ladder_rows.3.ladder_ref), custom_call_target="tpu_custom_call" | custom-call | flops 9437184 | bytes 2359296 | tf_op jit(solution)/shard_map/pack/pallas_call | solution.py:134
  59.8 7.7 %ladder_rows.2.ladder_ref = f32[2304,128]{1,0:T(8,128)S(1)} custom-call(s32[16,20]{1,0:T(8,128)S(1)} %fusion.2.index_ref, bf16[16,144,128]{2,1,0:T(8,128)(2,1)S(1)} %bitcast.18, bf16[8,144,128]{2,1,0:T(8,128)(2,1)S(1)} %collective-permute-done.1.refs_0_, bf16[8,144,128]{2,1,0:T(8,128)(2,1)S(1)} %collective-permute-done.2.refs_1_, ...), custom_call_target="tpu_custom_call" | custom-call | flops 1509949440 | bytes 10485760 | tf_op jit(solution)/shard_map/ladder_rows/pallas_call | solution.py:72
  67.5 2.7 %pack.3 = f32[5120,128]{1,0:T(8,128)S(1)} custom-call(f32[2304,128]{1,0:T(8,128)S(1)} %ladder_rows.2.ladder_ref, f32[2560,128]{1,0:T(8,128)S(1)} %pack.2.refs_0_), custom_call_target="tpu_custom_call" | custom-call | flops 9437184 | bytes 2359296 | tf_op jit(solution)/shard_map/pack/pallas_call | solution.py:134
  70.2 1.2 convert_element_type.8
  71.5 31.5 %all-to-all-start = ((f16[256,10,2,128]{3,2,1,0:T(2,128)(2,1)}), f16[256,10,2,128]{3,2,1,0:T(2,128)(2,1)}, u32[]{:S(2)}, u32[]{:S(2)}) async-start(f16[256,10,2,128]{3,2,1,0:T(2,128)(2,1)} %bitcast.24), calls=%async_computation | async-start | bytes 2621440 | tf_op jit(solution)/shard_map/all_to_all | solution.py:238
  103.3 2.6 %subtract_divide_fusion = (f32[3,96,16,128]{3,2,1,0:T(8,128)}, f32[3,96,16,128]{3,2,1,0:T(8,128)}) fusion(f32[128]{0:T(128)S(1)} %copy-done.8, f32[3,96,16]{2,1,0:T(8,128)S(1)} %broadcast_subtract_fusion, f32[3,48,16,128]{3,2,1,0:T(8,128)S(1)} %bitcast.16, f32[3,48,16,128]{3,2,1,0:T(8,128)S(1)} %bitcast.17), kind=kLoop, calls=%fused_computation | loop fusion | flops 2359296 | bytes 7096832 | tf_op jit(solution)/shard_map/div | solution.py:248
  105.9 32.3 %all-to-all-done = f16[256,10,2,128]{3,2,1,0:T(2,128)(2,1)} async-done(((f16[256,10,2,128]{3,2,1,0:T(2,128)(2,1)}), f16[256,10,2,128]{3,2,1,0:T(2,128)(2,1)}, u32[]{:S(2)}, u32[]{:S(2)}) %all-to-all-start) | async-done | bytes 1310752 | tf_op jit(solution)/shard_map/all_to_all | solution.py:238
  138.2 1.5 %convert.1.got_ref = f32[5120,128]{1,0:T(8,128)S(1)} convert(f16[5120,128]{1,0:T(8,128)(2,1)} %bitcast.13) | non-fusion elementwise | flops 655360 | bytes 3932160 | tf_op jit(solution)/shard_map/convert_element_type | solution.py:248
  139.7 1.7 %copy-done.1 = f32[3,96,16,128]{3,2,1,0:T(8,128)S(1)} copy-done((f32[3,96,16,128]{3,2,1,0:T(8,128)S(1)}, f32[3,96,16,128]{3,2,1,0:T(8,128)}, u32[]{:S(2)}) %copy-start.1) | copy-done | bytes 2359320
  141.4 3.9 %finish.1 = bf16[3,96,16,128]{3,2,1,0:T(8,128)(2,1)} custom-call(f32[5120,128]{1,0:T(8,128)S(1)} %convert.1.got_ref, f32[3,96,16,128]{3,2,1,0:T(8,128)S(1)} %copy-done.1, f32[3,96,16,128]{3,2,1,0:T(8,128)S(1)} %copy-done), custom_call_target="tpu_custom_call" | custom-call | flops 33554432 | bytes 8388608 | tf_op jit(solution)/shard_map/finish/pallas_call | solution.py:171
  (39 shorter events, 2.7 us)
Async XLA Ops:
  1.4 24.7 %copy-start.6 = (bf16[16,3,48,128]{3,0,2,1:T(8,128)(2,1)}, bf16[16,3,48,128]{3,0,2,1:T(8,128)(2,1)S(1)}, u32[]{:S(2)}) copy-start(bf16[16,3,48,128]{3,0,2,1:T(8,128)(2,1)S(1)} %get-tuple-element.6) | copy-start | bytes 1769476
  1.8 15.0 %collective-permute-start = (bf16[8,144,128]{2,1,0:T(8,128)(2,1)S(1)}, bf16[8,144,128]{2,1,0:T(8,128)(2,1)S(1)}, u32[]{:S(2)}, u32[]{:S(2)}) collective-permute-start(bf16[8,144,128]{2,1,0:T(8,128)(2,1)S(1)} %bitcast.26), channel_id=1, source_target_pairs={{0,1},{1,0},{2,3},{3,2},{4,5},{5,4},{6,7},{7,6},{8,9},{9,8},{10,11... | collective-permute-start | bytes 884744 | tf_op jit(solution)/shard_map/ppermute | solution.py:223
  9.7 16.5 %collective-permute-start.5 = (bf16[8,144,128]{2,1,0:T(8,128)(2,1)S(1)}, bf16[8,144,128]{2,1,0:T(8,128)(2,1)S(1)}, u32[]{:S(2)}, u32[]{:S(2)}) collective-permute-start(bf16[8,144,128]{2,1,0:T(8,128)(2,1)S(1)} %bitcast.25), channel_id=1, source_target_pairs={{0,1},{1,0},{2,3},{3,2},{4,5},{5,4},{6,7},{7,6},{8,9},{9,8},{10,11... | collective-permute-start | bytes 884744 | tf_op jit(solution)/shard_map/ppermute | solution.py:223
  9.8 36.2 %copy-start.7 = (s32[16,20]{1,0:T(8,128)S(1)}, s32[16,20]{1,0:T(8,128)}, u32[]{:S(2)}) copy-start(s32[16,20]{1,0:T(8,128)} %param.8) | copy-start | bytes 3844
  9.8 36.2 %copy-start.9 = (s32[16]{0:T(128)S(1)}, s32[16]{0:T(128)}, u32[]{:S(2)}) copy-start(s32[16]{0:T(128)} %param.9) | copy-start | bytes 196
  16.8 16.2 %collective-permute-start.2 = (bf16[8,144,128]{2,1,0:T(8,128)(2,1)S(1)}, bf16[8,144,128]{2,1,0:T(8,128)(2,1)S(1)}, u32[]{:S(2)}, u32[]{:S(2)}) collective-permute-start(bf16[8,144,128]{2,1,0:T(8,128)(2,1)S(1)} %after.3), channel_id=1, source_target_pairs={{0,1},{1,0},{2,3},{3,2},{4,5},{5,4},{6,7},{7,6},{8,9},{9,8},{10,11... | collective-permute-start | bytes 884744 | tf_op jit(solution)/shard_map/ppermute | solution.py:223
  22.6 18.2 %collective-permute-start.1 = (bf16[8,144,128]{2,1,0:T(8,128)(2,1)S(1)}, bf16[8,144,128]{2,1,0:T(8,128)(2,1)S(1)}, u32[]{:S(2)}, u32[]{:S(2)}) collective-permute-start(bf16[8,144,128]{2,1,0:T(8,128)(2,1)S(1)} %after.2), channel_id=1, source_target_pairs={{0,1},{1,0},{2,3},{3,2},{4,5},{5,4},{6,7},{7,6},{8,9},{9,8},{10,11... | collective-permute-start | bytes 884744 | tf_op jit(solution)/shard_map/ppermute | solution.py:223
  22.7 23.4 %collective-permute-start.6 = (bf16[8,144,128]{2,1,0:T(8,128)(2,1)S(1)}, bf16[8,144,128]{2,1,0:T(8,128)(2,1)S(1)}, u32[]{:S(2)}, u32[]{:S(2)}) collective-permute-start(bf16[8,144,128]{2,1,0:T(8,128)(2,1)S(1)} %collective-permute-done.refs_0_), channel_id=1, source_target_pairs={{0,2},{2,4},{4,6},{3,1},{5,3},{7,5},{8,10},{10,12},{12,14},{11,9},... | collective-permute-start | bytes 884744 | tf_op jit(solution)/shard_map/ppermute | solution.py:226
  26.2 20.6 %collective-permute-start.7 = (bf16[8,144,128]{2,1,0:T(8,128)(2,1)S(1)}, bf16[8,144,128]{2,1,0:T(8,128)(2,1)S(1)}, u32[]{:S(2)}, u32[]{:S(2)}) collective-permute-start(bf16[8,144,128]{2,1,0:T(8,128)(2,1)S(1)} %collective-permute-done.5.refs_1_), channel_id=1, source_target_pairs={{0,2},{2,4},{4,6},{3,1},{5,3},{7,5},{8,10},{10,12},{12,14},{11,9},... | collective-permute-start | bytes 884744 | tf_op jit(solution)/shard_map/ppermute | solution.py:226
  33.0 26.7 %collective-permute-start.4 = (bf16[8,144,128]{2,1,0:T(8,128)(2,1)S(1)}, bf16[8,144,128]{2,1,0:T(8,128)(2,1)S(1)}, u32[]{:S(2)}, u32[]{:S(2)}) collective-permute-start(bf16[8,144,128]{2,1,0:T(8,128)(2,1)S(1)} %collective-permute-done.2.refs_1_), channel_id=1, source_target_pairs={{0,2},{2,4},{4,6},{3,1},{5,3},{7,5},{8,10},{10,12},{12,14},{11,9},... | collective-permute-start | bytes 884744 | tf_op jit(solution)/shard_map/ppermute | solution.py:226
  40.8 19.0 %collective-permute-start.3 = (bf16[8,144,128]{2,1,0:T(8,128)(2,1)S(1)}, bf16[8,144,128]{2,1,0:T(8,128)(2,1)S(1)}, u32[]{:S(2)}, u32[]{:S(2)}) collective-permute-start(bf16[8,144,128]{2,1,0:T(8,128)(2,1)S(1)} %collective-permute-done.1.refs_0_), channel_id=1, source_target_pairs={{0,2},{2,4},{4,6},{3,1},{5,3},{7,5},{8,10},{10,12},{12,14},{11,9},... | collective-permute-start | bytes 884744 | tf_op jit(solution)/shard_map/ppermute | solution.py:226
  46.1 0.7 copy-start.2
  46.8 0.7 copy-start.4
  47.5 1.0 copy-start.3
  48.5 1.0 copy-start.5
  70.2 32.7 %copy-start.8 = (f32[128]{0:T(128)S(1)}, f32[128]{0:T(128)}, u32[]{:S(2)}) copy-start(f32[128]{0:T(128)} %param.11) | copy-start | bytes 1540
  70.2 32.8 %copy-start.10 = (f32[96]{0:T(128)S(1)}, f32[96]{0:T(128)}, u32[]{:S(2)}) copy-start(f32[96]{0:T(128)} %param.10) | copy-start | bytes 1156
  71.5 66.7 %all-to-all-start = ((f16[256,10,2,128]{3,2,1,0:T(2,128)(2,1)}), f16[256,10,2,128]{3,2,1,0:T(2,128)(2,1)}, u32[]{:S(2)}, u32[]{:S(2)}) async-start(f16[256,10,2,128]{3,2,1,0:T(2,128)(2,1)} %bitcast.24), calls=%async_computation | async-start | bytes 2621440 | tf_op jit(solution)/shard_map/all_to_all | solution.py:238
  105.9 33.8 %copy-start = (f32[3,96,16,128]{3,2,1,0:T(8,128)S(1)}, f32[3,96,16,128]{3,2,1,0:T(8,128)}, u32[]{:S(2)}) copy-start(f32[3,96,16,128]{3,2,1,0:T(8,128)} %get-tuple-element.11.factor_ref) | copy-start | bytes 7077892
  139.7 1.7 %copy-start.1 = (f32[3,96,16,128]{3,2,1,0:T(8,128)S(1)}, f32[3,96,16,128]{3,2,1,0:T(8,128)}, u32[]{:S(2)}) copy-start(f32[3,96,16,128]{3,2,1,0:T(8,128)} %get-tuple-element.12.own_ref) | copy-start | bytes 7077892

commit v6 on v5

--- a/solution.py
+++ b/solution.py
@@ -29,33 +29,34 @@
     return parts
 
 
-def ladder_kernel(pieces, index_ref, own_ref, *refs):
-    over_refs, next_refs = refs[:pieces], refs[pieces : 2 * pieces]
-    weight_ref, out_ref, held, weights, arrived = refs[2 * pieces :]
+GROUP = 4
+
+
+def ladder_kernel(index_ref, *refs):
+    weight_ref, out_ref, held, weights, landed, arrived = refs[-6:]
     slots = weight_ref.shape[1] // LANES
 
     def fetch(a):
         return pltpu.make_async_copy(weight_ref.at[a], weights.at[a], arrived.at[a])
 
-    for a in range(4):
+    columns, begin = [], 0
+    for n, ref in enumerate(refs[:-6]):
+        place = held.at[pl.ds(begin, ref.shape[0])]
+        columns.append(pltpu.make_async_copy(ref, place, landed.at[n]))
+        begin += ref.shape[0]
+    for copy in columns:
+        copy.start()
+    for a in range(2 * GROUP):
         fetch(a).start()
-    held[0:TILES] = own_ref[...]
-    for n, (over_ref, next_ref) in enumerate(zip(over_refs, next_refs)):
-        count = over_ref.shape[0]
-        held[TILES + n * count : TILES + (n + 1) * count] = over_ref[...]
-        held[2 * TILES + n * count : 2 * TILES + (n + 1) * count] = next_ref[...]
     held[3 * TILES] = jnp.zeros_like(held[3 * TILES])
-
-    @pl.loop(0, TILES // 4)
-    def _(step):
-        for n in range(4):
-            a = step * 4 + n
+    for copy in columns:
+        copy.wait()
+    for first in range(0, TILES, GROUP):
+        for a in range(first, first + GROUP):
             fetch(a).wait()
-
-            @pl.when(a + 4 < TILES)
-            def _(a=a):
-                fetch(a + 4).start()
-
+            if a + 2 * GROUP < TILES:
+                fetch(a + 2 * GROUP).start()
+        for a in range(first, first + GROUP):
             row = None
             for s in range(0, slots, 4):
                 four = jnp.concatenate([held[index_ref[a, s + t]] for t in range(4)], axis=1)
@@ -65,18 +66,19 @@
             out_ref[pl.ds(a, row.shape[0], stride=TILES), :] = row
 
 
-def ladder_rows(index, own, over, beyond, weights):
-    tiles, pairs, depth = own.shape
-    k = weights.shape[1]
-    smem, vmem = pl.BlockSpec(memory_space=pltpu.SMEM), pl.BlockSpec(memory_space=pltpu.VMEM)
-    return pl.pallas_call(
-        functools.partial(ladder_kernel, len(over)),
+def ladder_rows(index, columns, weights):
+    pairs, depth = columns[0].shape[1:]
+    tiles, k = weights.shape[:2]
+    anywhere = pl.BlockSpec(memory_space=pl.ANY)
+    return pl.pallas_call(
+        ladder_kernel,
         out_shape=jax.ShapeDtypeStruct((pairs * tiles, LANES), jnp.float32),
-        in_specs=[smem] + [vmem] * (1 + 2 * len(over)) + [pl.BlockSpec(memory_space=pl.ANY)],
-        out_specs=vmem,
+        in_specs=[pl.BlockSpec(memory_space=pltpu.SMEM)] + [anywhere] * (len(columns) + 1),
+        out_specs=pl.BlockSpec(memory_space=pltpu.VMEM),
         scratch_shapes=[
             pltpu.VMEM((3 * tiles + 1, pairs, depth), jnp.bfloat16),
             pltpu.VMEM(weights.shape, jnp.bfloat16),
+            pltpu.SemaphoreType.DMA((len(columns),)),
             pltpu.SemaphoreType.DMA((tiles,)),
         ],
         compiler_params=pltpu.CompilerParams(vmem_limit_bytes=48 * 2**20),
@@ -84,7 +86,7 @@
             flops=2 * pairs * k * LANES * tiles, bytes_accessed=2 * tiles * k * LANES, transcendentals=0
         ),
         name="ladder_rows",
-    )(index, own, *over, *beyond, weights)
+    )(index, *columns, weights)
 
 
 def pack_kernel(ladder_ref, *refs):
@@ -143,42 +145,60 @@
     )(ladder, *earlier)
 
 
-def finish_kernel(got_ref, own_ref, factor_ref, out_ref, rest, turned):
-    def store(i, j, partner):
-        out_ref[i, j] = (own_ref[i, j] + partner * factor_ref[i, j]).astype(out_ref.dtype)
-
-    for device in range(8):
-        block = got_ref[device * VIRT * MSG : (device + 1) * VIRT * MSG, :]
-        cut = [block[v * MSG : (v + 1) * MSG] for v in range(VIRT)]
-        cut = [c[:VALUES] * jnp.exp2(-c[VALUES : VALUES + 1]) for c in cut]
-        main = jnp.concatenate([c[:TILES] for c in cut], axis=0).T
-        rest[device * TILES : (device + 1) * TILES, :] = jnp.concatenate([c[TILES:] for c in cut], axis=0)
-        for k in range(8):
-            store(k % ROWS, device * ROWS + k // ROWS, main[k * TILES : (k + 1) * TILES])
-    for half in range(2):
-        parts = [rest[pl.ds(2 * v + half, 8, stride=TILES), :] for v in range(VIRT)]
+def finish_kernel(occ_ref, own_occ_ref, got_ref, first_ref, second_ref, va_ref, vb_ref, out_ref, rest, turned):
+    step = pl.program_id(0)
+    half = pl.num_programs(0) // 2
+
+    def work(ladder_ref):
+        def store(i, j, partner):
+            bottom = (own_occ_ref[i] + occ_ref[step * 8 * ROWS + j]) - va_ref[...] - vb_ref[...]
+            out_ref[i, j] = ((ladder_ref[i, j] + partner) * (1.0 / bottom)).astype(out_ref.dtype)
+
+        for device in range(8):
+            block = got_ref[device * VIRT * MSG : (device + 1) * VIRT * MSG, :]
+            cut = [block[v * MSG : (v + 1) * MSG] for v in range(VIRT)]
+            cut = [c[:VALUES] * jnp.exp2(-c[VALUES : VALUES + 1]) for c in cut]
+            main = jnp.concatenate([c[:TILES] for c in cut], axis=0).T
+            rest[device * TILES : (device + 1) * TILES, :] = jnp.concatenate([c[TILES:] for c in cut], axis=0)
+            for k in range(8):
+                store(k % ROWS, device * ROWS + k // ROWS, main[k * TILES : (k + 1) * TILES])
+        for side in range(2):
+            parts = [rest[pl.ds(2 * v + side, 8, stride=TILES), :] for v in range(VIRT)]
+            for n, part in enumerate(exchange_groups(parts)):
+                turned[pl.ds(side * 8 + n, 8, stride=TILES), :] = part
+        columns = turned[...].T
+        parts = [columns[v * TILES : (v + 1) * TILES] for v in range(VIRT)]
         for n, part in enumerate(exchange_groups(parts)):
-            turned[pl.ds(half * 8 + n, 8, stride=TILES), :] = part
-    columns = turned[...].T
-    parts = [columns[v * TILES : (v + 1) * TILES] for v in range(VIRT)]
-    for n, part in enumerate(exchange_groups(parts)):
-        store(ROWS - 1, n * ROWS + ROWS - 1, part)
-
-
-def finish(got, own, factor):
-    rows, partners = own.shape[:2]
-    tile = pl.BlockSpec((rows, 8 * rows, TILES, LANES), lambda g: (0, g, 0, 0))
+            store(ROWS - 1, n * ROWS + ROWS - 1, part)
+
+    @pl.when(step < half)
+    def _():
+        work(first_ref)
+
+    @pl.when(step >= half)
+    def _():
+        work(second_ref)
+
+
+def finish(occ, own_occ, got, ladders, va, vb):
+    rows, partners = own_occ.shape[0], occ.shape[0]
+    steps = partners // (8 * rows)
+    smem = pl.BlockSpec(memory_space=pltpu.SMEM)
+    shape = (rows, 8 * rows, TILES, LANES)
+    first = pl.BlockSpec(shape, lambda g: (0, jnp.minimum(g, steps // 2 - 1), 0, 0))
+    second = pl.BlockSpec(shape, lambda g: (0, jnp.maximum(g - steps // 2, 0), 0, 0))
+    table = pl.BlockSpec((TILES, LANES), lambda g: (0, 0))
     return pl.pallas_call(
         finish_kernel,
-        out_shape=jax.ShapeDtypeStruct(own.shape, jnp.bfloat16),
-        grid=(partners // (8 * rows),),
-        in_specs=[pl.BlockSpec((8 * VIRT * MSG, LANES), lambda g: (g, 0)), tile, tile],
-        out_specs=tile,
+        out_shape=jax.ShapeDtypeStruct((rows, partners, TILES, LANES), jnp.bfloat16),
+        grid=(steps,),
+        in_specs=[smem, smem, pl.BlockSpec((8 * VIRT * MSG, LANES), lambda g: (g, 0)), first, second, table, table],
+        out_specs=pl.BlockSpec(shape, lambda g: (0, g, 0, 0)),
         scratch_shapes=[pltpu.VMEM((8 * TILES, LANES), jnp.float32), pltpu.VMEM((LANES, LANES), jnp.float32)],
         compiler_params=pltpu.CompilerParams(vmem_limit_bytes=12 * 2**20),
         cost_estimate=pl.CostEstimate(flops=2**25, bytes_accessed=2**23, transcendentals=0),
         name="finish",
-    )(got, own, factor)
+    )(occ, own_occ, got, *ladders, va, vb)
 
 
 def after_kernel(x_ref, *refs):
@@ -230,22 +250,19 @@
     over_b = [swapped(after(own[1][:half], over_a[0])), swapped(after(own[1][half:], over_a[0]))]
     beyond_a = [passed_on(x) for x in over_a]
     beyond_b = [passed_on(x) for x in over_b]
+    beyond_a = [after(beyond_a[0], beyond_a[1]), beyond_a[1]]
     ladders = [
-        ladder_rows(index, own[0], over_a, beyond_a, weights),
-        ladder_rows(index, own[1], over_b, beyond_b, weights),
+        ladder_rows(index, [own[0], *over_a, *beyond_a], weights),
+        ladder_rows(index, [own[1], *over_b, *beyond_b], weights),
     ]
     sent = pack(ladders[1], pack(ladders[0])).astype(jnp.float16).reshape(-1, MSG // 2, 2, LANES)
     got = lax.all_to_all(sent, ("pair", "virt"), split_axis=0, concat_axis=0, tiled=True)
     own_occ = lax.dynamic_slice_in_dim(eps_occ, lax.axis_index("pair") * rows, rows)
     own_virt = lax.dynamic_slice_in_dim(eps_virt, me * tiles, tiles)
-    denominator = (
-        own_occ[:, None, None, None]
-        + eps_occ[None, :, None, None]
-        - own_virt[None, None, :, None]
-        - eps_virt[None, None, None, :]
-    )
-    ladder = jnp.concatenate([x.reshape(rows, -1, tiles, LANES) for x in ladders], axis=1)
-    return finish(got.reshape(-1, LANES).astype(jnp.float32), ladder / denominator, 1.0 / denominator)
+    va = jnp.broadcast_to(own_virt[:, None], (tiles, LANES))
+    vb = jnp.broadcast_to(eps_virt[None, :], (tiles, LANES))
+    ladders = [x.reshape(rows, -1, tiles, LANES) for x in ladders]
+    return finish(eps_occ, own_occ, got.reshape(-1, LANES).astype(jnp.float32), ladders, va, vb)
 
 
 def solution(mesh):

time: 146 us -> 140 us (0.959)
  local copies, waits for them, and re-layouts: 8.45 us -> 3.34 us
  waiting for transfers between devices: 45.5 us -> 48.5 us
  other arithmetic: 5.55 us -> 2.81 us
    unnamed x22 -> x12, local copies, waits for them, and re-layouts: 5.05 us -> 0.92 us
    all_to_all x1, waiting for transfers between devices: 32.3 us -> 35.1 us  [per_device(): lax.all_to_all(sent, ('pair', 'virt'), split_axis=0, concat_axis=0, tiled...]
    div x1 -> x0, other arithmetic: 2.58 us -> none  [per_device(): 1.0 / denominator]
  transfers between devices with their start and end apart: 9 -> 9, of which waited for: 4 -> 4; matrix products, arithmetic and copies ran while one was open for 3% -> 0% of each run, Pallas kernels for 7% -> 7%
where the time goes in v6:
time: 140 us; the launch traced here: 139 us
  starting transfers between devices  61 us (44%)
  waiting for transfers between devices  48.5 us (35%)
  Pallas kernels  23.5 us (17%)
  local copies, waits for them, and re-layouts  3.34 us (2%)
  other arithmetic  2.81 us (2%)
    all_to_all x1, waiting for transfers between devices, per_device(): lax.all_to_all(sent, ('pair', 'virt'), split_axis=0, concat_axis=0, tiled...  35.1 us
    all_to_all x1, starting transfers between devices, per_device(): lax.all_to_all(sent, ('pair', 'virt'), split_axis=0, concat_axis=0, tiled...  31.4 us
    ppermute x4, starting transfers between devices, passed_on(): return lax.ppermute(x, 'virt', relay)  15.8 us
    ppermute x4, starting transfers between devices, swapped(): return lax.ppermute(x, 'virt', swap)  13.8 us
    pallas_call x2, Pallas kernels, ladder_rows(): pl.pallas_call(ladder_kernel, out_shape=jax.ShapeDtypeStruct((pairs * til...  13.7 us
    ppermute x4, waiting for transfers between devices, swapped(): return lax.ppermute(x, 'virt', swap)  13.4 us
    pallas_call x2, Pallas kernels, pack(): pl.pallas_call(pack_kernel, out_shape=jax.ShapeDtypeStruct((before + rows...  5.38 us
    pallas_call x1, Pallas kernels, finish(): pl.pallas_call(finish_kernel, out_shape=jax.ShapeDtypeStruct((rows, partn...  4.4 us
  transfers between devices with their start and end apart: 9, of which 4 were waited for; matrix products, arithmetic and copies ran while one was open for 0% of the time, Pallas kernels for 7%

profile of v6, /device:TPU:1, one launch (start us, length us, event | category | flops | bytes accessed | tf_op | source)
XLA Modules:
  0.0 139.5 jit_solution(9470249140012901554)
XLA Ops:
  0.0 1.4 %slice_bitcast_fusion = (bf16[16,3,48,128]{3,0,2,1:T(8,128)(2,1)S(1)}, bf16[16,3,48,128]{3,0,2,1:T(8,128)(2,1)S(1)}) fusion(bf16[3,96,16,128]{3,2,1,0:T(8,128)(2,1)} %param.6), kind=kLoop, calls=%fused_computation | loop fusion | bytes 2359296 | tf_op jit(solution)/shard_map/transpose | solution.py:232
  1.5 0.3 fusion.4
  1.8 7.8 %collective-permute-start = (bf16[8,144,128]{2,1,0:T(8,128)(2,1)S(1)}, bf16[8,144,128]{2,1,0:T(8,128)(2,1)S(1)}, u32[]{:S(2)}, u32[]{:S(2)}) collective-permute-start(bf16[8,144,128]{2,1,0:T(8,128)(2,1)S(1)} %bitcast.26), channel_id=1, source_target_pairs={{0,1},{1,0},{2,3},{3,2},{4,5},{5,4},{6,7},{7,6},{8,9},{9,8},{10,11... | collective-permute-start | bytes 884744 | tf_op jit(solution)/shard_map/ppermute | solution.py:243
  9.9 6.9 %collective-permute-done.refs_0_.refs_1_ = bf16[8,144,128]{2,1,0:T(8,128)(2,1)S(1)} collective-permute-done((bf16[8,144,128]{2,1,0:T(8,128)(2,1)S(1)}, bf16[8,144,128]{2,1,0:T(8,128)(2,1)S(1)}, u32[]{:S(2)}, u32[]{:S(2)}) %collective-permute-start) | collective-permute-done | bytes 294944 | tf_op jit(solution)/shard_map/ppermute | solution.py:243
  16.8 5.7 %collective-permute-start.2 = (bf16[8,144,128]{2,1,0:T(8,128)(2,1)S(1)}, bf16[8,144,128]{2,1,0:T(8,128)(2,1)S(1)}, u32[]{:S(2)}, u32[]{:S(2)}) collective-permute-start(bf16[8,144,128]{2,1,0:T(8,128)(2,1)S(1)} %after.4), channel_id=1, source_target_pairs={{0,1},{1,0},{2,3},{3,2},{4,5},{5,4},{6,7},{7,6},{8,9},{9,8},{10,11... | collective-permute-start | bytes 884744 | tf_op jit(solution)/shard_map/ppermute | solution.py:243
  22.6 0.1 collective-permute-start.1
  22.7 3.5 %collective-permute-start.6 = (bf16[8,144,128]{2,1,0:T(8,128)(2,1)S(1)}, bf16[8,144,128]{2,1,0:T(8,128)(2,1)S(1)}, u32[]{:S(2)}, u32[]{:S(2)}) collective-permute-start(bf16[8,144,128]{2,1,0:T(8,128)(2,1)S(1)} %collective-permute-done.refs_0_.refs_1_), channel_id=1, source_target_pairs={{0,2},{2,4},{4,6},{3,1},{5,3},{7,5},{8,10},{10,12},{12,14},{11,9},... | collective-permute-start | bytes 884744 | tf_op jit(solution)/shard_map/ppermute | solution.py:246
  26.2 3.2 %collective-permute-start.7 = (bf16[8,144,128]{2,1,0:T(8,128)(2,1)S(1)}, bf16[8,144,128]{2,1,0:T(8,128)(2,1)S(1)}, u32[]{:S(2)}, u32[]{:S(2)}) collective-permute-start(bf16[8,144,128]{2,1,0:T(8,128)(2,1)S(1)} %collective-permute-done.5.refs_2_), channel_id=1, source_target_pairs={{0,2},{2,4},{4,6},{3,1},{5,3},{7,5},{8,10},{10,12},{12,14},{11,9},... | collective-permute-start | bytes 884744 | tf_op jit(solution)/shard_map/ppermute | solution.py:246
  29.4 0.2 copy.11
  29.6 0.9 copy-done.2
  30.5 0.2 copy.7
  30.7 2.4 %collective-permute-done.2.refs_2_ = bf16[8,144,128]{2,1,0:T(8,128)(2,1)S(1)} collective-permute-done((bf16[8,144,128]{2,1,0:T(8,128)(2,1)S(1)}, bf16[8,144,128]{2,1,0:T(8,128)(2,1)S(1)}, u32[]{:S(2)}, u32[]{:S(2)}) %collective-permute-start.2) | collective-permute-done | bytes 294944 | tf_op jit(solution)/shard_map/ppermute | solution.py:243
  33.0 3.8 %collective-permute-start.4 = (bf16[8,144,128]{2,1,0:T(8,128)(2,1)S(1)}, bf16[8,144,128]{2,1,0:T(8,128)(2,1)S(1)}, u32[]{:S(2)}, u32[]{:S(2)}) collective-permute-start(bf16[8,144,128]{2,1,0:T(8,128)(2,1)S(1)} %collective-permute-done.2.refs_2_), channel_id=1, source_target_pairs={{0,2},{2,4},{4,6},{3,1},{5,3},{7,5},{8,10},{10,12},{12,14},{11,9},... | collective-permute-start | bytes 884744 | tf_op jit(solution)/shard_map/ppermute | solution.py:246
  36.8 4.1 %collective-permute-done.1.refs_1_ = bf16[8,144,128]{2,1,0:T(8,128)(2,1)} collective-permute-done((bf16[8,144,128]{2,1,0:T(8,128)(2,1)S(1)}, bf16[8,144,128]{2,1,0:T(8,128)(2,1)}, u32[]{:S(2)}, u32[]{:S(2)}) %collective-permute-start.1) | collective-permute-done | bytes 294944 | tf_op jit(solution)/shard_map/ppermute | solution.py:243
  40.9 5.4 %collective-permute-start.3 = (bf16[8,144,128]{2,1,0:T(8,128)(2,1)}, bf16[8,144,128]{2,1,0:T(8,128)(2,1)S(1)}, u32[]{:S(2)}, u32[]{:S(2)}) collective-permute-start(bf16[8,144,128]{2,1,0:T(8,128)(2,1)} %collective-permute-done.1.refs_1_), channel_id=1, source_target_pairs={{0,2},{2,4},{4,6},{3,1},{5,3},{7,5},{8,10},{10,12},{12,14},{11,9},... | collective-permute-start | bytes 884744 | tf_op jit(solution)/shard_map/ppermute | solution.py:246
  46.4 6.9 %ladder_rows.3.ladder_ref = f32[2304,128]{1,0:T(8,128)S(1)} custom-call(s32[16,20]{1,0:T(8,128)S(1)} %fusion.2.index_ref, bf16[16,144,128]{2,1,0:T(8,128)(2,1)S(1)} %bitcast.19, bf16[8,144,128]{2,1,0:T(8,128)(2,1)S(1)} %collective-permute-done.refs_0_.refs_1_, bf16[8,144,128]{2,1,0:T(8,128)(2,1)S(1)} %collective-permute-done.5.refs_2_, ...), custom_call_target="tpu_custom_call" | custom-call | flops 1509949440 | bytes 10485760 | tf_op jit(solution)/shard_map/ladder_rows/pallas_call | solution.py:73
  53.3 2.6 %pack.2.refs_0_ = f32[2560,128]{1,0:T(8,128)S(1)} custom-call(f32[2304,128]{1,0:T(8,128)S(1)} %ladder_rows.3.ladder_ref), custom_call_target="tpu_custom_call" | custom-call | flops 9437184 | bytes 2359296 | tf_op jit(solution)/shard_map/pack/pallas_call | solution.py:136
  55.9 6.8 %ladder_rows.2.ladder_ref = f32[2304,128]{1,0:T(8,128)S(1)} custom-call(s32[16,20]{1,0:T(8,128)S(1)} %fusion.2.index_ref, bf16[16,144,128]{2,1,0:T(8,128)(2,1)S(1)} %bitcast.18, bf16[8,144,128]{2,1,0:T(8,128)(2,1)} %collective-permute-done.1.refs_1_, bf16[8,144,128]{2,1,0:T(8,128)(2,1)S(1)} %collective-permute-done.2.refs_2_, ...), custom_call_target="tpu_custom_call" | custom-call | flops 1509949440 | bytes 10485760 | tf_op jit(solution)/shard_map/ladder_rows/pallas_call | solution.py:73
  62.8 2.7 %pack.3 = f32[5120,128]{1,0:T(8,128)S(1)} custom-call(f32[2304,128]{1,0:T(8,128)S(1)} %ladder_rows.2.ladder_ref, f32[2560,128]{1,0:T(8,128)S(1)} %pack.2.refs_0_), custom_call_target="tpu_custom_call" | custom-call | flops 9437184 | bytes 2359296 | tf_op jit(solution)/shard_map/pack/pallas_call | solution.py:136
  65.5 1.2 convert_element_type.8
  66.8 31.4 %all-to-all-start = ((f16[256,10,2,128]{3,2,1,0:T(2,128)(2,1)}), f16[256,10,2,128]{3,2,1,0:T(2,128)(2,1)}, u32[]{:S(2)}, u32[]{:S(2)}) async-start(f16[256,10,2,128]{3,2,1,0:T(2,128)(2,1)} %bitcast.24), calls=%async_computation | async-start | bytes 2621440 | tf_op jit(solution)/shard_map/all_to_all | solution.py:259
  98.4 35.1 %all-to-all-done = f16[256,10,2,128]{3,2,1,0:T(2,128)(2,1)} async-done(((f16[256,10,2,128]{3,2,1,0:T(2,128)(2,1)}), f16[256,10,2,128]{3,2,1,0:T(2,128)(2,1)}, u32[]{:S(2)}, u32[]{:S(2)}) %all-to-all-start) | async-done | bytes 1310752 | tf_op jit(solution)/shard_map/all_to_all | solution.py:259
  133.5 1.5 %convert.1.got_ref = f32[5120,128]{1,0:T(8,128)S(1)} convert(f16[5120,128]{1,0:T(8,128)(2,1)} %bitcast.13) | non-fusion elementwise | flops 655360 | bytes 3932160 | tf_op jit(solution)/shard_map/convert_element_type | solution.py:265
  135.0 4.4 %finish.1 = bf16[3,96,16,128]{3,2,1,0:T(8,128)(2,1)} custom-call(f32[96]{0:T(128)S(1)} %copy-done, f32[3]{0:T(128)S(1)} %dynamic_slice.6.own_occ_ref, f32[5120,128]{1,0:T(8,128)S(1)} %convert.1.got_ref, f32[3,48,16,128]{3,2,1,0:T(8,128)S(1)} %bitcast.17, f32[3,48,16,128]{3,2,1,0:T(8,128)S(1)} %bitcast.16, f32[16,128]{1,0:T(8,128)S(1)} %broadcast_in_dim.27.va_ref, ...), custom_call_target="tpu_custom_call" | custom-call | flops 33554432 | bytes 8388608 | tf_op jit(solution)/shard_map/finish/pallas_call | solution.py:191
  (29 shorter events, 0.7 us)
Async XLA Ops:
  1.4 24.7 %copy-start.1 = (bf16[16,3,48,128]{3,0,2,1:T(8,128)(2,1)}, bf16[16,3,48,128]{3,0,2,1:T(8,128)(2,1)S(1)}, u32[]{:S(2)}) copy-start(bf16[16,3,48,128]{3,0,2,1:T(8,128)(2,1)S(1)} %get-tuple-element.6) | copy-start | bytes 1769476
  1.8 15.0 %collective-permute-start = (bf16[8,144,128]{2,1,0:T(8,128)(2,1)S(1)}, bf16[8,144,128]{2,1,0:T(8,128)(2,1)S(1)}, u32[]{:S(2)}, u32[]{:S(2)}) collective-permute-start(bf16[8,144,128]{2,1,0:T(8,128)(2,1)S(1)} %bitcast.26), channel_id=1, source_target_pairs={{0,1},{1,0},{2,3},{3,2},{4,5},{5,4},{6,7},{7,6},{8,9},{9,8},{10,11... | collective-permute-start | bytes 884744 | tf_op jit(solution)/shard_map/ppermute | solution.py:243
  9.7 16.5 %collective-permute-start.5 = (bf16[8,144,128]{2,1,0:T(8,128)(2,1)S(1)}, bf16[8,144,128]{2,1,0:T(8,128)(2,1)S(1)}, u32[]{:S(2)}, u32[]{:S(2)}) collective-permute-start(bf16[8,144,128]{2,1,0:T(8,128)(2,1)S(1)} %bitcast.25), channel_id=1, source_target_pairs={{0,1},{1,0},{2,3},{3,2},{4,5},{5,4},{6,7},{7,6},{8,9},{9,8},{10,11... | collective-permute-start | bytes 884744 | tf_op jit(solution)/shard_map/ppermute | solution.py:243
  16.8 16.2 %collective-permute-start.2 = (bf16[8,144,128]{2,1,0:T(8,128)(2,1)S(1)}, bf16[8,144,128]{2,1,0:T(8,128)(2,1)S(1)}, u32[]{:S(2)}, u32[]{:S(2)}) collective-permute-start(bf16[8,144,128]{2,1,0:T(8,128)(2,1)S(1)} %after.4), channel_id=1, source_target_pairs={{0,1},{1,0},{2,3},{3,2},{4,5},{5,4},{6,7},{7,6},{8,9},{9,8},{10,11... | collective-permute-start | bytes 884744 | tf_op jit(solution)/shard_map/ppermute | solution.py:243
  22.6 23.7 %copy-start.3 = (s32[16,20]{1,0:T(8,128)S(1)}, s32[16,20]{1,0:T(8,128)}, u32[]{:S(2)}) copy-start(s32[16,20]{1,0:T(8,128)} %param.8) | copy-start | bytes 3844
  22.6 23.7 %copy-start.4 = (s32[16]{0:T(128)S(1)}, s32[16]{0:T(128)}, u32[]{:S(2)}) copy-start(s32[16]{0:T(128)} %param.9) | copy-start | bytes 196
  22.6 18.3 %collective-permute-start.1 = (bf16[8,144,128]{2,1,0:T(8,128)(2,1)S(1)}, bf16[8,144,128]{2,1,0:T(8,128)(2,1)}, u32[]{:S(2)}, u32[]{:S(2)}) collective-permute-start(bf16[8,144,128]{2,1,0:T(8,128)(2,1)S(1)} %after.3), channel_id=1, source_target_pairs={{0,1},{1,0},{2,3},{3,2},{4,5},{5,4},{6,7},{7,6},{8,9},{9,8},{10,11... | collective-permute-start | bytes 884744 | tf_op jit(solution)/shard_map/ppermute | solution.py:243
  22.7 23.7 %collective-permute-start.6 = (bf16[8,144,128]{2,1,0:T(8,128)(2,1)S(1)}, bf16[8,144,128]{2,1,0:T(8,128)(2,1)S(1)}, u32[]{:S(2)}, u32[]{:S(2)}) collective-permute-start(bf16[8,144,128]{2,1,0:T(8,128)(2,1)S(1)} %collective-permute-done.refs_0_.refs_1_), channel_id=1, source_target_pairs={{0,2},{2,4},{4,6},{3,1},{5,3},{7,5},{8,10},{10,12},{12,14},{11,9},... | collective-permute-start | bytes 884744 | tf_op jit(solution)/shard_map/ppermute | solution.py:246
  26.2 20.2 %collective-permute-start.7 = (bf16[8,144,128]{2,1,0:T(8,128)(2,1)S(1)}, bf16[8,144,128]{2,1,0:T(8,128)(2,1)S(1)}, u32[]{:S(2)}, u32[]{:S(2)}) collective-permute-start(bf16[8,144,128]{2,1,0:T(8,128)(2,1)S(1)} %collective-permute-done.5.refs_2_), channel_id=1, source_target_pairs={{0,2},{2,4},{4,6},{3,1},{5,3},{7,5},{8,10},{10,12},{12,14},{11,9},... | collective-permute-start | bytes 884744 | tf_op jit(solution)/shard_map/ppermute | solution.py:246
  29.4 1.1 copy-start.2
  33.0 22.9 %collective-permute-start.4 = (bf16[8,144,128]{2,1,0:T(8,128)(2,1)S(1)}, bf16[8,144,128]{2,1,0:T(8,128)(2,1)S(1)}, u32[]{:S(2)}, u32[]{:S(2)}) collective-permute-start(bf16[8,144,128]{2,1,0:T(8,128)(2,1)S(1)} %collective-permute-done.2.refs_2_), channel_id=1, source_target_pairs={{0,2},{2,4},{4,6},{3,1},{5,3},{7,5},{8,10},{10,12},{12,14},{11,9},... | collective-permute-start | bytes 884744 | tf_op jit(solution)/shard_map/ppermute | solution.py:246
  40.9 15.0 %collective-permute-start.3 = (bf16[8,144,128]{2,1,0:T(8,128)(2,1)}, bf16[8,144,128]{2,1,0:T(8,128)(2,1)S(1)}, u32[]{:S(2)}, u32[]{:S(2)}) collective-permute-start(bf16[8,144,128]{2,1,0:T(8,128)(2,1)} %collective-permute-done.1.refs_1_), channel_id=1, source_target_pairs={{0,2},{2,4},{4,6},{3,1},{5,3},{7,5},{8,10},{10,12},{12,14},{11,9},... | collective-permute-start | bytes 884744 | tf_op jit(solution)/shard_map/ppermute | solution.py:246
  66.7 31.5 %copy-start.5 = (f32[128]{0:T(128)S(1)}, f32[128]{0:T(128)}, u32[]{:S(2)}) copy-start(f32[128]{0:T(128)} %param.11) | copy-start | bytes 1540
  66.8 31.6 %copy-start = (f32[96]{0:T(128)S(1)}, f32[96]{0:T(128)}, u32[]{:S(2)}) copy-start(f32[96]{0:T(128)} %occ_ref.1) | copy-start | bytes 1156
  66.8 66.7 %all-to-all-start = ((f16[256,10,2,128]{3,2,1,0:T(2,128)(2,1)}), f16[256,10,2,128]{3,2,1,0:T(2,128)(2,1)}, u32[]{:S(2)}, u32[]{:S(2)}) async-start(f16[256,10,2,128]{3,2,1,0:T(2,128)(2,1)} %bitcast.24), calls=%async_computation | async-start | bytes 2621440 | tf_op jit(solution)/shard_map/all_to_all | solution.py:259

commit v7 on v6

--- a/solution.py
+++ b/solution.py
@@ -29,34 +29,74 @@
     return parts
 
 
-GROUP = 4
-
-
-def ladder_kernel(index_ref, *refs):
-    weight_ref, out_ref, held, weights, landed, arrived = refs[-6:]
+def packer(ladder_ref, rest):
+    devices = ladder_ref.shape[0] // (VIRT * VALUES)
+    tile = ROWS * TILES
+    row = devices * tile
+
+    def widest(step, so_far):
+        return jnp.maximum(so_far, jnp.abs(ladder_ref[pl.ds(pl.multiple_of(step * tile, TILES), tile), :]))
+
+    largest = lax.fori_loop(0, ROWS * devices, widest, jnp.zeros((tile, LANES), jnp.float32), unroll=4)
+    largest = jnp.maximum(jnp.max(jnp.max(largest, axis=0, keepdims=True), axis=1, keepdims=True), 1e-30)
+    power = 14.0 - jnp.ceil(jnp.log2(jnp.broadcast_to(largest, (2, LANES))))
+    scale = jnp.exp2(power)[:1]
+
+    for octet in range(devices // 8):
+        for half in range(2):
+            first = octet * 8 * tile + (ROWS - 1) * (row + TILES) + half * 8
+            parts = [ladder_ref[pl.ds(first + n, 8, stride=tile), :] for n in range(8)]
+            for v, part in enumerate(exchange_groups(parts)):
+                rest[pl.ds(octet * 8 * TILES + 2 * v + half, 8, stride=TILES), :] = part
+
+    def rows(device):
+        first = device * tile
+        parts = [ladder_ref[pl.ds(first + (k // ROWS) * row + (k % ROWS) * TILES, TILES), :] * scale for k in range(8)]
+        last = rest[pl.ds(device * TILES, TILES), :] * scale
+        pieces = []
+        for v, part in enumerate(exchange_groups(parts)):
+            pieces += [part, last[2 * v : 2 * v + 2], power]
+        return jnp.concatenate(pieces, axis=0)
+
+    return devices, rows
+
+
+WAITS = (1, 1, 2, 4, 4, 4)
+AHEAD = 4
+
+
+def ladder_kernel(packs, index_ref, *refs):
+    columns_refs, refs = refs[: len(refs) - 6 - 3 * packs], refs[len(refs) - 6 - 3 * packs :]
+    weight_ref, refs = refs[0], refs[1:]
+    if packs:
+        earlier_ref, out_ref, message_ref, held, weights, landed, arrived, rest = refs
+    else:
+        out_ref, held, weights, landed, arrived = refs
     slots = weight_ref.shape[1] // LANES
 
     def fetch(a):
         return pltpu.make_async_copy(weight_ref.at[a], weights.at[a], arrived.at[a])
 
     columns, begin = [], 0
-    for n, ref in enumerate(refs[:-6]):
+    for n, ref in enumerate(columns_refs):
         place = held.at[pl.ds(begin, ref.shape[0])]
         columns.append(pltpu.make_async_copy(ref, place, landed.at[n]))
         begin += ref.shape[0]
     for copy in columns:
         copy.start()
-    for a in range(2 * GROUP):
+    for a in range(AHEAD):
         fetch(a).start()
     held[3 * TILES] = jnp.zeros_like(held[3 * TILES])
+    devices, rows = packer(earlier_ref, rest) if packs else (0, None)
     for copy in columns:
         copy.wait()
-    for first in range(0, TILES, GROUP):
-        for a in range(first, first + GROUP):
+    first = 0
+    for count in WAITS:
+        for a in range(first, first + count):
             fetch(a).wait()
-            if a + 2 * GROUP < TILES:
-                fetch(a + 2 * GROUP).start()
-        for a in range(first, first + GROUP):
+            if a + AHEAD < TILES:
+                fetch(a + AHEAD).start()
+        for a in range(first, first + count):
             row = None
             for s in range(0, slots, 4):
                 four = jnp.concatenate([held[index_ref[a, s + t]] for t in range(4)], axis=1)
@@ -64,85 +104,61 @@
                 term = jnp.dot(four, part, preferred_element_type=jnp.float32)
                 row = term if row is None else row + term
             out_ref[pl.ds(a, row.shape[0], stride=TILES), :] = row
-
-
-def ladder_rows(index, columns, weights):
+            for device in range(a * devices // TILES, (a + 1) * devices // TILES):
+                message_ref[device * VIRT * MSG : (device + 1) * VIRT * MSG, :] = rows(device)
+        first += count
+
+
+def ladder_rows(index, columns, weights, earlier=None):
     pairs, depth = columns[0].shape[1:]
     tiles, k = weights.shape[:2]
-    anywhere = pl.BlockSpec(memory_space=pl.ANY)
-    return pl.pallas_call(
-        ladder_kernel,
-        out_shape=jax.ShapeDtypeStruct((pairs * tiles, LANES), jnp.float32),
-        in_specs=[pl.BlockSpec(memory_space=pltpu.SMEM)] + [anywhere] * (len(columns) + 1),
-        out_specs=pl.BlockSpec(memory_space=pltpu.VMEM),
-        scratch_shapes=[
-            pltpu.VMEM((3 * tiles + 1, pairs, depth), jnp.bfloat16),
-            pltpu.VMEM(weights.shape, jnp.bfloat16),
-            pltpu.SemaphoreType.DMA((len(columns),)),
-            pltpu.SemaphoreType.DMA((tiles,)),
-        ],
+    anywhere, vmem = pl.BlockSpec(memory_space=pl.ANY), pl.BlockSpec(memory_space=pltpu.VMEM)
+    packs = earlier is not None
+    out_shape = [jax.ShapeDtypeStruct((pairs * tiles, LANES), jnp.float32)]
+    scratch = [
+        pltpu.VMEM((3 * tiles + 1, pairs, depth), jnp.bfloat16),
+        pltpu.VMEM(weights.shape, jnp.bfloat16),
+        pltpu.SemaphoreType.DMA((len(columns),)),
+        pltpu.SemaphoreType.DMA((tiles,)),
+    ]
+    if packs:
+        out_shape.append(jax.ShapeDtypeStruct((earlier.shape[0] // VALUES * MSG, LANES), jnp.float32))
+        scratch.append(pltpu.VMEM((earlier.shape[0] // (ROWS * ROWS), LANES), jnp.float32))
+    return pl.pallas_call(
+        functools.partial(ladder_kernel, int(packs)),
+        out_shape=out_shape,
+        in_specs=[pl.BlockSpec(memory_space=pltpu.SMEM)] + [anywhere] * (len(columns) + 1) + [vmem] * packs,
+        out_specs=[vmem] * len(out_shape),
+        scratch_shapes=scratch,
         compiler_params=pltpu.CompilerParams(vmem_limit_bytes=48 * 2**20),
         cost_estimate=pl.CostEstimate(
             flops=2 * pairs * k * LANES * tiles, bytes_accessed=2 * tiles * k * LANES, transcendentals=0
         ),
         name="ladder_rows",
-    )(index, *columns, weights)
-
-
-def pack_kernel(ladder_ref, *refs):
-    out_ref, rest = refs[-2:]
-    devices = ladder_ref.shape[0] // (VIRT * VALUES)
-    begin = 0
-    for earlier in refs[:-2]:
-        out_ref[begin : begin + earlier.shape[0], :] = earlier[...]
-        begin += earlier.shape[0]
-    tile = ROWS * TILES
-    row = devices * tile
-
-    def widest(step, so_far):
-        return jnp.maximum(so_far, jnp.abs(ladder_ref[pl.ds(pl.multiple_of(step * tile, TILES), tile), :]))
-
-    largest = lax.fori_loop(0, ROWS * devices, widest, jnp.zeros((tile, LANES), jnp.float32), unroll=4)
-    largest = jnp.maximum(jnp.max(jnp.max(largest, axis=0, keepdims=True), axis=1, keepdims=True), 1e-30)
-    power = 14.0 - jnp.ceil(jnp.log2(jnp.broadcast_to(largest, (2, LANES))))
-    scale = jnp.exp2(power)[:1]
-
-    @pl.loop(0, devices // 8)
-    def _(octet):
-        for half in range(2):
-            first = (ROWS - 1) * (row + TILES) + half * 8
-            parts = [ladder_ref[pl.ds(octet * 8 * tile + first + n, 8, stride=tile), :] for n in range(8)]
-            for v, part in enumerate(exchange_groups(parts)):
-                rest[pl.ds(octet * 8 * TILES + 2 * v + half, 8, stride=TILES), :] = part
-
-    @pl.loop(0, devices, unroll=2)
-    def _(device):
-        first = pl.multiple_of(device * tile, TILES)
-        parts = [
-            ladder_ref[pl.ds(first + (k // ROWS) * row + (k % ROWS) * TILES, TILES), :] * scale for k in range(8)
-        ]
-        last = rest[pl.ds(pl.multiple_of(device * TILES, TILES), TILES), :] * scale
-        pieces = []
-        for v, part in enumerate(exchange_groups(parts)):
-            pieces += [part, last[2 * v : 2 * v + 2], power]
-        place = pl.multiple_of(begin + device * VIRT * MSG, TILES)
-        out_ref[pl.ds(place, VIRT * MSG), :] = jnp.concatenate(pieces, axis=0)
-
-
-def pack(ladder, *earlier):
+    )(index, *columns, weights, *([earlier] if packs else []))
+
+
+def pack_kernel(ladder_ref, earlier_ref, out_ref, rest):
+    begin = earlier_ref.shape[0]
+    out_ref[:begin, :] = earlier_ref[...]
+    devices, rows = packer(ladder_ref, rest)
+    for device in range(devices):
+        out_ref[begin + device * VIRT * MSG : begin + (device + 1) * VIRT * MSG, :] = rows(device)
+
+
+def pack(ladder, earlier):
     rows = ladder.shape[0]
-    before = sum(x.shape[0] for x in earlier)
     vmem = pl.BlockSpec(memory_space=pltpu.VMEM)
     return pl.pallas_call(
         pack_kernel,
-        out_shape=jax.ShapeDtypeStruct((before + rows // VALUES * MSG, LANES), jnp.float32),
-        in_specs=[vmem] * (1 + len(earlier)),
+        out_shape=jax.ShapeDtypeStruct((earlier.shape[0] + rows // VALUES * MSG, LANES), jnp.float32),
+        in_specs=[vmem, vmem],
         out_specs=vmem,
         scratch_shapes=[pltpu.VMEM((rows // (ROWS * ROWS), LANES), jnp.float32)],
         compiler_params=pltpu.CompilerParams(vmem_limit_bytes=12 * 2**20),
         cost_estimate=pl.CostEstimate(flops=rows * LANES * 32, bytes_accessed=rows * LANES * 8, transcendentals=0),
         name="pack",
-    )(ladder, *earlier)
+    )(ladder, earlier)
 
 
 def finish_kernel(occ_ref, own_occ_ref, got_ref, first_ref, second_ref, va_ref, vb_ref, out_ref, rest, turned):
@@ -152,10 +168,12 @@
     def work(ladder_ref):
         def store(i, j, partner):
             bottom = (own_occ_ref[i] + occ_ref[step * 8 * ROWS + j]) - va_ref[...] - vb_ref[...]
-            out_ref[i, j] = ((ladder_ref[i, j] + partner) * (1.0 / bottom)).astype(out_ref.dtype)
+            own = ladder_ref[i, lax.rem(step, half) * 8 * ROWS + j]
+            out_ref[i, j] = ((own + partner) * (1.0 / bottom)).astype(out_ref.dtype)
 
         for device in range(8):
-            block = got_ref[device * VIRT * MSG : (device + 1) * VIRT * MSG, :]
+            first = pl.multiple_of((step * 8 + device) * VIRT * MSG, TILES)
+            block = got_ref[pl.ds(first, VIRT * MSG), :]
             cut = [block[v * MSG : (v + 1) * MSG] for v in range(VIRT)]
             cut = [c[:VALUES] * jnp.exp2(-c[VALUES : VALUES + 1]) for c in cut]
             main = jnp.concatenate([c[:TILES] for c in cut], axis=0).T
@@ -185,14 +203,12 @@
     steps = partners // (8 * rows)
     smem = pl.BlockSpec(memory_space=pltpu.SMEM)
     shape = (rows, 8 * rows, TILES, LANES)
-    first = pl.BlockSpec(shape, lambda g: (0, jnp.minimum(g, steps // 2 - 1), 0, 0))
-    second = pl.BlockSpec(shape, lambda g: (0, jnp.maximum(g - steps // 2, 0), 0, 0))
-    table = pl.BlockSpec((TILES, LANES), lambda g: (0, 0))
+    vmem = pl.BlockSpec(memory_space=pltpu.VMEM)
     return pl.pallas_call(
         finish_kernel,
         out_shape=jax.ShapeDtypeStruct((rows, partners, TILES, LANES), jnp.bfloat16),
         grid=(steps,),
-        in_specs=[smem, smem, pl.BlockSpec((8 * VIRT * MSG, LANES), lambda g: (g, 0)), first, second, table, table],
+        in_specs=[smem, smem, vmem, vmem, vmem, vmem, vmem],
         out_specs=pl.BlockSpec(shape, lambda g: (0, g, 0, 0)),
         scratch_shapes=[pltpu.VMEM((8 * TILES, LANES), jnp.float32), pltpu.VMEM((LANES, LANES), jnp.float32)],
         compiler_params=pltpu.CompilerParams(vmem_limit_bytes=12 * 2**20),
@@ -251,11 +267,10 @@
     beyond_a = [passed_on(x) for x in over_a]
     beyond_b = [passed_on(x) for x in over_b]
     beyond_a = [after(beyond_a[0], beyond_a[1]), beyond_a[1]]
-    ladders = [
-        ladder_rows(index, [own[0], *over_a, *beyond_a], weights),
-        ladder_rows(index, [own[1], *over_b, *beyond_b], weights),
-    ]
-    sent = pack(ladders[1], pack(ladders[0])).astype(jnp.float16).reshape(-1, MSG // 2, 2, LANES)
+    [ladder_a] = ladder_rows(index, [own[0], *over_a, *beyond_a], weights)
+    ladder_b, messages = ladder_rows(index, [own[1], *over_b, *beyond_b], weights, ladder_a)
+    ladders = [ladder_a, ladder_b]
+    sent = pack(ladder_b, messages).astype(jnp.float16).reshape(-1, MSG // 2, 2, LANES)
     got = lax.all_to_all(sent, ("pair", "virt"), split_axis=0, concat_axis=0, tiled=True)
     own_occ = lax.dynamic_slice_in_dim(eps_occ, lax.axis_index("pair") * rows, rows)
     own_virt = lax.dynamic_slice_in_dim(eps_virt, me * tiles, tiles)

time: 140 us -> 141 us (level)
    pallas_call x4 -> x3, Pallas kernels: 19.1 us -> 18.9 us  [the longest x2 16.2 us: ladder_rows(): pl.pallas_call(functools.partial(ladder_kernel, int(packs)), out_shape=ou...]
  transfers between devices with their start and end apart: 9 -> 9, of which waited for: 4 -> 4; matrix products, arithmetic and copies ran while one was open for 0% -> 0% of each run, Pallas kernels for 7% -> 6%
where the time goes in v7:
time: 141 us; the launch traced here: 140 us
  starting transfers between devices  62.2 us (44%)
  waiting for transfers between devices  48.5 us (34%)
  Pallas kernels  23.1 us (16%)
  local copies, waits for them, and re-layouts  3.34 us (2%)
  other arithmetic  2.8 us (2%)
    all_to_all x1, waiting for transfers between devices, per_device(): lax.all_to_all(sent, ('pair', 'virt'), split_axis=0, concat_axis=0, tiled...  35.1 us
    all_to_all x1, starting transfers between devices, per_device(): lax.all_to_all(sent, ('pair', 'virt'), split_axis=0, concat_axis=0, tiled...  32.7 us
    pallas_call x2, Pallas kernels, ladder_rows(): pl.pallas_call(functools.partial(ladder_kernel, int(packs)), out_shape=ou...  16.2 us
    ppermute x4, starting transfers between devices, passed_on(): return lax.ppermute(x, 'virt', relay)  15.8 us
    ppermute x4, starting transfers between devices, swapped(): return lax.ppermute(x, 'virt', swap)  13.8 us
    ppermute x4, waiting for transfers between devices, swapped(): return lax.ppermute(x, 'virt', swap)  13.4 us
    pallas_call x1, Pallas kernels, finish(): pl.pallas_call(finish_kernel, out_shape=jax.ShapeDtypeStruct((rows, partn...  4.21 us
  transfers between devices with their start and end apart: 9, of which 4 were waited for; matrix products, arithmetic and copies ran while one was open for 0% of the time, Pallas kernels for 6%

profile of v7, /device:TPU:1, one launch (start us, length us, event | category | flops | bytes accessed | tf_op | source)
XLA Modules:
  0.0 140.3 jit_solution(6545123348264658996)
XLA Ops:
  0.0 1.4 %slice_bitcast_fusion = (bf16[16,3,48,128]{3,0,2,1:T(8,128)(2,1)S(1)}, bf16[16,3,48,128]{3,0,2,1:T(8,128)(2,1)S(1)}) fusion(bf16[3,96,16,128]{3,2,1,0:T(8,128)(2,1)} %param.6), kind=kLoop, calls=%fused_computation | loop fusion | bytes 2359296 | tf_op jit(solution)/shard_map/transpose | solution.py:248
  1.5 0.3 fusion.4
  1.8 7.8 %collective-permute-start = (bf16[8,144,128]{2,1,0:T(8,128)(2,1)S(1)}, bf16[8,144,128]{2,1,0:T(8,128)(2,1)S(1)}, u32[]{:S(2)}, u32[]{:S(2)}) collective-permute-start(bf16[8,144,128]{2,1,0:T(8,128)(2,1)S(1)} %bitcast.26), channel_id=1, source_target_pairs={{0,1},{1,0},{2,3},{3,2},{4,5},{5,4},{6,7},{7,6},{8,9},{9,8},{10,11... | collective-permute-start | bytes 884744 | tf_op jit(solution)/shard_map/ppermute | solution.py:259
  9.7 0.1 collective-permute-start.5
  9.9 6.9 %collective-permute-done.refs_0_.refs_1_ = bf16[8,144,128]{2,1,0:T(8,128)(2,1)S(1)} collective-permute-done((bf16[8,144,128]{2,1,0:T(8,128)(2,1)S(1)}, bf16[8,144,128]{2,1,0:T(8,128)(2,1)S(1)}, u32[]{:S(2)}, u32[]{:S(2)}) %collective-permute-start) | collective-permute-done | bytes 294944 | tf_op jit(solution)/shard_map/ppermute | solution.py:259
  16.8 5.7 %collective-permute-start.2 = (bf16[8,144,128]{2,1,0:T(8,128)(2,1)S(1)}, bf16[8,144,128]{2,1,0:T(8,128)(2,1)S(1)}, u32[]{:S(2)}, u32[]{:S(2)}) collective-permute-start(bf16[8,144,128]{2,1,0:T(8,128)(2,1)S(1)} %after.4), channel_id=1, source_target_pairs={{0,1},{1,0},{2,3},{3,2},{4,5},{5,4},{6,7},{7,6},{8,9},{9,8},{10,11... | collective-permute-start | bytes 884744 | tf_op jit(solution)/shard_map/ppermute | solution.py:259
  22.6 0.1 collective-permute-start.1
  22.7 3.5 %collective-permute-start.6 = (bf16[8,144,128]{2,1,0:T(8,128)(2,1)S(1)}, bf16[8,144,128]{2,1,0:T(8,128)(2,1)S(1)}, u32[]{:S(2)}, u32[]{:S(2)}) collective-permute-start(bf16[8,144,128]{2,1,0:T(8,128)(2,1)S(1)} %collective-permute-done.refs_0_.refs_1_), channel_id=1, source_target_pairs={{0,2},{2,4},{4,6},{3,1},{5,3},{7,5},{8,10},{10,12},{12,14},{11,9},... | collective-permute-start | bytes 884744 | tf_op jit(solution)/shard_map/ppermute | solution.py:262
  26.2 3.2 %collective-permute-start.7 = (bf16[8,144,128]{2,1,0:T(8,128)(2,1)S(1)}, bf16[8,144,128]{2,1,0:T(8,128)(2,1)S(1)}, u32[]{:S(2)}, u32[]{:S(2)}) collective-permute-start(bf16[8,144,128]{2,1,0:T(8,128)(2,1)S(1)} %collective-permute-done.5.refs_2_), channel_id=1, source_target_pairs={{0,2},{2,4},{4,6},{3,1},{5,3},{7,5},{8,10},{10,12},{12,14},{11,9},... | collective-permute-start | bytes 884744 | tf_op jit(solution)/shard_map/ppermute | solution.py:262
  29.4 0.2 copy.11
  29.6 0.9 copy-done.2
  30.5 0.2 copy.7
  30.7 2.4 %collective-permute-done.2.refs_2_ = bf16[8,144,128]{2,1,0:T(8,128)(2,1)S(1)} collective-permute-done((bf16[8,144,128]{2,1,0:T(8,128)(2,1)S(1)}, bf16[8,144,128]{2,1,0:T(8,128)(2,1)S(1)}, u32[]{:S(2)}, u32[]{:S(2)}) %collective-permute-start.2) | collective-permute-done | bytes 294944 | tf_op jit(solution)/shard_map/ppermute | solution.py:259
  33.0 3.8 %collective-permute-start.4 = (bf16[8,144,128]{2,1,0:T(8,128)(2,1)S(1)}, bf16[8,144,128]{2,1,0:T(8,128)(2,1)S(1)}, u32[]{:S(2)}, u32[]{:S(2)}) collective-permute-start(bf16[8,144,128]{2,1,0:T(8,128)(2,1)S(1)} %collective-permute-done.2.refs_2_), channel_id=1, source_target_pairs={{0,2},{2,4},{4,6},{3,1},{5,3},{7,5},{8,10},{10,12},{12,14},{11,9},... | collective-permute-start | bytes 884744 | tf_op jit(solution)/shard_map/ppermute | solution.py:262
  36.8 4.1 %collective-permute-done.1.refs_1_ = bf16[8,144,128]{2,1,0:T(8,128)(2,1)} collective-permute-done((bf16[8,144,128]{2,1,0:T(8,128)(2,1)S(1)}, bf16[8,144,128]{2,1,0:T(8,128)(2,1)}, u32[]{:S(2)}, u32[]{:S(2)}) %collective-permute-start.1) | collective-permute-done | bytes 294944 | tf_op jit(solution)/shard_map/ppermute | solution.py:259
  40.9 5.4 %collective-permute-start.3 = (bf16[8,144,128]{2,1,0:T(8,128)(2,1)}, bf16[8,144,128]{2,1,0:T(8,128)(2,1)S(1)}, u32[]{:S(2)}, u32[]{:S(2)}) collective-permute-start(bf16[8,144,128]{2,1,0:T(8,128)(2,1)} %collective-permute-done.1.refs_1_), channel_id=1, source_target_pairs={{0,2},{2,4},{4,6},{3,1},{5,3},{7,5},{8,10},{10,12},{12,14},{11,9},... | collective-permute-start | bytes 884744 | tf_op jit(solution)/shard_map/ppermute | solution.py:262
  46.4 8.1 %ladder_rows.2.refs_6_ = f32[2304,128]{1,0:T(8,128)S(1)} custom-call(s32[16,20]{1,0:T(8,128)S(1)} %fusion.2.index_ref, bf16[16,144,128]{2,1,0:T(8,128)(2,1)S(1)} %bitcast.19, bf16[8,144,128]{2,1,0:T(8,128)(2,1)S(1)} %collective-permute-done.refs_0_.refs_1_, bf16[8,144,128]{2,1,0:T(8,128)(2,1)S(1)} %collective-permute-done.5.refs_2_, ...), custom_call_target="tpu_custom_call" | custom-call | flops 1509949440 | bytes 10485760 | tf_op jit(solution)/shard_map/ladder_rows/pallas_call | solution.py:127
  54.5 8.1 %ladder_rows.3 = (f32[2304,128]{1,0:T(8,128)S(1)}, f32[2560,128]{1,0:T(8,128)S(1)}) custom-call(s32[16,20]{1,0:T(8,128)S(1)} %fusion.2.index_ref, bf16[16,144,128]{2,1,0:T(8,128)(2,1)S(1)} %bitcast.18, bf16[8,144,128]{2,1,0:T(8,128)(2,1)} %collective-permute-done.1.refs_1_, bf16[8,144,128]{2,1,0:T(8,128)(2,1)S(1)} %collective-permute-done.2.refs_2_, ...), custom_call_target="tpu_custom_call" | custom-call | flops 1509949440 | bytes 10485760 | tf_op jit(solution)/shard_map/ladder_rows/pallas_call | solution.py:127
  62.6 2.7 %pack.1 = f32[5120,128]{1,0:T(8,128)S(1)} custom-call(f32[2304,128]{1,0:T(8,128)S(1)} %get-tuple-element.7.ladder_ref, f32[2560,128]{1,0:T(8,128)S(1)} %get-tuple-element.8.earlier_ref), custom_call_target="tpu_custom_call" | custom-call | flops 9437184 | bytes 2359296 | tf_op jit(solution)/shard_map/pack/pallas_call | solution.py:152
  65.3 1.2 convert_element_type.8
  66.6 32.7 %all-to-all-start = ((f16[256,10,2,128]{3,2,1,0:T(2,128)(2,1)}), f16[256,10,2,128]{3,2,1,0:T(2,128)(2,1)}, u32[]{:S(2)}, u32[]{:S(2)}) async-start(f16[256,10,2,128]{3,2,1,0:T(2,128)(2,1)} %bitcast.24), calls=%async_computation | async-start | bytes 2621440 | tf_op jit(solution)/shard_map/all_to_all | solution.py:274
  99.4 35.1 %all-to-all-done = f16[256,10,2,128]{3,2,1,0:T(2,128)(2,1)} async-done(((f16[256,10,2,128]{3,2,1,0:T(2,128)(2,1)}), f16[256,10,2,128]{3,2,1,0:T(2,128)(2,1)}, u32[]{:S(2)}, u32[]{:S(2)}) %all-to-all-start) | async-done | bytes 1310752 | tf_op jit(solution)/shard_map/all_to_all | solution.py:274
  134.5 1.5 %convert.1.got_ref = f32[5120,128]{1,0:T(8,128)S(1)} convert(f16[5120,128]{1,0:T(8,128)(2,1)} %bitcast.13) | non-fusion elementwise | flops 655360 | bytes 3932160 | tf_op jit(solution)/shard_map/convert_element_type | solution.py:280
  136.1 4.2 %finish.1 = bf16[3,96,16,128]{3,2,1,0:T(8,128)(2,1)} custom-call(f32[96]{0:T(128)S(1)} %copy-done, f32[3]{0:T(128)S(1)} %dynamic_slice.6.own_occ_ref, f32[5120,128]{1,0:T(8,128)S(1)} %convert.1.got_ref, f32[3,48,16,128]{3,2,1,0:T(8,128)S(1)} %bitcast.16, f32[3,48,16,128]{3,2,1,0:T(8,128)S(1)} %bitcast.17, f32[16,128]{1,0:T(8,128)S(1)} %broadcast_in_dim.27.va_ref, ...), custom_call_target="tpu_custom_call" | custom-call | flops 33554432 | bytes 8388608 | tf_op jit(solution)/shard_map/finish/pallas_call | solution.py:207
  (28 shorter events, 0.6 us)
Async XLA Ops:
  1.4 24.7 %copy-start.1 = (bf16[16,3,48,128]{3,0,2,1:T(8,128)(2,1)}, bf16[16,3,48,128]{3,0,2,1:T(8,128)(2,1)S(1)}, u32[]{:S(2)}) copy-start(bf16[16,3,48,128]{3,0,2,1:T(8,128)(2,1)S(1)} %get-tuple-element.10) | copy-start | bytes 1769476
  1.8 15.0 %collective-permute-start = (bf16[8,144,128]{2,1,0:T(8,128)(2,1)S(1)}, bf16[8,144,128]{2,1,0:T(8,128)(2,1)S(1)}, u32[]{:S(2)}, u32[]{:S(2)}) collective-permute-start(bf16[8,144,128]{2,1,0:T(8,128)(2,1)S(1)} %bitcast.26), channel_id=1, source_target_pairs={{0,1},{1,0},{2,3},{3,2},{4,5},{5,4},{6,7},{7,6},{8,9},{9,8},{10,11... | collective-permute-start | bytes 884744 | tf_op jit(solution)/shard_map/ppermute | solution.py:259
  9.7 16.5 %collective-permute-start.5 = (bf16[8,144,128]{2,1,0:T(8,128)(2,1)S(1)}, bf16[8,144,128]{2,1,0:T(8,128)(2,1)S(1)}, u32[]{:S(2)}, u32[]{:S(2)}) collective-permute-start(bf16[8,144,128]{2,1,0:T(8,128)(2,1)S(1)} %bitcast.25), channel_id=1, source_target_pairs={{0,1},{1,0},{2,3},{3,2},{4,5},{5,4},{6,7},{7,6},{8,9},{9,8},{10,11... | collective-permute-start | bytes 884744 | tf_op jit(solution)/shard_map/ppermute | solution.py:259
  16.8 16.2 %collective-permute-start.2 = (bf16[8,144,128]{2,1,0:T(8,128)(2,1)S(1)}, bf16[8,144,128]{2,1,0:T(8,128)(2,1)S(1)}, u32[]{:S(2)}, u32[]{:S(2)}) collective-permute-start(bf16[8,144,128]{2,1,0:T(8,128)(2,1)S(1)} %after.4), channel_id=1, source_target_pairs={{0,1},{1,0},{2,3},{3,2},{4,5},{5,4},{6,7},{7,6},{8,9},{9,8},{10,11... | collective-permute-start | bytes 884744 | tf_op jit(solution)/shard_map/ppermute | solution.py:259
  22.6 23.7 %copy-start.3 = (s32[16,20]{1,0:T(8,128)S(1)}, s32[16,20]{1,0:T(8,128)}, u32[]{:S(2)}) copy-start(s32[16,20]{1,0:T(8,128)} %param.8) | copy-start | bytes 3844
  22.6 23.7 %copy-start.4 = (s32[16]{0:T(128)S(1)}, s32[16]{0:T(128)}, u32[]{:S(2)}) copy-start(s32[16]{0:T(128)} %param.9) | copy-start | bytes 196
  22.6 18.3 %collective-permute-start.1 = (bf16[8,144,128]{2,1,0:T(8,128)(2,1)S(1)}, bf16[8,144,128]{2,1,0:T(8,128)(2,1)}, u32[]{:S(2)}, u32[]{:S(2)}) collective-permute-start(bf16[8,144,128]{2,1,0:T(8,128)(2,1)S(1)} %after.3), channel_id=1, source_target_pairs={{0,1},{1,0},{2,3},{3,2},{4,5},{5,4},{6,7},{7,6},{8,9},{9,8},{10,11... | collective-permute-start | bytes 884744 | tf_op jit(solution)/shard_map/ppermute | solution.py:259
  22.7 23.7 %collective-permute-start.6 = (bf16[8,144,128]{2,1,0:T(8,128)(2,1)S(1)}, bf16[8,144,128]{2,1,0:T(8,128)(2,1)S(1)}, u32[]{:S(2)}, u32[]{:S(2)}) collective-permute-start(bf16[8,144,128]{2,1,0:T(8,128)(2,1)S(1)} %collective-permute-done.refs_0_.refs_1_), channel_id=1, source_target_pairs={{0,2},{2,4},{4,6},{3,1},{5,3},{7,5},{8,10},{10,12},{12,14},{11,9},... | collective-permute-start | bytes 884744 | tf_op jit(solution)/shard_map/ppermute | solution.py:262
  26.2 20.2 %collective-permute-start.7 = (bf16[8,144,128]{2,1,0:T(8,128)(2,1)S(1)}, bf16[8,144,128]{2,1,0:T(8,128)(2,1)S(1)}, u32[]{:S(2)}, u32[]{:S(2)}) collective-permute-start(bf16[8,144,128]{2,1,0:T(8,128)(2,1)S(1)} %collective-permute-done.5.refs_2_), channel_id=1, source_target_pairs={{0,2},{2,4},{4,6},{3,1},{5,3},{7,5},{8,10},{10,12},{12,14},{11,9},... | collective-permute-start | bytes 884744 | tf_op jit(solution)/shard_map/ppermute | solution.py:262
  29.4 1.1 copy-start.2
  33.0 21.4 %collective-permute-start.4 = (bf16[8,144,128]{2,1,0:T(8,128)(2,1)S(1)}, bf16[8,144,128]{2,1,0:T(8,128)(2,1)S(1)}, u32[]{:S(2)}, u32[]{:S(2)}) collective-permute-start(bf16[8,144,128]{2,1,0:T(8,128)(2,1)S(1)} %collective-permute-done.2.refs_2_), channel_id=1, source_target_pairs={{0,2},{2,4},{4,6},{3,1},{5,3},{7,5},{8,10},{10,12},{12,14},{11,9},... | collective-permute-start | bytes 884744 | tf_op jit(solution)/shard_map/ppermute | solution.py:262
  40.9 13.6 %collective-permute-start.3 = (bf16[8,144,128]{2,1,0:T(8,128)(2,1)}, bf16[8,144,128]{2,1,0:T(8,128)(2,1)S(1)}, u32[]{:S(2)}, u32[]{:S(2)}) collective-permute-start(bf16[8,144,128]{2,1,0:T(8,128)(2,1)} %collective-permute-done.1.refs_1_), channel_id=1, source_target_pairs={{0,2},{2,4},{4,6},{3,1},{5,3},{7,5},{8,10},{10,12},{12,14},{11,9},... | collective-permute-start | bytes 884744 | tf_op jit(solution)/shard_map/ppermute | solution.py:262
  66.5 32.7 %copy-start.5 = (f32[128]{0:T(128)S(1)}, f32[128]{0:T(128)}, u32[]{:S(2)}) copy-start(f32[128]{0:T(128)} %param.11) | copy-start | bytes 1540
  66.5 32.8 %copy-start = (f32[96]{0:T(128)S(1)}, f32[96]{0:T(128)}, u32[]{:S(2)}) copy-start(f32[96]{0:T(128)} %occ_ref.1) | copy-start | bytes 1156
  66.6 68.0 %all-to-all-start = ((f16[256,10,2,128]{3,2,1,0:T(2,128)(2,1)}), f16[256,10,2,128]{3,2,1,0:T(2,128)(2,1)}, u32[]{:S(2)}, u32[]{:S(2)}) async-start(f16[256,10,2,128]{3,2,1,0:T(2,128)(2,1)} %bitcast.24), calls=%async_computation | async-start | bytes 2621440 | tf_op jit(solution)/shard_map/all_to_all | solution.py:274

commit v8 on v7

--- a/solution.py
+++ b/solution.py
@@ -61,8 +61,8 @@
     return devices, rows
 
 
-WAITS = (1, 1, 2, 4, 4, 4)
-AHEAD = 4
+WAITS = (2, 2, 4, 4, 4)
+AHEAD = 8
 
 
 def ladder_kernel(packs, index_ref, *refs):

time: 141 us -> 139 us (0.986)
  Pallas kernels: 23.1 us -> 20.3 us
    pallas_call x2, Pallas kernels: 16.2 us -> 13.3 us  [ladder_rows(): pl.pallas_call(functools.partial(ladder_kernel, int(packs)), out_shape=ou...]
    all_to_all x1, starting transfers between devices: 32.7 us -> 34.1 us  [per_device(): lax.all_to_all(sent, ('pair', 'virt'), split_axis=0, concat_axis=0, tiled...]
  transfers between devices with their start and end apart: 9 -> 9, of which waited for: 4 -> 4; matrix products, arithmetic and copies ran while one was open for 0% -> 0% of each run, Pallas kernels for 6% -> 5%
where the time goes in v8:
time: 139 us
  starting transfers between devices  63.6 us (46%)
  waiting for transfers between devices  48.5 us (35%)
  Pallas kernels  20.3 us (15%)
  local copies, waits for them, and re-layouts  3.34 us (2%)
  other arithmetic  2.8 us (2%)
    all_to_all x1, waiting for transfers between devices, per_device(): lax.all_to_all(sent, ('pair', 'virt'), split_axis=0, concat_axis=0, tiled...  35.1 us
    all_to_all x1, starting transfers between devices, per_device(): lax.all_to_all(sent, ('pair', 'virt'), split_axis=0, concat_axis=0, tiled...  34.1 us
    ppermute x4, starting transfers between devices, passed_on(): return lax.ppermute(x, 'virt', relay)  15.8 us
    ppermute x4, starting transfers between devices, swapped(): return lax.ppermute(x, 'virt', swap)  13.8 us
    ppermute x4, waiting for transfers between devices, swapped(): return lax.ppermute(x, 'virt', swap)  13.4 us
    pallas_call x2, Pallas kernels, ladder_rows(): pl.pallas_call(functools.partial(ladder_kernel, int(packs)), out_shape=ou...  13.3 us
    pallas_call x1, Pallas kernels, finish(): pl.pallas_call(finish_kernel, out_shape=jax.ShapeDtypeStruct((rows, partn...  4.21 us
  transfers between devices with their start and end apart: 9, of which 4 were waited for; matrix products, arithmetic and copies ran while one was open for 0% of the time, Pallas kernels for 5%

profile of v8, /device:TPU:1, one launch (start us, length us, event | category | flops | bytes accessed | tf_op | source)
XLA Modules:
  0.0 138.9 jit_solution(3395784861623594177)
XLA Ops:
  0.0 1.4 %slice_bitcast_fusion = (bf16[16,3,48,128]{3,0,2,1:T(8,128)(2,1)S(1)}, bf16[16,3,48,128]{3,0,2,1:T(8,128)(2,1)S(1)}) fusion(bf16[3,96,16,128]{3,2,1,0:T(8,128)(2,1)} %param.6), kind=kLoop, calls=%fused_computation | loop fusion | bytes 2359296 | tf_op jit(solution)/shard_map/transpose | solution.py:248
  1.5 0.3 fusion.4
  1.8 7.8 %collective-permute-start = (bf16[8,144,128]{2,1,0:T(8,128)(2,1)S(1)}, bf16[8,144,128]{2,1,0:T(8,128)(2,1)S(1)}, u32[]{:S(2)}, u32[]{:S(2)}) collective-permute-start(bf16[8,144,128]{2,1,0:T(8,128)(2,1)S(1)} %bitcast.26), channel_id=1, source_target_pairs={{0,1},{1,0},{2,3},{3,2},{4,5},{5,4},{6,7},{7,6},{8,9},{9,8},{10,11... | collective-permute-start | bytes 884744 | tf_op jit(solution)/shard_map/ppermute | solution.py:259
  9.7 0.1 collective-permute-start.5
  9.9 6.9 %collective-permute-done.refs_0_.refs_1_ = bf16[8,144,128]{2,1,0:T(8,128)(2,1)S(1)} collective-permute-done((bf16[8,144,128]{2,1,0:T(8,128)(2,1)S(1)}, bf16[8,144,128]{2,1,0:T(8,128)(2,1)S(1)}, u32[]{:S(2)}, u32[]{:S(2)}) %collective-permute-start) | collective-permute-done | bytes 294944 | tf_op jit(solution)/shard_map/ppermute | solution.py:259
  16.8 5.7 %collective-permute-start.2 = (bf16[8,144,128]{2,1,0:T(8,128)(2,1)S(1)}, bf16[8,144,128]{2,1,0:T(8,128)(2,1)S(1)}, u32[]{:S(2)}, u32[]{:S(2)}) collective-permute-start(bf16[8,144,128]{2,1,0:T(8,128)(2,1)S(1)} %after.4), channel_id=1, source_target_pairs={{0,1},{1,0},{2,3},{3,2},{4,5},{5,4},{6,7},{7,6},{8,9},{9,8},{10,11... | collective-permute-start | bytes 884744 | tf_op jit(solution)/shard_map/ppermute | solution.py:259
  22.6 0.1 collective-permute-start.1
  22.7 3.5 %collective-permute-start.6 = (bf16[8,144,128]{2,1,0:T(8,128)(2,1)S(1)}, bf16[8,144,128]{2,1,0:T(8,128)(2,1)S(1)}, u32[]{:S(2)}, u32[]{:S(2)}) collective-permute-start(bf16[8,144,128]{2,1,0:T(8,128)(2,1)S(1)} %collective-permute-done.refs_0_.refs_1_), channel_id=1, source_target_pairs={{0,2},{2,4},{4,6},{3,1},{5,3},{7,5},{8,10},{10,12},{12,14},{11,9},... | collective-permute-start | bytes 884744 | tf_op jit(solution)/shard_map/ppermute | solution.py:262
  26.2 3.2 %collective-permute-start.7 = (bf16[8,144,128]{2,1,0:T(8,128)(2,1)S(1)}, bf16[8,144,128]{2,1,0:T(8,128)(2,1)S(1)}, u32[]{:S(2)}, u32[]{:S(2)}) collective-permute-start(bf16[8,144,128]{2,1,0:T(8,128)(2,1)S(1)} %collective-permute-done.5.refs_2_), channel_id=1, source_target_pairs={{0,2},{2,4},{4,6},{3,1},{5,3},{7,5},{8,10},{10,12},{12,14},{11,9},... | collective-permute-start | bytes 884744 | tf_op jit(solution)/shard_map/ppermute | solution.py:262
  29.4 0.2 copy.11
  29.6 0.9 copy-done.2
  30.5 0.2 copy.7
  30.7 2.4 %collective-permute-done.2.refs_2_ = bf16[8,144,128]{2,1,0:T(8,128)(2,1)S(1)} collective-permute-done((bf16[8,144,128]{2,1,0:T(8,128)(2,1)S(1)}, bf16[8,144,128]{2,1,0:T(8,128)(2,1)S(1)}, u32[]{:S(2)}, u32[]{:S(2)}) %collective-permute-start.2) | collective-permute-done | bytes 294944 | tf_op jit(solution)/shard_map/ppermute | solution.py:259
  33.0 3.8 %collective-permute-start.4 = (bf16[8,144,128]{2,1,0:T(8,128)(2,1)S(1)}, bf16[8,144,128]{2,1,0:T(8,128)(2,1)S(1)}, u32[]{:S(2)}, u32[]{:S(2)}) collective-permute-start(bf16[8,144,128]{2,1,0:T(8,128)(2,1)S(1)} %collective-permute-done.2.refs_2_), channel_id=1, source_target_pairs={{0,2},{2,4},{4,6},{3,1},{5,3},{7,5},{8,10},{10,12},{12,14},{11,9},... | collective-permute-start | bytes 884744 | tf_op jit(solution)/shard_map/ppermute | solution.py:262
  36.8 4.1 %collective-permute-done.1.refs_1_ = bf16[8,144,128]{2,1,0:T(8,128)(2,1)} collective-permute-done((bf16[8,144,128]{2,1,0:T(8,128)(2,1)S(1)}, bf16[8,144,128]{2,1,0:T(8,128)(2,1)}, u32[]{:S(2)}, u32[]{:S(2)}) %collective-permute-start.1) | collective-permute-done | bytes 294944 | tf_op jit(solution)/shard_map/ppermute | solution.py:259
  40.9 5.4 %collective-permute-start.3 = (bf16[8,144,128]{2,1,0:T(8,128)(2,1)}, bf16[8,144,128]{2,1,0:T(8,128)(2,1)S(1)}, u32[]{:S(2)}, u32[]{:S(2)}) collective-permute-start(bf16[8,144,128]{2,1,0:T(8,128)(2,1)} %collective-permute-done.1.refs_1_), channel_id=1, source_target_pairs={{0,2},{2,4},{4,6},{3,1},{5,3},{7,5},{8,10},{10,12},{12,14},{11,9},... | collective-permute-start | bytes 884744 | tf_op jit(solution)/shard_map/ppermute | solution.py:262
  46.4 6.7 %ladder_rows.2.refs_6_ = f32[2304,128]{1,0:T(8,128)S(1)} custom-call(s32[16,20]{1,0:T(8,128)S(1)} %fusion.2.index_ref, bf16[16,144,128]{2,1,0:T(8,128)(2,1)S(1)} %bitcast.19, bf16[8,144,128]{2,1,0:T(8,128)(2,1)S(1)} %collective-permute-done.refs_0_.refs_1_, bf16[8,144,128]{2,1,0:T(8,128)(2,1)S(1)} %collective-permute-done.5.refs_2_, ...), custom_call_target="tpu_custom_call" | custom-call | flops 1509949440 | bytes 10485760 | tf_op jit(solution)/shard_map/ladder_rows/pallas_call | solution.py:127
  53.1 6.6 %ladder_rows.3 = (f32[2304,128]{1,0:T(8,128)S(1)}, f32[2560,128]{1,0:T(8,128)S(1)}) custom-call(s32[16,20]{1,0:T(8,128)S(1)} %fusion.2.index_ref, bf16[16,144,128]{2,1,0:T(8,128)(2,1)S(1)} %bitcast.18, bf16[8,144,128]{2,1,0:T(8,128)(2,1)} %collective-permute-done.1.refs_1_, bf16[8,144,128]{2,1,0:T(8,128)(2,1)S(1)} %collective-permute-done.2.refs_2_, ...), custom_call_target="tpu_custom_call" | custom-call | flops 1509949440 | bytes 10485760 | tf_op jit(solution)/shard_map/ladder_rows/pallas_call | solution.py:127
  59.7 2.7 %pack.1 = f32[5120,128]{1,0:T(8,128)S(1)} custom-call(f32[2304,128]{1,0:T(8,128)S(1)} %get-tuple-element.7.ladder_ref, f32[2560,128]{1,0:T(8,128)S(1)} %get-tuple-element.8.earlier_ref), custom_call_target="tpu_custom_call" | custom-call | flops 9437184 | bytes 2359296 | tf_op jit(solution)/shard_map/pack/pallas_call | solution.py:152
  62.5 1.2 convert_element_type.8
  63.7 34.1 %all-to-all-start = ((f16[256,10,2,128]{3,2,1,0:T(2,128)(2,1)}), f16[256,10,2,128]{3,2,1,0:T(2,128)(2,1)}, u32[]{:S(2)}, u32[]{:S(2)}) async-start(f16[256,10,2,128]{3,2,1,0:T(2,128)(2,1)} %bitcast.24), calls=%async_computation | async-start | bytes 2621440 | tf_op jit(solution)/shard_map/all_to_all | solution.py:274
  98.0 35.1 %all-to-all-done = f16[256,10,2,128]{3,2,1,0:T(2,128)(2,1)} async-done(((f16[256,10,2,128]{3,2,1,0:T(2,128)(2,1)}), f16[256,10,2,128]{3,2,1,0:T(2,128)(2,1)}, u32[]{:S(2)}, u32[]{:S(2)}) %all-to-all-start) | async-done | bytes 1310752 | tf_op jit(solution)/shard_map/all_to_all | solution.py:274
  133.1 1.5 %convert.1.got_ref = f32[5120,128]{1,0:T(8,128)S(1)} convert(f16[5120,128]{1,0:T(8,128)(2,1)} %bitcast.13) | non-fusion elementwise | flops 655360 | bytes 3932160 | tf_op jit(solution)/shard_map/convert_element_type | solution.py:280
  134.7 4.2 %finish.1 = bf16[3,96,16,128]{3,2,1,0:T(8,128)(2,1)} custom-call(f32[96]{0:T(128)S(1)} %copy-done, f32[3]{0:T(128)S(1)} %dynamic_slice.6.own_occ_ref, f32[5120,128]{1,0:T(8,128)S(1)} %convert.1.got_ref, f32[3,48,16,128]{3,2,1,0:T(8,128)S(1)} %bitcast.16, f32[3,48,16,128]{3,2,1,0:T(8,128)S(1)} %bitcast.17, f32[16,128]{1,0:T(8,128)S(1)} %broadcast_in_dim.27.va_ref, ...), custom_call_target="tpu_custom_call" | custom-call | flops 33554432 | bytes 8388608 | tf_op jit(solution)/shard_map/finish/pallas_call | solution.py:207
  (28 shorter events, 0.6 us)
Async XLA Ops:
  1.4 24.7 %copy-start.1 = (bf16[16,3,48,128]{3,0,2,1:T(8,128)(2,1)}, bf16[16,3,48,128]{3,0,2,1:T(8,128)(2,1)S(1)}, u32[]{:S(2)}) copy-start(bf16[16,3,48,128]{3,0,2,1:T(8,128)(2,1)S(1)} %get-tuple-element.10) | copy-start | bytes 1769476
  1.8 15.0 %collective-permute-start = (bf16[8,144,128]{2,1,0:T(8,128)(2,1)S(1)}, bf16[8,144,128]{2,1,0:T(8,128)(2,1)S(1)}, u32[]{:S(2)}, u32[]{:S(2)}) collective-permute-start(bf16[8,144,128]{2,1,0:T(8,128)(2,1)S(1)} %bitcast.26), channel_id=1, source_target_pairs={{0,1},{1,0},{2,3},{3,2},{4,5},{5,4},{6,7},{7,6},{8,9},{9,8},{10,11... | collective-permute-start | bytes 884744 | tf_op jit(solution)/shard_map/ppermute | solution.py:259
  9.7 16.5 %collective-permute-start.5 = (bf16[8,144,128]{2,1,0:T(8,128)(2,1)S(1)}, bf16[8,144,128]{2,1,0:T(8,128)(2,1)S(1)}, u32[]{:S(2)}, u32[]{:S(2)}) collective-permute-start(bf16[8,144,128]{2,1,0:T(8,128)(2,1)S(1)} %bitcast.25), channel_id=1, source_target_pairs={{0,1},{1,0},{2,3},{3,2},{4,5},{5,4},{6,7},{7,6},{8,9},{9,8},{10,11... | collective-permute-start | bytes 884744 | tf_op jit(solution)/shard_map/ppermute | solution.py:259
  16.8 16.2 %collective-permute-start.2 = (bf16[8,144,128]{2,1,0:T(8,128)(2,1)S(1)}, bf16[8,144,128]{2,1,0:T(8,128)(2,1)S(1)}, u32[]{:S(2)}, u32[]{:S(2)}) collective-permute-start(bf16[8,144,128]{2,1,0:T(8,128)(2,1)S(1)} %after.4), channel_id=1, source_target_pairs={{0,1},{1,0},{2,3},{3,2},{4,5},{5,4},{6,7},{7,6},{8,9},{9,8},{10,11... | collective-permute-start | bytes 884744 | tf_op jit(solution)/shard_map/ppermute | solution.py:259
  22.6 23.7 %copy-start.3 = (s32[16,20]{1,0:T(8,128)S(1)}, s32[16,20]{1,0:T(8,128)}, u32[]{:S(2)}) copy-start(s32[16,20]{1,0:T(8,128)} %param.8) | copy-start | bytes 3844
  22.6 23.7 %copy-start.4 = (s32[16]{0:T(128)S(1)}, s32[16]{0:T(128)}, u32[]{:S(2)}) copy-start(s32[16]{0:T(128)} %param.9) | copy-start | bytes 196
  22.6 18.3 %collective-permute-start.1 = (bf16[8,144,128]{2,1,0:T(8,128)(2,1)S(1)}, bf16[8,144,128]{2,1,0:T(8,128)(2,1)}, u32[]{:S(2)}, u32[]{:S(2)}) collective-permute-start(bf16[8,144,128]{2,1,0:T(8,128)(2,1)S(1)} %after.3), channel_id=1, source_target_pairs={{0,1},{1,0},{2,3},{3,2},{4,5},{5,4},{6,7},{7,6},{8,9},{9,8},{10,11... | collective-permute-start | bytes 884744 | tf_op jit(solution)/shard_map/ppermute | solution.py:259
  22.7 23.7 %collective-permute-start.6 = (bf16[8,144,128]{2,1,0:T(8,128)(2,1)S(1)}, bf16[8,144,128]{2,1,0:T(8,128)(2,1)S(1)}, u32[]{:S(2)}, u32[]{:S(2)}) collective-permute-start(bf16[8,144,128]{2,1,0:T(8,128)(2,1)S(1)} %collective-permute-done.refs_0_.refs_1_), channel_id=1, source_target_pairs={{0,2},{2,4},{4,6},{3,1},{5,3},{7,5},{8,10},{10,12},{12,14},{11,9},... | collective-permute-start | bytes 884744 | tf_op jit(solution)/shard_map/ppermute | solution.py:262
  26.2 20.2 %collective-permute-start.7 = (bf16[8,144,128]{2,1,0:T(8,128)(2,1)S(1)}, bf16[8,144,128]{2,1,0:T(8,128)(2,1)S(1)}, u32[]{:S(2)}, u32[]{:S(2)}) collective-permute-start(bf16[8,144,128]{2,1,0:T(8,128)(2,1)S(1)} %collective-permute-done.5.refs_2_), channel_id=1, source_target_pairs={{0,2},{2,4},{4,6},{3,1},{5,3},{7,5},{8,10},{10,12},{12,14},{11,9},... | collective-permute-start | bytes 884744 | tf_op jit(solution)/shard_map/ppermute | solution.py:262
  29.4 1.1 copy-start.2
  33.0 20.0 %collective-permute-start.4 = (bf16[8,144,128]{2,1,0:T(8,128)(2,1)S(1)}, bf16[8,144,128]{2,1,0:T(8,128)(2,1)S(1)}, u32[]{:S(2)}, u32[]{:S(2)}) collective-permute-start(bf16[8,144,128]{2,1,0:T(8,128)(2,1)S(1)} %collective-permute-done.2.refs_2_), channel_id=1, source_target_pairs={{0,2},{2,4},{4,6},{3,1},{5,3},{7,5},{8,10},{10,12},{12,14},{11,9},... | collective-permute-start | bytes 884744 | tf_op jit(solution)/shard_map/ppermute | solution.py:262
  40.9 12.2 %collective-permute-start.3 = (bf16[8,144,128]{2,1,0:T(8,128)(2,1)}, bf16[8,144,128]{2,1,0:T(8,128)(2,1)S(1)}, u32[]{:S(2)}, u32[]{:S(2)}) collective-permute-start(bf16[8,144,128]{2,1,0:T(8,128)(2,1)} %collective-permute-done.1.refs_1_), channel_id=1, source_target_pairs={{0,2},{2,4},{4,6},{3,1},{5,3},{7,5},{8,10},{10,12},{12,14},{11,9},... | collective-permute-start | bytes 884744 | tf_op jit(solution)/shard_map/ppermute | solution.py:262
  63.7 34.1 %copy-start.5 = (f32[128]{0:T(128)S(1)}, f32[128]{0:T(128)}, u32[]{:S(2)}) copy-start(f32[128]{0:T(128)} %param.11) | copy-start | bytes 1540
  63.7 34.2 %copy-start = (f32[96]{0:T(128)S(1)}, f32[96]{0:T(128)}, u32[]{:S(2)}) copy-start(f32[96]{0:T(128)} %occ_ref.1) | copy-start | bytes 1156
  63.7 69.4 %all-to-all-start = ((f16[256,10,2,128]{3,2,1,0:T(2,128)(2,1)}), f16[256,10,2,128]{3,2,1,0:T(2,128)(2,1)}, u32[]{:S(2)}, u32[]{:S(2)}) async-start(f16[256,10,2,128]{3,2,1,0:T(2,128)(2,1)} %bitcast.24), calls=%async_computation | async-start | bytes 2621440 | tf_op jit(solution)/shard_map/all_to_all | solution.py:274

commit v9 on v8

--- a/solution.py
+++ b/solution.py
@@ -163,12 +163,12 @@
 
 def finish_kernel(occ_ref, own_occ_ref, got_ref, first_ref, second_ref, va_ref, vb_ref, out_ref, rest, turned):
     step = pl.program_id(0)
-    half = pl.num_programs(0) // 2
-
-    def work(ladder_ref):
+    split = first_ref.shape[1] // (8 * ROWS)
+
+    def work(ladder_ref, since):
         def store(i, j, partner):
             bottom = (own_occ_ref[i] + occ_ref[step * 8 * ROWS + j]) - va_ref[...] - vb_ref[...]
-            own = ladder_ref[i, lax.rem(step, half) * 8 * ROWS + j]
+            own = ladder_ref[i, (step - since) * 8 * ROWS + j]
             out_ref[i, j] = ((own + partner) * (1.0 / bottom)).astype(out_ref.dtype)
 
         for device in range(8):
@@ -189,13 +189,13 @@
         for n, part in enumerate(exchange_groups(parts)):
             store(ROWS - 1, n * ROWS + ROWS - 1, part)
 
-    @pl.when(step < half)
+    @pl.when(step < split)
     def _():
-        work(first_ref)
-
-    @pl.when(step >= half)
+        work(first_ref, 0)
+
+    @pl.when(step >= split)
     def _():
-        work(second_ref)
+        work(second_ref, split)
 
 
 def finish(occ, own_occ, got, ladders, va, vb):
@@ -233,7 +233,7 @@
     )(x, *first)
 
 
-CHUNKS = (16, 16)
+CHUNKS = (24, 8)
 
 
 def per_device(amplitudes, integrals, cd_tiles, tile_counts, eps_occ, eps_virt):
@@ -263,7 +263,7 @@
 
     half = tiles // 2
     over_a = [swapped(own[0][:half]), swapped(own[0][half:])]
-    over_b = [swapped(after(own[1][:half], over_a[0])), swapped(after(own[1][half:], over_a[0]))]
+    over_b = [swapped(after(own[1], over_a[0]))]
     beyond_a = [passed_on(x) for x in over_a]
     beyond_b = [passed_on(x) for x in over_b]
     beyond_a = [after(beyond_a[0], beyond_a[1]), beyond_a[1]]

time: 139 us -> 144 us (1.036)
  waiting for transfers between devices: 48.5 us -> 52.6 us
    all_to_all x1, starting transfers between devices: 34.1 us -> 38.5 us  [per_device(): lax.all_to_all(sent, ('pair', 'virt'), split_axis=0, concat_axis=0, tiled...]
    ppermute x4 -> x3, waiting for transfers between devices: 13.4 us -> 17.2 us  [swapped(): return lax.ppermute(x, 'virt', swap)]
    ppermute x4 -> x3, starting transfers between devices: 15.8 us -> 12.3 us  [passed_on(): return lax.ppermute(x, 'virt', relay)]
    pallas_call x2, Pallas kernels: 13.3 us -> 15.4 us  [ladder_rows(): pl.pallas_call(functools.partial(ladder_kernel, int(packs)), out_shape=ou...]
    pallas_call x1, Pallas kernels: 2.7 us -> 1.2 us  [pack(): pl.pallas_call(pack_kernel, out_shape=jax.ShapeDtypeStruct((earlier.shape...]
    ppermute x4 -> x3, starting transfers between devices: 13.8 us -> 13.7 us  [swapped(): return lax.ppermute(x, 'virt', swap)]
  transfers between devices with their start and end apart: 9 -> 7, of which waited for: 4 -> 5; matrix products, arithmetic and copies ran while one was open for 0% -> 1% of each run, Pallas kernels for 5% -> 6%
where the time goes in v9:
time: 144 us
  starting transfers between devices  64.5 us (45%)
  waiting for transfers between devices  52.6 us (37%)
  Pallas kernels  20.8 us (14%)
  local copies, waits for them, and re-layouts  3.13 us (2%)
  other arithmetic  2.79 us (2%)
    all_to_all x1, starting transfers between devices, per_device(): lax.all_to_all(sent, ('pair', 'virt'), split_axis=0, concat_axis=0, tiled...  38.5 us
    all_to_all x1, waiting for transfers between devices, per_device(): lax.all_to_all(sent, ('pair', 'virt'), split_axis=0, concat_axis=0, tiled...  35.1 us
    ppermute x3, waiting for transfers between devices, swapped(): return lax.ppermute(x, 'virt', swap)  17.2 us
    pallas_call x2, Pallas kernels, ladder_rows(): pl.pallas_call(functools.partial(ladder_kernel, int(packs)), out_shape=ou...  15.4 us
    ppermute x3, starting transfers between devices, swapped(): return lax.ppermute(x, 'virt', swap)  13.7 us
    ppermute x3, starting transfers between devices, passed_on(): return lax.ppermute(x, 'virt', relay)  12.3 us
    pallas_call x1, Pallas kernels, finish(): pl.pallas_call(finish_kernel, out_shape=jax.ShapeDtypeStruct((rows, partn...  4.21 us
  transfers between devices with their start and end apart: 7, of which 5 were waited for; matrix products, arithmetic and copies ran while one was open for 1% of the time, Pallas kernels for 6%

profile of v9, /device:TPU:1, one launch (start us, length us, event | category | flops | bytes accessed | tf_op | source)
XLA Modules:
  0.0 144.0 jit_solution(6355537335196256625)
XLA Ops:
  0.0 1.3 slice_bitcast_fusion
  1.3 0.2 fusion.4
  1.6 7.8 %collective-permute-start = (bf16[8,216,128]{2,1,0:T(8,128)(2,1)S(1)}, bf16[8,216,128]{2,1,0:T(8,128)(2,1)S(1)}, u32[]{:S(2)}, u32[]{:S(2)}) collective-permute-start(bf16[8,216,128]{2,1,0:T(8,128)(2,1)S(1)} %bitcast.23), channel_id=1, source_target_pairs={{0,1},{1,0},{2,3},{3,2},{4,5},{5,4},{6,7},{7,6},{8,9},{9,8},{10,11... | collective-permute-start | bytes 1327112 | tf_op jit(solution)/shard_map/ppermute | solution.py:259
  9.5 0.1 collective-permute-start.3
  9.6 1.0 slice_bitcast_fusion.1
  10.6 0.1 copy.7
  10.6 9.1 %collective-permute-done.refs_0_.refs_1_ = bf16[8,216,128]{2,1,0:T(8,128)(2,1)S(1)} collective-permute-done((bf16[8,216,128]{2,1,0:T(8,128)(2,1)S(1)}, bf16[8,216,128]{2,1,0:T(8,128)(2,1)S(1)}, u32[]{:S(2)}, u32[]{:S(2)}) %collective-permute-start) | collective-permute-done | bytes 442400 | tf_op jit(solution)/shard_map/ppermute | solution.py:259
  19.8 5.7 %collective-permute-start.1 = (bf16[16,72,128]{2,1,0:T(8,128)(2,1)S(1)}, bf16[16,72,128]{2,1,0:T(8,128)(2,1)}, u32[]{:S(2)}, u32[]{:S(2)}) collective-permute-start(bf16[16,72,128]{2,1,0:T(8,128)(2,1)S(1)} %after.2), channel_id=1, source_target_pairs={{0,1},{1,0},{2,3},{3,2},{4,5},{5,4},{6,7},{7,6},{8,9},{9,8},{10,11... | collective-permute-start | bytes 884744 | tf_op jit(solution)/shard_map/ppermute | solution.py:259
  25.5 3.2 %collective-permute-start.4 = (bf16[8,216,128]{2,1,0:T(8,128)(2,1)S(1)}, bf16[8,216,128]{2,1,0:T(8,128)(2,1)S(1)}, u32[]{:S(2)}, u32[]{:S(2)}) collective-permute-start(bf16[8,216,128]{2,1,0:T(8,128)(2,1)S(1)} %collective-permute-done.refs_0_.refs_1_), channel_id=1, source_target_pairs={{0,2},{2,4},{4,6},{3,1},{5,3},{7,5},{8,10},{10,12},{12,14},{11,9},... | collective-permute-start | bytes 1327112 | tf_op jit(solution)/shard_map/ppermute | solution.py:262
  28.7 4.1 %collective-permute-done.3.refs_2_ = bf16[8,216,128]{2,1,0:T(8,128)(2,1)S(1)} collective-permute-done((bf16[8,216,128]{2,1,0:T(8,128)(2,1)S(1)}, bf16[8,216,128]{2,1,0:T(8,128)(2,1)S(1)}, u32[]{:S(2)}, u32[]{:S(2)}) %collective-permute-start.3) | collective-permute-done | bytes 442400 | tf_op jit(solution)/shard_map/ppermute | solution.py:259
  32.8 3.8 %collective-permute-start.5 = (bf16[8,216,128]{2,1,0:T(8,128)(2,1)S(1)}, bf16[8,216,128]{2,1,0:T(8,128)(2,1)S(1)}, u32[]{:S(2)}, u32[]{:S(2)}) collective-permute-start(bf16[8,216,128]{2,1,0:T(8,128)(2,1)S(1)} %collective-permute-done.3.refs_2_), channel_id=1, source_target_pairs={{0,2},{2,4},{4,6},{3,1},{5,3},{7,5},{8,10},{10,12},{12,14},{11,9},... | collective-permute-start | bytes 1327112 | tf_op jit(solution)/shard_map/ppermute | solution.py:262
  36.6 4.1 %collective-permute-done.1.refs_1_ = bf16[16,72,128]{2,1,0:T(8,128)(2,1)} collective-permute-done((bf16[16,72,128]{2,1,0:T(8,128)(2,1)S(1)}, bf16[16,72,128]{2,1,0:T(8,128)(2,1)}, u32[]{:S(2)}, u32[]{:S(2)}) %collective-permute-start.1) | collective-permute-done | bytes 294944 | tf_op jit(solution)/shard_map/ppermute | solution.py:259
  40.7 5.4 %collective-permute-start.2 = (bf16[16,72,128]{2,1,0:T(8,128)(2,1)}, bf16[16,72,128]{2,1,0:T(8,128)(2,1)S(1)}, u32[]{:S(2)}, u32[]{:S(2)}) collective-permute-start(bf16[16,72,128]{2,1,0:T(8,128)(2,1)} %collective-permute-done.1.refs_1_), channel_id=1, source_target_pairs={{0,2},{2,4},{4,6},{3,1},{5,3},{7,5},{8,10},{10,12},{12,14},{11,9},... | collective-permute-start | bytes 884744 | tf_op jit(solution)/shard_map/ppermute | solution.py:262
  46.1 0.2 copy.9
  46.4 0.2 collective-permute-done.5.refs_0_.refs_4_
  46.6 9.2 %ladder_rows.2.refs_4_ = f32[3456,128]{1,0:T(8,128)S(1)} custom-call(s32[16,20]{1,0:T(8,128)S(1)} %fusion.2.index_ref, bf16[16,216,128]{2,1,0:T(8,128)(2,1)S(1)} %bitcast.15, bf16[8,216,128]{2,1,0:T(8,128)(2,1)S(1)} %collective-permute-done.refs_0_.refs_1_, bf16[8,216,128]{2,1,0:T(8,128)(2,1)S(1)} %collective-permute-done.3.refs_2_, ...), custom_call_target="tpu_custom_call" | custom-call | flops 2264924160 | bytes 10485760 | tf_op jit(solution)/shard_map/ladder_rows/pallas_call | solution.py:127
  55.9 6.1 %ladder_rows.3 = (f32[1152,128]{1,0:T(8,128)S(1)}, f32[3840,128]{1,0:T(8,128)S(1)}) custom-call(s32[16,20]{1,0:T(8,128)S(1)} %fusion.2.index_ref, bf16[16,72,128]{2,1,0:T(8,128)(2,1)S(1)} %bitcast.17, bf16[16,72,128]{2,1,0:T(8,128)(2,1)} %collective-permute-done.1.refs_1_, bf16[16,72,128]{2,1,0:T(8,128)(2,1)S(1)} %collective-permute-done.2.refs_2_, ...), custom_call_target="tpu_custom_call" | custom-call | flops 754974720 | bytes 10485760 | tf_op jit(solution)/shard_map/ladder_rows/pallas_call | solution.py:127
  62.0 1.2 pack.1
  63.2 1.2 convert_element_type.8
  64.4 38.5 %all-to-all-start = ((f16[256,10,2,128]{3,2,1,0:T(2,128)(2,1)}), f16[256,10,2,128]{3,2,1,0:T(2,128)(2,1)}, u32[]{:S(2)}, u32[]{:S(2)}) async-start(f16[256,10,2,128]{3,2,1,0:T(2,128)(2,1)} %bitcast.21), calls=%async_computation | async-start | bytes 2621440 | tf_op jit(solution)/shard_map/all_to_all | solution.py:274
  103.0 0.1 dynamic_slice.7
  103.2 35.1 %all-to-all-done = f16[256,10,2,128]{3,2,1,0:T(2,128)(2,1)} async-done(((f16[256,10,2,128]{3,2,1,0:T(2,128)(2,1)}), f16[256,10,2,128]{3,2,1,0:T(2,128)(2,1)}, u32[]{:S(2)}, u32[]{:S(2)}) %all-to-all-start) | async-done | bytes 1310752 | tf_op jit(solution)/shard_map/all_to_all | solution.py:274
  138.3 1.5 %convert.1.got_ref = f32[5120,128]{1,0:T(8,128)S(1)} convert(f16[5120,128]{1,0:T(8,128)(2,1)} %bitcast.11) | non-fusion elementwise | flops 655360 | bytes 3932160 | tf_op jit(solution)/shard_map/convert_element_type | solution.py:280
  139.8 4.2 %finish.1 = bf16[3,96,16,128]{3,2,1,0:T(8,128)(2,1)} custom-call(f32[96]{0:T(128)S(1)} %copy-done, f32[3]{0:T(128)S(1)} %dynamic_slice.6.own_occ_ref, f32[5120,128]{1,0:T(8,128)S(1)} %convert.1.got_ref, f32[3,72,16,128]{3,2,1,0:T(8,128)S(1)} %bitcast.14, f32[3,24,16,128]{3,2,1,0:T(8,128)S(1)} %bitcast.18, f32[16,128]{1,0:T(8,128)S(1)} %broadcast_in_dim.27.va_ref, ...), custom_call_target="tpu_custom_call" | custom-call | flops 33554432 | bytes 8388608 | tf_op jit(solution)/shard_map/finish/pallas_call | solution.py:207
  (18 shorter events, 0.4 us)
Async XLA Ops:
  1.6 18.2 %collective-permute-start = (bf16[8,216,128]{2,1,0:T(8,128)(2,1)S(1)}, bf16[8,216,128]{2,1,0:T(8,128)(2,1)S(1)}, u32[]{:S(2)}, u32[]{:S(2)}) collective-permute-start(bf16[8,216,128]{2,1,0:T(8,128)(2,1)S(1)} %bitcast.23), channel_id=1, source_target_pairs={{0,1},{1,0},{2,3},{3,2},{4,5},{5,4},{6,7},{7,6},{8,9},{9,8},{10,11... | collective-permute-start | bytes 1327112 | tf_op jit(solution)/shard_map/ppermute | solution.py:259
  9.4 36.6 %copy-start.1 = (s32[16,20]{1,0:T(8,128)S(1)}, s32[16,20]{1,0:T(8,128)}, u32[]{:S(2)}) copy-start(s32[16,20]{1,0:T(8,128)} %param.8) | copy-start | bytes 3844
  9.5 36.6 %copy-start.2 = (s32[16]{0:T(128)S(1)}, s32[16]{0:T(128)}, u32[]{:S(2)}) copy-start(s32[16]{0:T(128)} %param.9) | copy-start | bytes 196
  9.5 23.3 %collective-permute-start.3 = (bf16[8,216,128]{2,1,0:T(8,128)(2,1)S(1)}, bf16[8,216,128]{2,1,0:T(8,128)(2,1)S(1)}, u32[]{:S(2)}, u32[]{:S(2)}) collective-permute-start(bf16[8,216,128]{2,1,0:T(8,128)(2,1)S(1)} %bitcast.22), channel_id=1, source_target_pairs={{0,1},{1,0},{2,3},{3,2},{4,5},{5,4},{6,7},{7,6},{8,9},{9,8},{10,11... | collective-permute-start | bytes 1327112 | tf_op jit(solution)/shard_map/ppermute | solution.py:259
  19.8 20.9 %collective-permute-start.1 = (bf16[16,72,128]{2,1,0:T(8,128)(2,1)S(1)}, bf16[16,72,128]{2,1,0:T(8,128)(2,1)}, u32[]{:S(2)}, u32[]{:S(2)}) collective-permute-start(bf16[16,72,128]{2,1,0:T(8,128)(2,1)S(1)} %after.2), channel_id=1, source_target_pairs={{0,1},{1,0},{2,3},{3,2},{4,5},{5,4},{6,7},{7,6},{8,9},{9,8},{10,11... | collective-permute-start | bytes 884744 | tf_op jit(solution)/shard_map/ppermute | solution.py:259
  25.5 20.8 %collective-permute-start.4 = (bf16[8,216,128]{2,1,0:T(8,128)(2,1)S(1)}, bf16[8,216,128]{2,1,0:T(8,128)(2,1)S(1)}, u32[]{:S(2)}, u32[]{:S(2)}) collective-permute-start(bf16[8,216,128]{2,1,0:T(8,128)(2,1)S(1)} %collective-permute-done.refs_0_.refs_1_), channel_id=1, source_target_pairs={{0,2},{2,4},{4,6},{3,1},{5,3},{7,5},{8,10},{10,12},{12,14},{11,9},... | collective-permute-start | bytes 1327112 | tf_op jit(solution)/shard_map/ppermute | solution.py:262
  32.8 13.8 %collective-permute-start.5 = (bf16[8,216,128]{2,1,0:T(8,128)(2,1)S(1)}, bf16[8,216,128]{2,1,0:T(8,128)(2,1)S(1)}, u32[]{:S(2)}, u32[]{:S(2)}) collective-permute-start(bf16[8,216,128]{2,1,0:T(8,128)(2,1)S(1)} %collective-permute-done.3.refs_2_), channel_id=1, source_target_pairs={{0,2},{2,4},{4,6},{3,1},{5,3},{7,5},{8,10},{10,12},{12,14},{11,9},... | collective-permute-start | bytes 1327112 | tf_op jit(solution)/shard_map/ppermute | solution.py:262
  40.7 15.2 %collective-permute-start.2 = (bf16[16,72,128]{2,1,0:T(8,128)(2,1)}, bf16[16,72,128]{2,1,0:T(8,128)(2,1)S(1)}, u32[]{:S(2)}, u32[]{:S(2)}) collective-permute-start(bf16[16,72,128]{2,1,0:T(8,128)(2,1)} %collective-permute-done.1.refs_1_), channel_id=1, source_target_pairs={{0,2},{2,4},{4,6},{3,1},{5,3},{7,5},{8,10},{10,12},{12,14},{11,9},... | collective-permute-start | bytes 884744 | tf_op jit(solution)/shard_map/ppermute | solution.py:262
  64.4 38.6 %copy-start.3 = (f32[128]{0:T(128)S(1)}, f32[128]{0:T(128)}, u32[]{:S(2)}) copy-start(f32[128]{0:T(128)} %param.11) | copy-start | bytes 1540
  64.4 38.7 %copy-start = (f32[96]{0:T(128)S(1)}, f32[96]{0:T(128)}, u32[]{:S(2)}) copy-start(f32[96]{0:T(128)} %occ_ref.1) | copy-start | bytes 1156
  64.4 73.8 %all-to-all-start = ((f16[256,10,2,128]{3,2,1,0:T(2,128)(2,1)}), f16[256,10,2,128]{3,2,1,0:T(2,128)(2,1)}, u32[]{:S(2)}, u32[]{:S(2)}) async-start(f16[256,10,2,128]{3,2,1,0:T(2,128)(2,1)} %bitcast.21), calls=%async_computation | async-start | bytes 2621440 | tf_op jit(solution)/shard_map/all_to_all | solution.py:274
